TPU v7x, 32 devices: a whole 2x2x4 slice. The times are simulated.
32 devices in a mesh: blk: 8 (over y, x, core), head: 4 (over z).
Axes of the slice: x: 2, y: 2, z: 4, core: 2. Of those that a mesh axis runs over, the one named last changes fastest.
Arguments:
- tokens: bfloat16 [16384, 1024], P(('blk', 'head')), may hold values from -6 to 6
- cotangent: bfloat16 [16384, 1024], P(('blk', 'head')), may hold values from -6 to 6
- lengths: int32 [32], replicated, may hold values from 1 to 14407, as said below
- valid_count: int32 [1], replicated, may hold values from 14337 to 16256
- first_gain: bfloat16 [1024], P(('blk', 'head')), may hold values from 0.25 to 1.75
- first_shift: bfloat16 [1024], P(('blk', 'head')), may hold values from -1.75 to 1.75
- joined_weight: bfloat16 [1024, 3072], P(('blk', 'head')), as said below
- joined_bias: bfloat16 [2048], P(('blk', 'head')), may hold values from -1.75 to 1.75
- dense_weight: bfloat16 [1024, 1024], P(('blk', 'head')), may hold values from -0.5 to 0.5
- dense_bias: bfloat16 [1024], P(('blk', 'head')), may hold values from -1.75 to 1.75
- second_gain: bfloat16 [1024], P(('blk', 'head')), may hold values from 0.25 to 1.75
- second_shift: bfloat16 [1024], P(('blk', 'head')), may hold values from -1.75 to 1.75
- up_weight: bfloat16 [1024, 4096], P(('blk', 'head')), may hold values from -0.1875 to 0.1875
- up_bias: bfloat16 [4096], P(('blk', 'head')), may hold values from -1.75 to 1.75
- down_weight: bfloat16 [4096, 1024], P(('blk', 'head')), may hold values from -0.09375 to 0.09375
- down_bias: bfloat16 [1024], P(('blk', 'head')), may hold values from -1.75 to 1.75
Outputs:
- layer_output: bfloat16 [16384, 1024], P(('blk', 'head'))
- input_grad: bfloat16 [16384, 1024], P(('blk', 'head'))
- first_gain_grad: float32 [1024], P(('blk', 'head'))
- first_shift_grad: float32 [1024], P(('blk', 'head'))
- joined_weight_grad: float32 [1024, 3072], P(('blk', 'head'))
- joined_bias_grad: float32 [2048], P(('blk', 'head'))
- dense_weight_grad: float32 [1024, 1024], P(('blk', 'head'))
- dense_bias_grad: float32 [1024], P(('blk', 'head'))
- second_gain_grad: float32 [1024], P(('blk', 'head'))
- second_shift_grad: float32 [1024], P(('blk', 'head'))
- up_weight_grad: float32 [1024, 4096], P(('blk', 'head'))
- up_bias_grad: float32 [4096], P(('blk', 'head'))
- down_weight_grad: float32 [4096, 1024], P(('blk', 'head'))
- down_bias_grad: float32 [1024], P(('blk', 'head'))
Inputs may be any that keep to these rules, and one draw needn't show every extreme that they name: The lengths sum to 16384; the longest document stands at index 16. `joined_weight`: entries are independent, of mean 0, within 6 * (2 / 1024)^(1/2) in magnitude.
All inputs are finite; a program needn't handle non-finite values.
Results may differ from a plain program's by a relative error of at most 0.013.
Values may be sent and summed in bfloat16 or wider, within the bound.
No kernel may reach another device: no remote copies, remote signals or barrier semaphores. Data moves between devices by JAX's collectives and lax.ppermute only.
A program may use at most 256 MiB of HBM per device.

v0:
```python
import jax
import jax.numpy as jnp
from jax import lax
from jax.sharding import PartitionSpec as P

HEADS = 16
HEAD_DIM = 64
WINDOW = 1024
NDOCS = 32


norm_eps = 1e-05


def shifted(block, axis, distance):
    devices = range(lax.axis_size(axis))
    route = [(i - distance, i) for i in devices if i - distance in devices]
    return lax.ppermute(block, axis, route)


def layer_norm(values, gain_row, shift_row):
    centred = values - jnp.mean(values, axis=-1, keepdims=True)
    spread = jnp.mean(centred * centred, axis=-1, keepdims=True)
    return centred * lax.rsqrt(spread + norm_eps) * gain_row + shift_row


def gelu_tanh(values):
    return jax.nn.gelu(values, approximate=True)


def cross_dot(left_side, right_side):
    return lax.dot_general(
        left_side, right_side, (((0,), (0,)), ((), ())), preferred_element_type=jnp.float32
    )


def back_dot(left_side, right_side):
    return lax.dot_general(
        left_side, right_side, (((1,), (1,)), ((), ())), preferred_element_type=jnp.float32
    )


def segment_ids(lengths, valid_count, positions):
    doc_ends = jnp.cumsum(lengths)
    passed = jnp.sum((doc_ends[None, :] <= positions[:, None]).astype(jnp.int32), axis=1)
    inside = jnp.where(positions < valid_count[0], passed, NDOCS)
    return jnp.where(positions < 0, -1, inside)


def head_slopes(first_head, head_group):
    order = first_head + jnp.arange(head_group, dtype=jnp.int32)
    return jnp.exp2(-8.0 * (order.astype(jnp.float32) + 1.0) / HEADS)


def widen_bias(joined_bias):
    pair_view = joined_bias.reshape(HEADS, 2, HEAD_DIM)
    key_zeros = jnp.zeros_like(pair_view[:, :1])
    return jnp.concatenate([pair_view[:, :1], key_zeros, pair_view[:, 1:]], axis=1).reshape(
        3 * HEADS * HEAD_DIM
    )


def on_device(
    tokens,
    cotangent,
    lengths,
    valid_count,
    first_gain,
    first_shift,
    joined_weight,
    joined_bias,
    dense_weight,
    dense_bias,
    second_gain,
    second_shift,
    up_weight,
    up_bias,
    down_weight,
    down_bias,
):
    shards = (
        first_gain,
        first_shift,
        joined_weight,
        joined_bias,
        dense_weight,
        dense_bias,
        second_gain,
        second_shift,
        up_weight,
        up_bias,
        down_weight,
        down_bias,
    )
    gathered = (
        lax.all_gather(shards[0], ("blk", "head"), axis=0, tiled=True),
        lax.all_gather(shards[1], ("blk", "head"), axis=0, tiled=True),
        lax.all_gather(shards[2], ("blk", "head"), axis=0, tiled=True),
        lax.all_gather(shards[3], ("blk", "head"), axis=0, tiled=True),
        lax.all_gather(shards[4], ("blk", "head"), axis=0, tiled=True),
        lax.all_gather(shards[5], ("blk", "head"), axis=0, tiled=True),
        lax.all_gather(shards[6], ("blk", "head"), axis=0, tiled=True),
        lax.all_gather(shards[7], ("blk", "head"), axis=0, tiled=True),
        lax.all_gather(shards[8], ("blk", "head"), axis=0, tiled=True),
        lax.all_gather(shards[9], ("blk", "head"), axis=0, tiled=True),
        lax.all_gather(shards[10], ("blk", "head"), axis=0, tiled=True),
        lax.all_gather(shards[11], ("blk", "head"), axis=0, tiled=True),
    )
    (
        gain_one,
        shift_one,
        joined_mat,
        joined_vec,
        dense_mat,
        dense_vec,
        gain_two,
        shift_two,
        up_mat,
        up_vec,
        down_mat,
        down_vec,
    ) = gathered
    tok_rows = tokens.shape[0]
    head_count = lax.axis_size("head")
    head_group = HEADS // head_count
    block_rows = tok_rows * head_count
    query_rows = min(512, block_rows)
    block_count = block_rows // query_rows
    scale = HEAD_DIM ** (-0.5)
    blk_index = lax.axis_index("blk")
    head_index = lax.axis_index("head")
    values = tokens.astype(jnp.float32)
    gain_one_f = gain_one.astype(jnp.float32)
    shift_one_f = shift_one.astype(jnp.float32)
    normed_one = layer_norm(values, gain_one_f, shift_one_f).astype(jnp.bfloat16)
    joined = jnp.dot(normed_one, joined_mat, preferred_element_type=jnp.float32) + widen_bias(
        joined_vec.astype(jnp.float32)
    )
    by_heads = lax.all_to_all(
        joined.astype(jnp.bfloat16), "head", split_axis=1, concat_axis=0, tiled=True
    )
    grouped = by_heads.reshape(block_rows, head_group, 3 * HEAD_DIM)
    queries = grouped[:, :, :HEAD_DIM]
    pairs_own = grouped[:, :, HEAD_DIM:].reshape(block_rows, head_group * 2 * HEAD_DIM)
    prior_pairs = shifted(pairs_own[block_rows - WINDOW :], "blk", 1)
    pairs_ext = jnp.concatenate([prior_pairs, pairs_own], axis=0).reshape(
        WINDOW + block_rows, head_group, 2, HEAD_DIM
    )
    first_pos = blk_index * block_rows - WINDOW
    positions = first_pos + jnp.arange(WINDOW + block_rows, dtype=jnp.int32)
    seg_ext = segment_ids(lengths, valid_count, positions)
    slopes = head_slopes(head_index * head_group, head_group)
    row_index = jnp.arange(query_rows, dtype=jnp.int32)
    key_index = jnp.arange(query_rows + WINDOW, dtype=jnp.int32)
    gap_size = row_index[:, None] + WINDOW - key_index[None, :]
    offsets = (-gap_size).astype(jnp.float32)

    def block_scores(start):
        query_block = lax.dynamic_slice_in_dim(queries, start, query_rows, 0)
        pair_block = lax.dynamic_slice_in_dim(pairs_ext, start, query_rows + WINDOW, 0)
        seg_query = lax.dynamic_slice_in_dim(seg_ext, start + WINDOW, query_rows, 0)
        seg_keys = lax.dynamic_slice_in_dim(seg_ext, start, query_rows + WINDOW, 0)
        allowed = (seg_query[:, None] == seg_keys[None, :]) & (gap_size >= 0) & (gap_size < WINDOW)
        raw = (
            jnp.einsum(
                "qhd,khd->hqk", query_block, pair_block[:, :, 0], preferred_element_type=jnp.float32
            )
            * scale
        )
        raw = raw + slopes[:, None, None] * offsets[None]
        return (jnp.where(allowed[None], raw, -1e30), query_block, pair_block)

    def attend(start):
        scores, query_block, pair_block = block_scores(start)
        top_score = jnp.max(scores, axis=-1, keepdims=True)
        raised = jnp.exp(scores - top_score)
        row_total = jnp.sum(raised, axis=-1, keepdims=True)
        attend_prob = (raised / row_total).astype(jnp.bfloat16)
        context_block = jnp.einsum(
            "hqk,khd->qhd", attend_prob, pair_block[:, :, 1], preferred_element_type=jnp.float32
        )
        log_total = top_score[..., 0] + jnp.log(row_total[..., 0])
        return (context_block.astype(jnp.bfloat16), log_total)

    starts = jnp.arange(block_count, dtype=jnp.int32) * query_rows
    context_parts, log_totals = lax.map(attend, starts)
    context = context_parts.reshape(block_rows, head_group * HEAD_DIM)
    context_tok = lax.all_to_all(context, "head", split_axis=0, concat_axis=1, tiled=True)
    branch_one = jnp.dot(
        context_tok, dense_mat, preferred_element_type=jnp.float32
    ) + dense_vec.astype(jnp.float32)
    middle = values + branch_one
    gain_two_f = gain_two.astype(jnp.float32)
    shift_two_f = shift_two.astype(jnp.float32)
    normed_two = layer_norm(middle, gain_two_f, shift_two_f).astype(jnp.bfloat16)
    pre_act = jnp.dot(normed_two, up_mat, preferred_element_type=jnp.float32) + up_vec.astype(
        jnp.float32
    )
    hidden = gelu_tanh(pre_act).astype(jnp.bfloat16)
    branch_two = jnp.dot(hidden, down_mat, preferred_element_type=jnp.float32) + down_vec.astype(
        jnp.float32
    )
    token_first = (blk_index * head_count + head_index) * tok_rows
    live_rows = token_first + jnp.arange(tok_rows, dtype=jnp.int32) < valid_count[0]
    layer_output = jnp.where(live_rows[:, None], middle + branch_two, 0.0).astype(jnp.bfloat16)
    again = (
        lax.all_gather(shards[0], ("blk", "head"), axis=0, tiled=True),
        lax.all_gather(shards[1], ("blk", "head"), axis=0, tiled=True),
        lax.all_gather(shards[2], ("blk", "head"), axis=0, tiled=True),
        lax.all_gather(shards[3], ("blk", "head"), axis=0, tiled=True),
        lax.all_gather(shards[4], ("blk", "head"), axis=0, tiled=True),
        lax.all_gather(shards[5], ("blk", "head"), axis=0, tiled=True),
        lax.all_gather(shards[6], ("blk", "head"), axis=0, tiled=True),
        lax.all_gather(shards[7], ("blk", "head"), axis=0, tiled=True),
        lax.all_gather(shards[8], ("blk", "head"), axis=0, tiled=True),
        lax.all_gather(shards[9], ("blk", "head"), axis=0, tiled=True),
        lax.all_gather(shards[10], ("blk", "head"), axis=0, tiled=True),
        lax.all_gather(shards[11], ("blk", "head"), axis=0, tiled=True),
    )
    joined_back = again[2]
    dense_back = again[4]
    up_back = again[8]
    down_back = again[10]
    out_change = jnp.where(live_rows[:, None], cotangent.astype(jnp.float32), 0.0)
    change_low = out_change.astype(jnp.bfloat16)
    down_vec_grad = jnp.sum(out_change, axis=0)
    down_mat_grad = cross_dot(hidden, change_low)
    hidden_change = back_dot(change_low, down_back)
    gelu_pull = jax.vjp(gelu_tanh, pre_act)[1]
    pre_change = gelu_pull(hidden_change)[0].astype(jnp.bfloat16)
    up_vec_grad = jnp.sum(pre_change.astype(jnp.float32), axis=0)
    up_mat_grad = cross_dot(normed_two, pre_change)
    normed_change = back_dot(pre_change, up_back)
    second_pull = jax.vjp(layer_norm, middle, gain_two_f, shift_two_f)[1]
    middle_norm, gain_two_grad, shift_two_grad = second_pull(normed_change)
    middle_change = out_change + middle_norm
    branch_change = middle_change.astype(jnp.bfloat16)
    dense_vec_grad = jnp.sum(branch_change.astype(jnp.float32), axis=0)
    dense_mat_grad = cross_dot(context_tok, branch_change)
    context_change = back_dot(branch_change, dense_back).astype(jnp.bfloat16)
    change_heads = lax.all_to_all(
        context_change, "head", split_axis=1, concat_axis=0, tiled=True
    ).reshape(block_rows, head_group, HEAD_DIM)

    def attend_back(carry_pairs, step_index):
        start = step_index * query_rows
        scores, query_block, pair_block = block_scores(start)
        attend_prob = jnp.exp(scores - log_totals[step_index][..., None])
        prob_low = attend_prob.astype(jnp.bfloat16)
        change_block = lax.dynamic_slice_in_dim(change_heads, start, query_rows, 0)
        prob_change = jnp.einsum(
            "qhd,khd->hqk", change_block, pair_block[:, :, 1], preferred_element_type=jnp.float32
        )
        inner = jnp.sum(attend_prob * prob_change, axis=-1, keepdims=True)
        score_change = (attend_prob * (prob_change - inner)).astype(jnp.bfloat16)
        query_change = (
            jnp.einsum(
                "hqk,khd->qhd",
                score_change,
                pair_block[:, :, 0],
                preferred_element_type=jnp.float32,
            )
            * scale
        )
        key_change = (
            jnp.einsum(
                "hqk,qhd->khd", score_change, query_block, preferred_element_type=jnp.float32
            )
            * scale
        )
        value_change = jnp.einsum(
            "hqk,qhd->khd", prob_low, change_block, preferred_element_type=jnp.float32
        )
        window_sum = lax.dynamic_slice_in_dim(
            carry_pairs, start, query_rows + WINDOW, 0
        ) + jnp.stack([key_change, value_change], axis=2)
        return (lax.dynamic_update_slice_in_dim(carry_pairs, window_sum, start, 0), query_change)

    carry_init = jnp.zeros((WINDOW + block_rows, head_group, 2, HEAD_DIM), jnp.float32)
    pair_grads, query_grads = lax.scan(
        attend_back, carry_init, jnp.arange(block_count, dtype=jnp.int32)
    )
    prior_change = pair_grads[:WINDOW].reshape(WINDOW, head_group * 2 * HEAD_DIM)
    returned = shifted(prior_change.astype(jnp.bfloat16), "blk", -1).astype(prior_change.dtype)
    own_change = pair_grads[WINDOW:].reshape(block_rows, head_group * 2 * HEAD_DIM)
    own_change = jnp.concatenate(
        [own_change[: block_rows - WINDOW], own_change[block_rows - WINDOW :] + returned], axis=0
    )
    joined_change = jnp.concatenate(
        [
            query_grads.reshape(block_rows, head_group, HEAD_DIM),
            own_change.reshape(block_rows, head_group, 2 * HEAD_DIM),
        ],
        axis=2,
    )
    joined_change = joined_change.reshape(block_rows, head_group * 3 * HEAD_DIM).astype(
        jnp.bfloat16
    )
    token_change = lax.all_to_all(joined_change, "head", split_axis=0, concat_axis=1, tiled=True)
    summed = jnp.sum(token_change.astype(jnp.float32), axis=0).reshape(HEADS, 3, HEAD_DIM)
    joined_vec_grad = jnp.concatenate([summed[:, :1], summed[:, 2:]], axis=1).reshape(
        2 * HEADS * HEAD_DIM
    )
    joined_mat_grad = cross_dot(normed_one, token_change)
    normed_one_change = back_dot(token_change, joined_back)
    first_pull = jax.vjp(layer_norm, values, gain_one_f, shift_one_f)[1]
    values_norm, gain_one_grad, shift_one_grad = first_pull(normed_one_change)
    input_grad = (middle_change + values_norm).astype(jnp.bfloat16)
    grads_local = (
        gain_one_grad,
        shift_one_grad,
        joined_mat_grad,
        joined_vec_grad,
        dense_mat_grad,
        dense_vec_grad,
        gain_two_grad,
        shift_two_grad,
        up_mat_grad,
        up_vec_grad,
        down_mat_grad,
        down_vec_grad,
    )
    owned = (
        lax.psum_scatter(grads_local[0], ("blk", "head"), scatter_dimension=0, tiled=True),
        lax.psum_scatter(grads_local[1], ("blk", "head"), scatter_dimension=0, tiled=True),
        lax.psum_scatter(grads_local[2], ("blk", "head"), scatter_dimension=0, tiled=True),
        lax.psum_scatter(grads_local[3], ("blk", "head"), scatter_dimension=0, tiled=True),
        lax.psum_scatter(grads_local[4], ("blk", "head"), scatter_dimension=0, tiled=True),
        lax.psum_scatter(grads_local[5], ("blk", "head"), scatter_dimension=0, tiled=True),
        lax.psum_scatter(grads_local[6], ("blk", "head"), scatter_dimension=0, tiled=True),
        lax.psum_scatter(grads_local[7], ("blk", "head"), scatter_dimension=0, tiled=True),
        lax.psum_scatter(grads_local[8], ("blk", "head"), scatter_dimension=0, tiled=True),
        lax.psum_scatter(grads_local[9], ("blk", "head"), scatter_dimension=0, tiled=True),
        lax.psum_scatter(grads_local[10], ("blk", "head"), scatter_dimension=0, tiled=True),
        lax.psum_scatter(grads_local[11], ("blk", "head"), scatter_dimension=0, tiled=True),
    )
    return (
        layer_output,
        input_grad,
        owned[0],
        owned[1],
        owned[2],
        owned[3],
        owned[4],
        owned[5],
        owned[6],
        owned[7],
        owned[8],
        owned[9],
        owned[10],
        owned[11],
    )


def solution(mesh):
    placed = (
        P(("blk", "head"), None),
        P(("blk", "head"), None),
        P(),
        P(),
        P(("blk", "head")),
        P(("blk", "head")),
        P(("blk", "head"), None),
        P(("blk", "head")),
        P(("blk", "head"), None),
        P(("blk", "head")),
        P(("blk", "head")),
        P(("blk", "head")),
        P(("blk", "head"), None),
        P(("blk", "head")),
        P(("blk", "head"), None),
        P(("blk", "head")),
    )
    return jax.shard_map(
        on_device,
        mesh=mesh,
        in_specs=placed,
        out_specs=(
            P(("blk", "head"), None),
            P(("blk", "head"), None),
            P(("blk", "head")),
            P(("blk", "head")),
            P(("blk", "head"), None),
            P(("blk", "head")),
            P(("blk", "head"), None),
            P(("blk", "head")),
            P(("blk", "head")),
            P(("blk", "head")),
            P(("blk", "head"), None),
            P(("blk", "head")),
            P(("blk", "head"), None),
            P(("blk", "head")),
        ),
        check_vma=False,
    )
```

profile of v0, /device:TPU:0, one launch (start us, length us, event | category | flops | bytes accessed | tf_op | source)
XLA Modules:
  0.0 1670.2 jit_solution(3061031231610628619)
XLA Ops:
  15.3 42.5 %all-reduce.16 = (bf16[2048]{0:T(1024)(128)(2,1)S(1)}, bf16[1024]{0:T(1024)(128)(2,1)S(1)}, bf16[1024]{0:T(1024)(128)(2,1)S(1)}, bf16[1024]{0:T(1024)(128)(2,1)S...) all-reduce(bf16[2048]{0:T(1024)(128)(2,1)S(1)} %dynamic-update-slic, ...), channel_id=1, replica_groups=mesh['blk'=8,'head'=4] {'blk','head'}, use_global_device_ids=true, to_apply=%add.2 | all-reduce | flops 8192 | bytes 32768
  62.1 21.1 %all-gather.6.cloned.1.call-done = bf16[1024,3072]{1,0:T(8,128)(2,1)} async-done(((bf16[32,3072]{1,0:T(8,128)(2,1)}), bf16[1024,3072]{1,0:T(8,128)(2,1)}) %all-gather.6.cloned.1.call-update) | async-done | bytes 6291472 | tf_op jit(solution)/shard_map/all_gather | solution.py:98
  83.2 6.7 add_convert_fusion
  90.1 89.5 %all_to_all.67 = bf16[512,4,768]{2,0,1:T(8,128)(2,1)S(1)} all-to-all(bf16[512,4,768]{2,0,1:T(8,128)(2,1)S(1)} %bitcast.142), channel_id=1, replica_groups=mesh['blk'=8,'head'=4] {'head'}, dimensions={1} | all-to-all | bytes 6291456 | tf_op jit(solution)/shard_map/all_to_all | solution.py:139
  184.0 4.7 reshape.294
  198.1 103.9 %while.34 = (s32[]{:T(128)}, bf16[4,512,4,64]{1,3,2,0:T(8,128)(2,1)}, f32[4,4,512]{2,1,0:T(4,128)S(1)}, s32[4]{0:T(128)S(1)}, bf16[3072,4,2,64]{0,3,1,2:T(8,128)...) while((s32[]{:T(128)}, ...), condition=%wide.region_7.8_spmd.clone.clone.clone, body=%wide.region_4.7_spmd.clone.clone.clone.sunk | while | flops 843970560 | bytes 98136440 | solution.py:186
  205.1 5.6 fusion.127
  210.6 4.5 copy-done
  217.0 7.1 fusion.129
  231.1 5.5 fusion.127
  243.0 7.1 fusion.129
  257.1 5.5 fusion.127
  262.6 4.5 copy-done
  269.0 7.1 fusion.129
  283.0 5.5 fusion.127
  294.9 7.0 fusion.129
  305.6 92.2 %all-gather = bf16[32,1,128]{2,1,0:T(2,128)(2,1)S(1)} all-gather(bf16[1,1,128]{2,1,0:T(2,128)(2,1)S(1)} %bitcast.160), channel_id=1, replica_groups=mesh['blk'=8,'head'=4] {'blk','head'}, dimensions={0}, use_global_device_ids=true | all-gather | bytes 8448 | tf_op jit(solution)/shard_map/all_gather | solution.py:105
  402.0 10.7 fusion.83
  412.7 14.3 convert_reduce_fusion
  427.0 5.5 multiply_reduce_fusion.1
  445.3 29.1 %all-to-all-done.2 = bf16[512,4,256]{2,0,1:T(8,128)(2,1)S(1)} async-done(((bf16[512,4,256]{2,0,1:T(8,128)(2,1)}), bf16[512,4,256]{2,0,1:T(8,128)(2,1)S(1)}, u32[]{:S(2)}, u32[]{:S(2)}) %all-to-all-start.2) | async-done | bytes 1048608 | tf_op jit(solution)/shard_map/all_to_all | solution.py:241
  480.7 178.4 %while.35 = (s32[]{:T(128)}, f32[3072,4,2,64]{0,3,2,1:T(8,128)}, bf16[4,512,4,64]{1,3,2,0:T(8,128)(2,1)}, s32[4]{0:T(128)S(1)}, bf16[2048,4,64]{0,2,1:T(8,128)(2...) while((s32[]{:T(128)}, f32[3072,4,2,64]{0,3,2,1:T(8,128)}, ...), condition=%wide.region_14.15_spmd.clone.clone.clone, body=%wide.region_12.14_spmd.clone.clone.clone.sunk | while | flops 2057041920 | bytes 215290512 | solution.py:280
  481.9 7.6 fusion.136
  493.3 11.2 multiply_reduce_fusion.5
  504.6 6.1 fusion.138
  510.7 6.2 multiply_convert_fusion.5
  526.6 7.6 fusion.136
  538.0 11.2 multiply_reduce_fusion.5
  549.2 6.1 fusion.138
  555.3 6.3 multiply_convert_fusion.5
  571.2 7.6 fusion.136
  582.6 11.2 multiply_reduce_fusion.5
  593.8 6.1 fusion.138
  600.0 6.3 multiply_convert_fusion.5
  615.8 7.6 fusion.136
  627.2 11.2 multiply_reduce_fusion.5
  638.4 6.0 fusion.138
  644.5 6.2 multiply_convert_fusion.5
  677.7 69.2 %all_to_all.68 = bf16[4,512,768]{1,2,0:T(8,128)(2,1)S(1)} all-to-all(bf16[4,512,768]{1,2,0:T(8,128)(2,1)S(1)} %copy.78), channel_id=1, replica_groups=mesh['blk'=8,'head'=4] {'head'}, dimensions={0} | all-to-all | bytes 6291456 | tf_op jit(solution)/shard_map/all_to_all | solution.py:299
  748.8 6.9 fusion.78
  757.3 10.5 fusion.82
  768.5 16.6 fusion.68
  785.8 13.3 select_convert_fusion
  799.8 7.5 fusion.84
  811.4 62.7 %all-reduce.15 = (f32[1024]{0:T(1024)S(1)}, f32[1024]{0:T(1024)S(1)}, f32[2048]{0:T(1024)S(1)}, f32[1024]{0:T(1024)S(1)}, f32[1024]{0:T(1024)S(1)}, /*index=5*/f...) all-reduce(f32[1024]{0:T(1024)S(1)} %get-tuple-element.544, ...), channel_id=2, replica_groups=mesh['blk'=8,'head'=4] {'blk','head'}, use_global_device_ids=true, to_apply=%region_18.19.clone | all-reduce | flops 12288 | bytes 98304
  878.8 52.6 %reduce-scatter.5.cloned.1.call-done = f32[32,3072]{1,0:T(8,128)} async-done(((f32[1024,3072]{1,0:T(8,128)}), f32[32,3072]{1,0:T(8,128)}) %reduce-scatter.5.cloned.1.call-update) | async-done | bytes 393232 | tf_op jit(solution)/shard_map/reduce_scatter | solution.py:326
  931.4 366.3 %reduce-scatter.9.cloned.1.call-done = f32[32,4096]{1,0:T(8,128)} async-done(((f32[1024,4096]{1,0:T(8,128)}), f32[32,4096]{1,0:T(8,128)}) %reduce-scatter.9.cloned.1.call-update) | async-done | bytes 524304 | tf_op jit(solution)/shard_map/reduce_scatter | solution.py:332
  1297.7 365.2 %reduce-scatter.11.cloned.1.call-done = f32[128,1024]{1,0:T(8,128)} async-done(((f32[4096,1024]{1,0:T(8,128)}), f32[128,1024]{1,0:T(8,128)}) %reduce-scatter.11.cloned.1.call-update) | async-done | bytes 524304 | tf_op jit(solution)/shard_map/reduce_scatter | solution.py:334
  (366 shorter events, 153.8 us)
Async XLA Ops:
  7.2 76.0 %all-gather.6.cloned.1.call-start = ((), (), s32[]{:S(2)}) async-start(), calls=%async_computation.8 | async-start | bytes 6488064 | tf_op jit(solution)/shard_map/all_gather | solution.py:98
  7.9 390.0 %all-gather.8.cloned.1.call-start = ((), (), s32[]{:S(2)}) async-start(), calls=%async_computation.9 | async-start | bytes 2162688 | tf_op jit(solution)/shard_map/all_gather | solution.py:100
  8.7 393.3 %all-gather.10.cloned.1.call-start = ((), (), s32[]{:S(2)}) async-start(), calls=%async_computation.10 | async-start | bytes 8650752 | tf_op jit(solution)/shard_map/all_gather | solution.py:104
  9.4 403.3 %all-gather.12.cloned.1.call-start = ((), (), s32[]{:S(2)}) async-start(), calls=%async_computation.11 | async-start | bytes 8650752 | tf_op jit(solution)/shard_map/all_gather | solution.py:106
  58.1 31.7 %copy-start.41 = (f32[1024]{0:T(1024)}, f32[1024]{0:T(1024)S(1)}, u32[]{:S(2)}) copy-start(f32[1024]{0:T(1024)S(1)} %convert_element_type.120) | copy-start | bytes 12292
  58.2 31.7 %copy-start.19 = (f32[1024]{0:T(1024)}, f32[1024]{0:T(1024)S(1)}, u32[]{:S(2)}) copy-start(f32[1024]{0:T(1024)S(1)} %convert_element_type.119) | copy-start | bytes 12292
  59.9 30.0 %copy-start.21 = (f32[512]{0:T(512)}, f32[512]{0:T(512)S(1)}, u32[]{:S(2)}) copy-start(f32[512]{0:T(512)S(1)} %broadcast_multiply_fusion.1) | copy-start | bytes 6148
  62.1 27.8 %copy-start.23 = (f32[512]{0:T(512)}, f32[512]{0:T(512)S(1)}, u32[]{:S(2)}) copy-start(f32[512]{0:T(512)S(1)} %fusion.74) | copy-start | bytes 6148
  189.8 4.9 collective-permute-start
  198.1 107.5 %copy-start.49 = (bf16[128]{0:T(256)(128)(2,1)S(1)}, bf16[128]{0:T(256)(128)(2,1)}, u32[]{:S(2)}) copy-start(bf16[128]{0:T(256)(128)(2,1)} %param.33) | copy-start | bytes 772
  302.0 95.9 %all-to-all-start.1 = ((bf16[4,512,256]{1,2,0:T(8,128)(2,1)}), bf16[4,512,256]{1,2,0:T(8,128)(2,1)S(1)}, u32[]{:S(2)}, u32[]{:S(2)}) async-start(bf16[4,512,256]{1,2,0:T(8,128)(2,1)} %bitcast.152), calls=%async_computation.1 | async-start | bytes 2097152 | tf_op jit(solution)/shard_map/all_to_all | solution.py:188
  305.6 96.4 %copy-start.43 = (f32[1024]{0:T(1024)}, f32[1024]{0:T(1024)S(1)}, u32[]{:S(2)}) copy-start(f32[1024]{0:T(1024)S(1)} %convert_element_type.128) | copy-start | bytes 12292
  305.6 126.9 %copy-start.35 = (f32[1024]{0:T(1024)}, f32[1024]{0:T(1024)S(1)}, u32[]{:S(2)}) copy-start(f32[1024]{0:T(1024)S(1)} %convert_element_type.127) | copy-start | bytes 12292
  397.9 14.8 copy-start.33
  397.9 35.4 %copy-start.45 = (pred[512]{0:T(512)(128)(4,1)}, pred[512]{0:T(512)(128)(4,1)S(1)}, u32[]{:S(2)}) copy-start(pred[512]{0:T(512)(128)(4,1)S(1)} %add_compare_fusion) | copy-start | bytes 1540
  401.6 30.9 %copy-start.3 = (f32[512,1024]{1,0:T(8,128)}, f32[512,1024]{1,0:T(8,128)S(1)}, u32[]{:S(2)}) copy-start(f32[512,1024]{1,0:T(8,128)S(1)} %get-tuple-element.621) | copy-start | bytes 6291460
  401.6 30.9 %copy-start.29 = (f32[512]{0:T(512)}, f32[512]{0:T(512)S(1)}, u32[]{:S(2)}) copy-start(f32[512]{0:T(512)S(1)} %broadcast_multiply_fusion) | copy-start | bytes 6148
  401.9 30.6 %copy-start.37 = (f32[512]{0:T(512)}, f32[512]{0:T(512)S(1)}, u32[]{:S(2)}) copy-start(f32[512]{0:T(512)S(1)} %fusion.75) | copy-start | bytes 6148
  402.0 10.7 copy-start.9
  412.7 14.3 copy-start.50
  438.4 36.1 %all-to-all-start.2 = ((bf16[512,4,256]{2,0,1:T(8,128)(2,1)}), bf16[512,4,256]{2,0,1:T(8,128)(2,1)S(1)}, u32[]{:S(2)}, u32[]{:S(2)}) async-start(bf16[512,4,256]{2,0,1:T(8,128)(2,1)} %bitcast.103), calls=%async_computation.2 | async-start | bytes 2097152 | tf_op jit(solution)/shard_map/all_to_all | solution.py:241
  441.9 437.0 %reduce-scatter.7.cloned.1.call-start = ((), (), s32[]{:S(2)}) async-start(), calls=%async_computation.13 | async-start | bytes 4325376 | tf_op jit(solution)/shard_map/reduce_scatter | solution.py:328
  445.3 486.1 %reduce-scatter.5.cloned.1.call-start = ((), (), s32[]{:S(2)}) async-start(), calls=%async_computation.12 | async-start | bytes 12976128 | tf_op jit(solution)/shard_map/reduce_scatter | solution.py:326
  492.0 18.6 %slice-start = ((s8[12582912]{0:T(1024)(128)(4,1)}), s8[4194304]{0:T(1024)(128)(4,1)S(1)}, s32[]{:S(2)}) async-start(s8[12582912]{0:T(1024)(128)(4,1)} %bitcast.136), calls=%async_computation.16 | async-start | bytes 8388608 | tf_op jit(solution)/shard_map/while
  493.3 17.4 %slice-start.1 = ((s8[12582912]{0:T(1024)(128)(4,1)}), s8[4194304]{0:T(1024)(128)(4,1)S(1)}, s32[]{:S(2)}) async-start(s8[12582912]{0:T(1024)(128)(4,1)} %bitcast.136), calls=%async_computation.17 | async-start | bytes 8388608 | tf_op jit(solution)/shard_map/while
  493.3 17.4 %slice-start.2 = ((s8[12582912]{0:T(1024)(128)(4,1)}), s8[4194304]{0:T(1024)(128)(4,1)S(1)}, s32[]{:S(2)}) async-start(s8[12582912]{0:T(1024)(128)(4,1)} %bitcast.136), calls=%async_computation.18 | async-start | bytes 8388608 | tf_op jit(solution)/shard_map/while
  504.6 14.6 slice-start.3
  536.7 18.6 %slice-start = ((s8[12582912]{0:T(1024)(128)(4,1)}), s8[4194304]{0:T(1024)(128)(4,1)S(1)}, s32[]{:S(2)}) async-start(s8[12582912]{0:T(1024)(128)(4,1)} %bitcast.136), calls=%async_computation.16 | async-start | bytes 8388608 | tf_op jit(solution)/shard_map/while
  538.0 17.3 %slice-start.1 = ((s8[12582912]{0:T(1024)(128)(4,1)}), s8[4194304]{0:T(1024)(128)(4,1)S(1)}, s32[]{:S(2)}) async-start(s8[12582912]{0:T(1024)(128)(4,1)} %bitcast.136), calls=%async_computation.17 | async-start | bytes 8388608 | tf_op jit(solution)/shard_map/while
  538.0 17.3 %slice-start.2 = ((s8[12582912]{0:T(1024)(128)(4,1)}), s8[4194304]{0:T(1024)(128)(4,1)S(1)}, s32[]{:S(2)}) async-start(s8[12582912]{0:T(1024)(128)(4,1)} %bitcast.136), calls=%async_computation.18 | async-start | bytes 8388608 | tf_op jit(solution)/shard_map/while
  549.2 14.5 slice-start.3
  581.3 18.6 %slice-start = ((s8[12582912]{0:T(1024)(128)(4,1)}), s8[4194304]{0:T(1024)(128)(4,1)S(1)}, s32[]{:S(2)}) async-start(s8[12582912]{0:T(1024)(128)(4,1)} %bitcast.136), calls=%async_computation.16 | async-start | bytes 8388608 | tf_op jit(solution)/shard_map/while
  582.6 17.3 %slice-start.1 = ((s8[12582912]{0:T(1024)(128)(4,1)}), s8[4194304]{0:T(1024)(128)(4,1)S(1)}, s32[]{:S(2)}) async-start(s8[12582912]{0:T(1024)(128)(4,1)} %bitcast.136), calls=%async_computation.17 | async-start | bytes 8388608 | tf_op jit(solution)/shard_map/while
  582.6 17.3 %slice-start.2 = ((s8[12582912]{0:T(1024)(128)(4,1)}), s8[4194304]{0:T(1024)(128)(4,1)S(1)}, s32[]{:S(2)}) async-start(s8[12582912]{0:T(1024)(128)(4,1)} %bitcast.136), calls=%async_computation.18 | async-start | bytes 8388608 | tf_op jit(solution)/shard_map/while
  593.8 14.6 slice-start.3
  625.9 18.6 %slice-start = ((s8[12582912]{0:T(1024)(128)(4,1)}), s8[4194304]{0:T(1024)(128)(4,1)S(1)}, s32[]{:S(2)}) async-start(s8[12582912]{0:T(1024)(128)(4,1)} %bitcast.136), calls=%async_computation.16 | async-start | bytes 8388608 | tf_op jit(solution)/shard_map/while
  627.2 17.3 %slice-start.1 = ((s8[12582912]{0:T(1024)(128)(4,1)}), s8[4194304]{0:T(1024)(128)(4,1)S(1)}, s32[]{:S(2)}) async-start(s8[12582912]{0:T(1024)(128)(4,1)} %bitcast.136), calls=%async_computation.17 | async-start | bytes 8388608 | tf_op jit(solution)/shard_map/while
  627.2 17.3 %slice-start.2 = ((s8[12582912]{0:T(1024)(128)(4,1)}), s8[4194304]{0:T(1024)(128)(4,1)S(1)}, s32[]{:S(2)}) async-start(s8[12582912]{0:T(1024)(128)(4,1)} %bitcast.136), calls=%async_computation.18 | async-start | bytes 8388608 | tf_op jit(solution)/shard_map/while
  638.4 14.5 slice-start.3
  662.6 8.0 collective-permute-start.1
  677.6 71.2 %copy-start.2 = (bf16[512,1024]{1,0:T(8,128)(2,1)S(1)}, bf16[512,1024]{1,0:T(8,128)(2,1)}, u32[]{:S(2)}) copy-start(bf16[512,1024]{1,0:T(8,128)(2,1)} %param.20) | copy-start | bytes 3145732
  677.6 71.2 %copy-start.20 = (f32[1024]{0:T(1024)S(1)}, f32[1024]{0:T(1024)}, u32[]{:S(2)}) copy-start(f32[1024]{0:T(1024)} %copy-done.19) | copy-start | bytes 12292
  677.6 71.1 %copy-start.22 = (f32[512]{0:T(512)S(1)}, f32[512]{0:T(512)}, u32[]{:S(2)}) copy-start(f32[512]{0:T(512)} %copy-done.21) | copy-start | bytes 6148
  677.7 71.1 %copy-start.24 = (f32[512]{0:T(512)S(1)}, f32[512]{0:T(512)}, u32[]{:S(2)}) copy-start(f32[512]{0:T(512)} %copy-done.23) | copy-start | bytes 6148
  677.7 71.1 %copy-start.42 = (f32[1024]{0:T(1024)S(1)}, f32[1024]{0:T(1024)}, u32[]{:S(2)}) copy-start(f32[1024]{0:T(1024)} %copy-done.41) | copy-start | bytes 12292
  755.7 542.0 %reduce-scatter.9.cloned.1.call-start = ((), (), s32[]{:S(2)}) async-start(), calls=%async_computation.14 | async-start | bytes 17301504 | tf_op jit(solution)/shard_map/reduce_scatter | solution.py:332
  767.8 895.1 %reduce-scatter.11.cloned.1.call-start = ((), (), s32[]{:S(2)}) async-start(), calls=%async_computation.15 | async-start | bytes 17301504 | tf_op jit(solution)/shard_map/reduce_scatter | solution.py:334
  785.8 13.3 copy-start.8
  (48 other events, 155.5 us)
Sparse Core Ops, SparseCore 0:
  10.9 72.2 all-gather.5
  86.1 62.8 all-gather.7
  152.0 81.1 all-gather.9
  236.0 76.3 all-gather.11
  445.4 158.5 reduce-scatter.6
  755.9 175.4 reduce-scatter.4
  934.4 363.3 reduce-scatter.8
  1300.7 362.1 reduce-scatter.10
where the time goes:
time: 1680 us; the launch traced here: 1670 us
  waiting for transfers between devices  841 us (50%)
  blocking collectives  356 us (21%)
  matrix products  273 us (16%)
  local copies, waits for them, and re-layouts  78.9 us (5%)
  other arithmetic  63.8 us (4%)
  loops' own time  29.5 us (2%)
    reduce_scatter x1, waiting for transfers between devices, on_device(): lax.psum_scatter(grads_local[8], ('blk', 'head'), scatter_dimension=0, ti...  366 us
    reduce_scatter x1, waiting for transfers between devices, on_device(): lax.psum_scatter(grads_local[10], ('blk', 'head'), scatter_dimension=0, t...  365 us
    unnamed x2, blocking collectives  105 us
    all_gather x1, blocking collectives, on_device(): lax.all_gather(shards[9], ('blk', 'head'), axis=0, tiled=True)  92.2 us
    all_to_all x1, blocking collectives, on_device(): lax.all_to_all(joined.astype(jnp.bfloat16), 'head', split_axis=1, concat_...  89.5 us
    all_to_all x1, blocking collectives, on_device(): lax.all_to_all(joined_change, 'head', split_axis=0, concat_axis=1, tiled=...  69.2 us
    dot_general x8, matrix products, block_scores(): jnp.einsum('qhd,khd->hqk', query_block, pair_block[:, :, 0], preferred_el...  67.1 us
    reduce_scatter x1, waiting for transfers between devices, on_device(): lax.psum_scatter(grads_local[2], ('blk', 'head'), scatter_dimension=0, ti...  52.6 us
  transfers between devices with their start and end apart: 12, of which 6 were waited for; matrix products, arithmetic and copies ran while one was open for 22% of the time, Pallas kernels for 0%

commit v1 on v0

v1 whole, which is shorter than its diff:
```python
import functools

import jax
import jax.numpy as jnp
import numpy as np
from jax import lax
from jax.experimental import pallas as pl
from jax.experimental.pallas import tpu as pltpu
from jax.sharding import PartitionSpec as P

HEADS = 16
HEAD_DIM = 64
WINDOW = 1024
NDOCS = 32

BOTH = ("blk", "head")
norm_eps = 1e-05
bf16 = jnp.bfloat16
f32 = jnp.float32

MASKED = -1e30
TILE = 256
LANES = 128
SLOPE_LANE = NDOCS + 1
ROW_LANE = SLOPE_LANE + 6
SCALE = HEAD_DIM**-0.5


class Grid:
    def __init__(self):
        blocks, heads = lax.axis_size("blk"), lax.axis_size("head")
        self.count = blocks * heads
        self.size = (2, blocks // 4, 2, heads)
        blk, z = lax.axis_index("blk"), lax.axis_index("head")
        self.here = (blk // (2 * self.size[1]), blk // 2 % self.size[1], blk % 2, z)
        self.linear = blk * heads + z

    def next_along(self, axis):
        places = np.arange(self.count).reshape(self.size)
        return list(zip(places.ravel().tolist(), np.roll(places, -1, axis).ravel().tolist()))

    def shift(self, block, axis):
        return lax.ppermute(block, BOTH, self.next_along(axis))

    def to_later(self, block):
        return lax.ppermute(block, BOTH, [(i, i + 1) for i in range(self.count - 1)])

    def to_earlier(self, block):
        return lax.ppermute(block, BOTH, [(i + 1, i) for i in range(self.count - 1)])


Y, X, CORE, Z = range(4)


def ring_gather(grid, block, axis):
    pieces = [block]
    for _ in range(grid.size[axis] - 1):
        pieces.append(grid.shift(pieces[-1], axis))
    return pieces


def gather(grid, shard):
    rows, width = shard.shape
    size = grid.size
    y, x, core, z = grid.here
    half = size[Z] // 2
    line = jnp.zeros((size[Z], rows, width), shard.dtype)
    for step, piece in enumerate(ring_gather(grid, shard, Z)):
        line = lax.dynamic_update_slice(line, piece[None], ((z - step) % size[Z], 0, 0))
    whole = jnp.zeros((*size, rows, width), shard.dtype)
    for part, (one, two) in enumerate(((X, Y), (Y, X))):
        near = jnp.stack(ring_gather(grid, line[part * half : (part + 1) * half], one))
        for far_step, piece in enumerate(ring_gather(grid, near, two)):
            other = grid.shift(piece, CORE)
            for near_step in range(size[one]):
                at = {one: (grid.here[one] - near_step) % size[one], two: (grid.here[two] - far_step) % size[two]}
                for block, which in ((piece, core), (other, 1 - core)):
                    whole = lax.dynamic_update_slice(
                        whole, block[near_step][None, None, None], (at[Y], at[X], which, part * half, 0, 0)
                    )
    return whole.reshape(grid.count * rows, width)


def ring_reduce(grid, terms, axis, dim, last_type=bf16):
    count, place = grid.size[axis], grid.here[axis]

    def term(step):
        return lax.dynamic_index_in_dim(terms, (place - step) % count, dim, keepdims=False)

    total = term(1)
    for step in range(2, count + 1):
        arrived = grid.shift(total, axis)
        total = (arrived.astype(f32) + term(step).astype(f32)).astype(last_type if step == count else terms.dtype)
    return total


def reduce_scatter(grid, terms):
    rows, width = terms.shape[0] // grid.count, terms.shape[1]
    terms = ring_reduce(grid, terms.reshape(*grid.size, rows, width), CORE, 2, terms.dtype)
    half = grid.size[Z] // 2
    one = ring_reduce(grid, terms[:, :, :half], X, 1, terms.dtype)
    one = ring_reduce(grid, one, Y, 0, terms.dtype)
    two = ring_reduce(grid, terms[:, :, half:], Y, 0, terms.dtype)
    two = ring_reduce(grid, two, X, 0, terms.dtype)
    return ring_reduce(grid, jnp.concatenate([one, two], axis=0), Z, 0, f32)


def reduce_scatter_small(grid, terms):
    terms = terms.reshape(*grid.size, terms.shape[1])
    for axis, dim in ((CORE, 2), (X, 1), (Y, 0), (Z, 0)):
        terms = ring_reduce(grid, terms, axis, dim, terms.dtype)
    return terms


def dot_nn(left, right):
    return lax.dot_general(left, right, (((1,), (0,)), ((), ())), preferred_element_type=f32)


def dot_nt(left, right):
    return lax.dot_general(left, right, (((1,), (1,)), ((), ())), preferred_element_type=f32)


def dot_tn(left, right):
    return lax.dot_general(left, right, (((0,), (0,)), ((), ())), preferred_element_type=f32)


def thirds(values):
    high = values.astype(bf16)
    rest = values - high.astype(f32)
    middle = rest.astype(bf16)
    return high, middle, (rest - middle.astype(f32)).astype(bf16)


def slope_lanes():
    lanes = np.zeros((HEADS // 2, 8, LANES), np.float32)
    for h in range(HEADS):
        rest = np.float32(2.0 ** (-8.0 * (h + 1) / HEADS))
        for part in range(3):
            piece = np.float32(rest.astype(bf16))
            rest = np.float32(rest - piece)
            lanes[h // 2, h % 2, SLOPE_LANE + part] = piece
            lanes[h // 2, h % 2, SLOPE_LANE + 3 + part] = piece
    return lanes


def side_lanes(seg_ext, tok_rows):
    lane = jnp.arange(LANES, dtype=jnp.int32)
    doc = lane[None, :] <= NDOCS
    seg_query = seg_ext[seg_ext.shape[0] - tok_rows :]
    query_side = jnp.where(doc & (lane[None, :] == seg_query[:, None]), 1.0, 0.0).astype(bf16)
    key_pos = jnp.arange(seg_ext.shape[0], dtype=jnp.int32)[:, None]
    key_side = jnp.where(doc & (lane[None, :] != seg_ext[:, None]), MASKED, 0.0)
    key_side = jnp.where((lane >= SLOPE_LANE) & (lane < SLOPE_LANE + 3), (key_pos // TILE * TILE).astype(f32), key_side)
    key_side = jnp.where((lane >= SLOPE_LANE + 3) & (lane < ROW_LANE), (key_pos % TILE).astype(f32), key_side)
    key_side = jnp.where((lane >= ROW_LANE) & (lane < ROW_LANE + 3), 1.0, key_side)
    return query_side, key_side.astype(bf16)


def key_tiles(tile):
    wide = WINDOW // TILE
    edges = [(tile + step) * TILE for step in (0, 1, wide, wide + 1)]
    return [slice(edges[i], edges[i + 1]) for i in range(3)]


def attend_kernel(query, key, value, query_side, key_side, slope, context, log_total):
    pair = pl.program_id(0)
    lane = lax.broadcasted_iota(jnp.int32, (TILE, LANES), 1)
    causal = lax.broadcasted_iota(jnp.int32, (TILE, TILE), 0) >= lax.broadcasted_iota(jnp.int32, (TILE, TILE), 1)
    keys = jnp.concatenate([key[...], key_side[...]], axis=1)
    for tile in range(query.shape[0] // TILE):
        rows = slice(tile * TILE, (tile + 1) * TILE)
        first, middle, last = key_tiles(tile)
        scaled = query[rows, :] * jnp.asarray(SCALE, bf16)
        outs, logs = [], []
        for half in range(2):
            mine = (lane >= HEAD_DIM) == (half == 1)
            side = query_side[rows, :] + slope[0, half : half + 1, :].astype(bf16)
            queries = jnp.concatenate([jnp.where(mine, scaled, jnp.zeros_like(scaled)), side], axis=1)
            inner = dot_nt(queries, keys[middle])
            outer = jnp.where(causal, dot_nt(queries, keys[last]), dot_nt(queries, keys[first]))
            top = jnp.maximum(jnp.max(inner, axis=1, keepdims=True), jnp.max(outer, axis=1, keepdims=True))
            inner = jnp.exp(inner - top)
            outer = jnp.exp(outer - top)
            total = jnp.sum(inner, axis=1, keepdims=True) + jnp.sum(outer, axis=1, keepdims=True)
            summed = dot_nn(inner.astype(bf16), value[middle, :])
            summed += dot_nn(jnp.where(causal, outer, 0.0).astype(bf16), value[last, :])
            summed += dot_nn(jnp.where(causal, 0.0, outer).astype(bf16), value[first, :])
            outs.append(summed / total)
            logs.append(top + jnp.log(total))
        context[rows, :] = jnp.where(lane < HEAD_DIM, outs[0], outs[1]).astype(bf16)
        before = jnp.where(pair == 0, jnp.zeros((TILE, LANES), f32), log_total[rows, :])
        log_total[rows, :] = jnp.where(lane == 2 * pair, logs[0], jnp.where(lane == 2 * pair + 1, logs[1], before))


def attend(queries, pairs, query_side, key_side, slopes):
    tok_rows, width = queries.shape
    key_rows = pairs.shape[0]
    steps = HEADS // 2
    return pl.pallas_call(
        attend_kernel,
        grid=(steps,),
        in_specs=[
            pl.BlockSpec((tok_rows, LANES), lambda p: (0, p)),
            pl.BlockSpec((key_rows, LANES), lambda p: (0, p)),
            pl.BlockSpec((key_rows, LANES), lambda p: (0, steps + p)),
            pl.BlockSpec((tok_rows, LANES), lambda p: (0, 0)),
            pl.BlockSpec((key_rows, LANES), lambda p: (0, 0)),
            pl.BlockSpec((1, 8, LANES), lambda p: (p, 0, 0)),
        ],
        out_specs=[
            pl.BlockSpec((tok_rows, LANES), lambda p: (0, p)),
            pl.BlockSpec((tok_rows, LANES), lambda p: (0, 0)),
        ],
        out_shape=[
            jax.ShapeDtypeStruct((tok_rows, width), bf16),
            jax.ShapeDtypeStruct((tok_rows, LANES), f32),
        ],
        compiler_params=pltpu.CompilerParams(vmem_limit_bytes=40 * 2**20),
        cost_estimate=pl.CostEstimate(
            flops=HEADS * tok_rows * 1280 * 1024,
            bytes_accessed=4 * (key_rows + tok_rows) * width,
            transcendentals=HEADS * tok_rows * WINDOW,
        ),
    )(queries, pairs, pairs, query_side, key_side, slopes)


def attend_back_kernel(
    query, key, value, change, context, log_total, query_side, key_side, slope,
    query_change, key_change, value_change, key_sum, value_sum,
):
    pair = pl.program_id(0)
    lane = lax.broadcasted_iota(jnp.int32, (TILE, LANES), 1)
    causal = lax.broadcasted_iota(jnp.int32, (TILE, TILE), 0) <= lax.broadcasted_iota(jnp.int32, (TILE, TILE), 1)
    keys = jnp.concatenate([key[...], key_side[...]], axis=1)
    values = jnp.concatenate([value[...], key_side[...]], axis=1)
    keys_across = key[...].T
    key_sum[...] = jnp.zeros_like(key_sum)
    value_sum[...] = jnp.zeros_like(value_sum)

    def row_lanes(column):
        high, middle, low = thirds(column)
        lanes = jnp.where(lane == ROW_LANE + 2, low, jnp.zeros((TILE, LANES), bf16))
        return jnp.where(lane == ROW_LANE, high, jnp.where(lane == ROW_LANE + 1, middle, lanes))

    for tile in range(query.shape[0] // TILE):
        rows = slice(tile * TILE, (tile + 1) * TILE)
        first, middle, last = key_tiles(tile)
        scaled = query[rows, :] * jnp.asarray(SCALE, bf16)
        changed = change[rows, :]
        product = changed.astype(f32) * context[rows, :].astype(f32)
        logs = log_total[rows, :]
        parts = []
        for half in range(2):
            mine = (lane >= HEAD_DIM) == (half == 1)
            asked = jnp.where(mine, scaled, jnp.zeros_like(scaled))
            moved = jnp.where(mine, changed, jnp.zeros_like(changed))
            log_row = jnp.sum(jnp.where(lane == 2 * pair + half, logs, 0.0), axis=1, keepdims=True)
            inner_row = jnp.sum(jnp.where(mine, product, 0.0), axis=1, keepdims=True)
            side = query_side[rows, :] + slope[0, half : half + 1, :].astype(bf16) + row_lanes(-log_row)
            queries = jnp.concatenate([asked, side], axis=1)
            changes = jnp.concatenate([moved, row_lanes(-inner_row)], axis=1)
            prob = jnp.exp(dot_nt(keys[middle], queries))
            prob_edge = jnp.exp(jnp.where(causal, dot_nt(keys[last], queries), dot_nt(keys[first], queries)))
            score = (prob * dot_nt(values[middle], changes)).astype(bf16)
            score_edge = prob_edge * jnp.where(causal, dot_nt(values[last], changes), dot_nt(values[first], changes))
            score_last = jnp.where(causal, score_edge, 0.0).astype(bf16)
            score_first = jnp.where(causal, 0.0, score_edge).astype(bf16)
            value_sum[middle, :] += dot_nn(prob.astype(bf16), moved)
            value_sum[last, :] += dot_nn(jnp.where(causal, prob_edge, 0.0).astype(bf16), moved)
            value_sum[first, :] += dot_nn(jnp.where(causal, 0.0, prob_edge).astype(bf16), moved)
            key_sum[middle, :] += dot_nn(score, asked)
            key_sum[last, :] += dot_nn(score_last, asked)
            key_sum[first, :] += dot_nn(score_first, asked)
            parts.append(
                dot_nn(keys_across[:, middle], score)
                + dot_nn(keys_across[:, last], score_last)
                + dot_nn(keys_across[:, first], score_first)
            )
        entry = lax.broadcasted_iota(jnp.int32, (LANES, TILE), 0)
        query_change[rows, :] = (jnp.where(entry < HEAD_DIM, parts[0], parts[1]).T * SCALE).astype(bf16)
    key_change[...] = key_sum[...].astype(bf16)
    value_change[...] = value_sum[...].astype(bf16)


def attend_back(queries, pairs, change, context, log_total, query_side, key_side, slopes):
    tok_rows, width = queries.shape
    key_rows = pairs.shape[0]
    steps = HEADS // 2
    by_query = pl.BlockSpec((tok_rows, LANES), lambda p: (0, p))
    by_key = pl.BlockSpec((key_rows, LANES), lambda p: (0, p))
    return pl.pallas_call(
        attend_back_kernel,
        grid=(steps,),
        in_specs=[
            by_query,
            by_key,
            pl.BlockSpec((key_rows, LANES), lambda p: (0, steps + p)),
            by_query,
            by_query,
            pl.BlockSpec((tok_rows, LANES), lambda p: (0, 0)),
            pl.BlockSpec((tok_rows, LANES), lambda p: (0, 0)),
            pl.BlockSpec((key_rows, LANES), lambda p: (0, 0)),
            pl.BlockSpec((1, 8, LANES), lambda p: (p, 0, 0)),
        ],
        out_specs=[by_query, by_key, by_key],
        out_shape=[
            jax.ShapeDtypeStruct((tok_rows, width), bf16),
            jax.ShapeDtypeStruct((key_rows, width), bf16),
            jax.ShapeDtypeStruct((key_rows, width), bf16),
        ],
        scratch_shapes=[pltpu.VMEM((key_rows, LANES), f32), pltpu.VMEM((key_rows, LANES), f32)],
        compiler_params=pltpu.CompilerParams(vmem_limit_bytes=40 * 2**20),
        cost_estimate=pl.CostEstimate(
            flops=HEADS * tok_rows * 1280 * 2560,
            bytes_accessed=8 * (key_rows + tok_rows) * width,
            transcendentals=HEADS * tok_rows * WINDOW,
        ),
    )(queries, pairs, pairs, change, context, log_total, query_side, key_side, slopes)


def segment_ids(lengths, valid_count, positions):
    doc_ends = jnp.cumsum(lengths)
    passed = jnp.sum((doc_ends[None, :] <= positions[:, None]).astype(jnp.int32), axis=1)
    inside = jnp.where(positions < valid_count[0], passed, NDOCS)
    return jnp.where(positions < 0, -1, inside)


def normalize(values):
    centred = values - jnp.mean(values, axis=-1, keepdims=True)
    inverse = lax.rsqrt(jnp.mean(centred * centred, axis=-1, keepdims=True) + norm_eps)
    return centred * inverse, inverse


def norm_back(change, normal, inverse, gain):
    scaled = change * gain
    mean_one = jnp.mean(scaled, axis=-1, keepdims=True)
    mean_two = jnp.mean(scaled * normal, axis=-1, keepdims=True)
    return inverse * (scaled - mean_one - normal * mean_two)


ROOT = np.sqrt(2.0 / np.pi).astype(np.float32)


def gelu_parts(values):
    square = values * values
    bent = jnp.tanh(ROOT * (values + 0.044715 * (values * square)))
    rise = 0.5 * (1.0 + bent)
    slope = rise + 0.5 * values * (1.0 - bent * bent) * (ROOT * (1.0 + 3.0 * 0.044715 * square))
    return values * rise, slope


def to_kinds(columns):
    rows = columns.shape[0]
    return columns.reshape(rows, HEADS, 3, HEAD_DIM).swapaxes(1, 2).reshape(rows, 3 * HEADS * HEAD_DIM)


def from_kinds(columns):
    rows = columns.shape[0]
    return columns.reshape(rows, 3, HEADS, HEAD_DIM).swapaxes(1, 2).reshape(rows, 3 * HEADS * HEAD_DIM)


def on_device(
    tokens,
    cotangent,
    lengths,
    valid_count,
    first_gain,
    first_shift,
    joined_weight,
    joined_bias,
    dense_weight,
    dense_bias,
    second_gain,
    second_shift,
    up_weight,
    up_bias,
    down_weight,
    down_bias,
):
    grid = Grid()
    tok_rows, width = tokens.shape
    hops = WINDOW // tok_rows
    shard_rows = joined_weight.shape[0]

    vectors = (first_gain, first_shift, joined_bias, dense_bias, second_gain, second_shift, up_bias, down_bias)
    counts = [v.shape[0] for v in vectors]
    riders = jnp.concatenate(vectors).reshape(shard_rows, -1)
    rider_width = riders.shape[1]
    riders = jnp.pad(riders, ((0, 0), (0, -rider_width % LANES)))
    joined_all = gather(grid, jnp.concatenate([to_kinds(joined_weight), riders], axis=1))
    before = [tokens]
    for _ in range(hops):
        before.append(grid.to_later(before[-1]))
    dense_mat = gather(grid, dense_weight)
    up_mat = gather(grid, up_weight)
    down_mat = gather(grid, down_weight)
    joined_mat = joined_all[:, : 3 * width]
    rows_of = joined_all[:, 3 * width : 3 * width + rider_width].reshape(grid.count, -1).astype(f32)
    cuts = np.cumsum([0] + counts)
    gain_one, shift_one, joined_vec, dense_vec, gain_two, shift_two, up_vec, down_vec = (
        rows_of[:, cuts[i] : cuts[i + 1]].reshape(-1) for i in range(len(counts))
    )
    joined_pairs = joined_vec.reshape(HEADS, 2, HEAD_DIM)
    query_vec = joined_pairs[:, 0].reshape(-1)
    pair_vec = jnp.concatenate([jnp.zeros_like(query_vec), joined_pairs[:, 1].reshape(-1)])

    first_pos = grid.linear * tok_rows - WINDOW
    positions = first_pos + jnp.arange(WINDOW + tok_rows, dtype=jnp.int32)
    seg_ext = segment_ids(lengths, valid_count, positions)
    query_side, key_side = side_lanes(seg_ext, tok_rows)
    slopes = jnp.asarray(slope_lanes())
    live_rows = (positions[WINDOW:] < valid_count[0])[:, None]

    values = tokens.astype(f32)
    normal_ext, inverse_ext = normalize(jnp.concatenate(before[::-1], axis=0).astype(f32))
    normed_ext = (normal_ext * gain_one + shift_one).astype(bf16)
    normed_one = normed_ext[WINDOW:]
    queries = (dot_nn(normed_one, joined_mat[:, :width]) + query_vec).astype(bf16)
    pairs = (dot_nn(normed_ext, joined_mat[:, width:]) + pair_vec).astype(bf16)
    context, log_total = attend(queries, pairs, query_side, key_side, slopes)
    middle = values + dot_nn(context, dense_mat) + dense_vec
    normal_two, inverse_two = normalize(middle)
    normed_two = (normal_two * gain_two + shift_two).astype(bf16)
    pre_act = dot_nn(normed_two, up_mat) + up_vec
    hidden, slope = gelu_parts(pre_act)
    hidden = hidden.astype(bf16)
    layer_output = jnp.where(live_rows, middle + (dot_nn(hidden, down_mat) + down_vec), 0.0).astype(bf16)

    change_low = jnp.where(live_rows, cotangent, jnp.zeros_like(cotangent))
    out_change = change_low.astype(f32)
    down_vec_grad = jnp.sum(out_change, axis=0)
    down_grad = reduce_scatter(grid, dot_tn(hidden, change_low).astype(bf16))
    pre_change = (dot_nt(change_low, down_mat) * slope).astype(bf16)
    up_vec_grad = jnp.sum(pre_change.astype(f32), axis=0)
    up_grad = reduce_scatter(grid, dot_tn(normed_two, pre_change).astype(bf16))
    normed_change = dot_nt(pre_change, up_mat)
    gain_two_grad = jnp.sum(normed_change * normal_two, axis=0)
    shift_two_grad = jnp.sum(normed_change, axis=0)
    middle_change = out_change + norm_back(normed_change, normal_two, inverse_two, gain_two)
    branch_change = middle_change.astype(bf16)
    dense_vec_grad = jnp.sum(branch_change.astype(f32), axis=0)
    dense_grad = reduce_scatter(grid, dot_tn(context, branch_change).astype(bf16))
    context_change = dot_nt(branch_change, dense_mat).astype(bf16)
    query_change, key_change, value_change = attend_back(
        queries, pairs, context_change, context, log_total, query_side, key_side, slopes
    )
    ext_change = dot_nt(key_change, joined_mat[:, width : 2 * width]) + dot_nt(value_change, joined_mat[:, 2 * width :])
    own_change = ext_change[WINDOW:] + dot_nt(query_change, joined_mat[:, :width])
    returned = jnp.zeros((tok_rows, width), f32)
    for hop in range(hops):
        returned = returned + ext_change[hop * tok_rows : (hop + 1) * tok_rows]
        returned = grid.to_earlier(returned.astype(bf16)).astype(f32)
    joined_grad = reduce_scatter(
        grid,
        jnp.concatenate(
            [dot_tn(normed_one, query_change), dot_tn(normed_ext, key_change), dot_tn(normed_ext, value_change)], axis=1
        ).astype(bf16),
    )
    part_change = jnp.concatenate([ext_change[:WINDOW], own_change], axis=0)
    gain_one_grad = jnp.sum(part_change * normal_ext, axis=0)
    shift_one_grad = jnp.sum(part_change, axis=0)
    joined_vec_grad = jnp.stack(
        [
            jnp.sum(query_change.astype(f32), axis=0).reshape(HEADS, HEAD_DIM),
            jnp.sum(value_change.astype(f32), axis=0).reshape(HEADS, HEAD_DIM),
        ],
        axis=1,
    ).reshape(-1)
    input_grad = (
        middle_change + norm_back(own_change + returned, normal_ext[WINDOW:], inverse_ext[WINDOW:], gain_one)
    ).astype(bf16)
    vector_grads = (
        gain_one_grad, shift_one_grad, joined_vec_grad, dense_vec_grad, gain_two_grad, shift_two_grad, up_vec_grad,
        down_vec_grad,
    )
    owned = reduce_scatter_small(grid, jnp.concatenate([v.reshape(grid.count, -1) for v in vector_grads], axis=1))
    owned = [owned[cuts[i] : cuts[i + 1]] for i in range(len(counts))]
    return (
        layer_output,
        input_grad,
        owned[0],
        owned[1],
        from_kinds(joined_grad),
        owned[2],
        dense_grad,
        owned[3],
        owned[4],
        owned[5],
        up_grad,
        owned[6],
        down_grad,
        owned[7],
    )


def solution(mesh):
    rows, vector, same = P(BOTH, None), P(BOTH), P()
    return jax.shard_map(
        on_device,
        mesh=mesh,
        in_specs=(
            rows, rows, same, same, vector, vector, rows, vector, rows, vector, vector, vector, rows, vector, rows, vector
        ),
        out_specs=(rows, rows, vector, vector, rows, vector, rows, vector, vector, vector, rows, vector, rows, vector),
        check_vma=False,
    )
```

time: 1680 us -> 685 us (0.41)
  waiting for transfers between devices: 841 us -> 274 us
  blocking collectives: 356 us -> 0 us
  matrix products: 273 us -> 103 us
  starting transfers between devices: 11.5 us -> 72.6 us
  Pallas kernels: 0 us -> 54.8 us
  local copies, waits for them, and re-layouts: 78.9 us -> 110 us
  loops' own time: 29.5 us -> 0 us
    reduce_scatter x4 -> x0, waiting for transfers between devices: 784 us -> none  [the longest x1 366 us: on_device(): lax.psum_scatter(grads_local[8], ('blk', 'head'), scatter_dimension=0, ti...]
    ppermute x2 -> x86, waiting for transfers between devices: 4.46 us -> 274 us  [the longest x82 271 us: shift(): return lax.ppermute(block, BOTH, self.next_along(axis))]
    dot_general x40 -> x17, matrix products: 273 us -> 103 us  [the longest x6 35.6 us: dot_tn(): lax.dot_general(left, right, (((0,), (0,)), ((), ())), preferred_element_...]
    all_to_all x2 -> x0, blocking collectives: 159 us -> none  [the longest x1 89.5 us: on_device(): lax.all_to_all(joined.astype(jnp.bfloat16), 'head', split_axis=1, concat_...]
    unnamed x2 -> x0, blocking collectives: 105 us -> none
    all_gather x1 -> x0, blocking collectives: 92.2 us -> none  [on_device(): lax.all_gather(shards[9], ('blk', 'head'), axis=0, tiled=True)]
    ppermute x2 -> x86, starting transfers between devices: 4.11 us -> 72.6 us  [the longest x82 65 us: shift(): return lax.ppermute(block, BOTH, self.next_along(axis))]
    pallas_call x0 -> x2, Pallas kernels: none -> 54.8 us  [the longest x1 32.8 us: attend_back(): pl.pallas_call(attend_back_kernel, grid=(steps,), in_specs=[by_query, by_...]
  transfers between devices with their start and end apart: 12 -> 86, of which waited for: 6 -> 41; matrix products, arithmetic and copies ran while one was open for 22% -> 24% of each run, Pallas kernels for 0% -> 3%
where the time goes in v1:
time: 685 us; the launch traced here: 676 us
  waiting for transfers between devices  274 us (40%)
  local copies, waits for them, and re-layouts  110 us (16%)
  matrix products  103 us (15%)
  starting transfers between devices  72.6 us (11%)
  other arithmetic  58.8 us (9%)
  Pallas kernels  54.8 us (8%)
    ppermute x82, waiting for transfers between devices, shift(): return lax.ppermute(block, BOTH, self.next_along(axis))  271 us
    ppermute x82, starting transfers between devices, shift(): return lax.ppermute(block, BOTH, self.next_along(axis))  65 us
    dynamic_update_slice x64, local copies, waits for them, and re-layouts, gather(): lax.dynamic_update_slice(whole, block[near_step][None, None, None], (at[Y...  43.2 us
    dot_general x6, matrix products, dot_tn(): lax.dot_general(left, right, (((0,), (0,)), ((), ())), preferred_element_...  35.6 us
    dot_general x6, matrix products, dot_nt(): lax.dot_general(left, right, (((1,), (1,)), ((), ())), preferred_element_...  34.8 us
    pallas_call x1, Pallas kernels, attend_back(): pl.pallas_call(attend_back_kernel, grid=(steps,), in_specs=[by_query, by_...  32.8 us
    dot_general x5, matrix products, dot_nn(): lax.dot_general(left, right, (((1,), (0,)), ((), ())), preferred_element_...  32.1 us
    convert_element_type x28, other arithmetic, ring_reduce(): (arrived.astype(f32) + term(step).astype(f32)).astype(last_type if step =...  22.4 us
  transfers between devices with their start and end apart: 86, of which 41 were waited for; matrix products, arithmetic and copies ran while one was open for 24% of the time, Pallas kernels for 3%

profile of v1, /device:TPU:0, one launch (start us, length us, event | category | flops | bytes accessed | tf_op | source)
XLA Modules:
  0.0 676.5 jit_solution(8382969406261974083)
XLA Ops:
  0.7 5.4 concatenate.57
  24.6 17.6 %collective-permute-done.13 = bf16[32,1024]{1,0:T(8,128)(2,1)S(1)} collective-permute-done((bf16[32,1024]{1,0:T(8,128)(2,1)}, bf16[32,1024]{1,0:T(8,128)(2,1)S(1)}, u32[]{:S(2)}, u32[]{:S(2)}) %collective-permute-start.13) | collective-permute-done | bytes 65568 | tf_op jit(solution)/shard_map/ppermute | solution.py:43
  44.3 10.6 %collective-permute-done.14 = bf16[32,1024]{1,0:T(8,128)(2,1)S(1)} collective-permute-done((bf16[32,1024]{1,0:T(8,128)(2,1)S(1)}, bf16[32,1024]{1,0:T(8,128)(2,1)S(1)}, u32[]{:S(2)}, u32[]{:S(2)}) %collective-permute-start.14) | collective-permute-done | bytes 65568 | tf_op jit(solution)/shard_map/ppermute | solution.py:43
  55.8 5.3 collective-permute-done.15
  72.4 4.2 collective-permute-done.3
  78.7 7.5 %collective-permute-done.25 = bf16[32,4096]{1,0:T(8,128)(2,1)S(1)} collective-permute-done((bf16[32,4096]{1,0:T(8,128)(2,1)}, bf16[32,4096]{1,0:T(8,128)(2,1)S(1)}, u32[]{:S(2)}, u32[]{:S(2)}) %collective-permute-start.25) | collective-permute-done | bytes 262176 | tf_op jit(solution)/shard_map/ppermute | solution.py:43
  88.9 9.5 %collective-permute-done.4 = bf16[32,3200]{1,0:T(8,128)(2,1)S(1)} collective-permute-done((bf16[32,3200]{1,0:T(8,128)(2,1)S(1)}, bf16[32,3200]{1,0:T(8,128)(2,1)S(1)}, u32[]{:S(2)}, u32[]{:S(2)}) %collective-permute-start.4) | collective-permute-done | bytes 204832 | tf_op jit(solution)/shard_map/ppermute | solution.py:43
  99.3 9.6 %collective-permute-done.26 = bf16[32,4096]{1,0:T(8,128)(2,1)S(1)} collective-permute-done((bf16[32,4096]{1,0:T(8,128)(2,1)S(1)}, bf16[32,4096]{1,0:T(8,128)(2,1)S(1)}, u32[]{:S(2)}, u32[]{:S(2)}) %collective-permute-start.26) | collective-permute-done | bytes 262176 | tf_op jit(solution)/shard_map/ppermute | solution.py:43
  110.0 4.4 broadcast_in_dim.193
  115.6 4.3 broadcast_in_dim.199
  127.9 5.5 collective-permute-done.9
  138.8 5.8 collective-permute-done.42
  150.1 5.7 collective-permute-done.31
  158.6 21.5 %collective-permute-done.7 = bf16[2,2,32,3200]{3,2,1,0:T(8,128)(2,1)S(1)} collective-permute-done((bf16[2,2,32,3200]{3,2,1,0:T(8,128)(2,1)S(1)}, bf16[2,2,32,3200]{3,2,1,0:T(8,128)(2,1)S(1)}, u32[]{:S(2)}, u32[]{:S(2)}) %collective-permute-start.7) | collective-permute-done | bytes 819232 | tf_op jit(solution)/shard_map/ppermute | solution.py:43
  193.9 12.5 %collective-permute-done.40 = bf16[2,2,128,1024]{3,2,1,0:T(8,128)(2,1)} collective-permute-done((bf16[2,2,128,1024]{3,2,1,0:T(8,128)(2,1)S(1)}, bf16[2,2,128,1024]{3,2,1,0:T(8,128)(2,1)}, u32[]{:S(2)}, u32[]{:S(2)}) %collective-permute-start.40) | collective-permute-done | bytes 1048608 | tf_op jit(solution)/shard_map/ppermute | solution.py:43
  211.7 20.4 %collective-permute-done.29 = bf16[2,2,32,4096]{3,2,1,0:T(8,128)(2,1)S(1)} collective-permute-done((bf16[2,2,32,4096]{3,2,1,0:T(8,128)(2,1)S(1)}, bf16[2,2,32,4096]{3,2,1,0:T(8,128)(2,1)S(1)}, u32[]{:S(2)}, u32[]{:S(2)}) %collective-permute-start.29) | collective-permute-done | bytes 1048608 | tf_op jit(solution)/shard_map/ppermute | solution.py:43
  242.1 4.2 add_convert_fusion.1
  250.4 7.1 %add_convert_fusion.key.value = bf16[1536,2048]{1,0:T(8,128)(2,1)S(1)} fusion(bf16[1536,1024]{1,0:T(8,128)(2,1)S(1)} %add_convert_fusion.1, f32[2048]{0:T(1024)S(1)} %concatenate.59, bf16[1024,3200]{1,0:T(8,128)(2,1)S(1)} %bitcast.533), kind=kOutput, calls=%fused_computation | convolution fusion | flops 6448742400 | bytes 13639680 | tf_op jit(solution)/shard_map/dot_general | solution.py:116
  257.6 21.9 %shard_map.272 = (bf16[512,1024]{1,0:T(8,128)(2,1)S(1)}, f32[512,128]{1,0:T(8,128)S(1)}) custom-call(bf16[512,1024]{1,0:T(8,128)(2,1)S(1)} %add_convert_fusion.4.query, bf16[1536,2048]{1,0:T(8,128)(2,1)S(1)} %add_convert_fusion.key.value, bf16[1536,2048]{1,0:T(8,128)(2,1)S(1)} %add_convert_fusion.key.value, ...), custom_call_target="tpu_custom_call" | custom-call | flops 10737418240 | bytes 8388608 | tf_op jit(solution)/shard_map/pallas_call | solution.py:199
  311.9 7.3 %fusion.165 = f32[512,4096]{1,0:T(8,128)S(1)} fusion(bf16[1024,4096]{1,0:T(8,128)(2,1)} %bitcast.78, f32[512,1024]{1,0:T(8,128)S(1)} %copy-done.20, f32[1024]{0:T(1024)S(1)} %add.843, f32[1024]{0:T(1024)S(1)} %mul.170, f32[512]{0:T(512)S(1)} %add_rsqrt_fusion.1, f32[512]{0:T(512)S(1)} %broadcast_multiply_fusion.5), kind=kOutput, calls=%fused_computation.424 | convolution fusion | flops 4297588736 | bytes 18886656 | tf_op jit(solution)/shard_map/dot_general | solution.py:116
  323.7 11.0 %convert_reduce_fusion = (f32[4096]{0:T(1024)S(1)}, bf16[512,4096]{1,0:T(8,128)(2,1)S(1)}) fusion(f32[512,4096]{1,0:T(8,128)S(1)} %fusion.165, f32[4096]{0:T(1024)S(1)} %copy-done.53, bf16[4096,1024]{1,0:T(8,128)(2,1)} %bitcast.104, bf16[512,1024]{1,0:T(8,128)(2,1)S(1)} %copy-done.43, pred[512]{0:T(512)(128)(4,1)S(1)} %slice_compare_fusion), kind=kOutput, calls=%fused_computation.17 | convolution fusion | flops 4339527680 | bytes 22053376 | tf_op jit(solution)/shard_map/dot_general | solution.py:120
  334.8 9.0 %multiply_reduce_fusion = (f32[1024]{0:T(1024)S(1)}, f32[512]{0:T(512)S(1)}, f32[512]{0:T(512)S(1)}, f32[1024]{0:T(1024)S(1)}, f32[512,1024]{1,0:T(8,128)S(1)}) fusion(f32[512,1024]{1,0:T(8,128)S(1)} %copy-done.20, f32[512]{0:T(512)S(1)} %add_rsqrt_fusion.1, f32[512]{0:T(512)S(1)} %broadcast_multiply_fusion.5, f32[1024]{0:T(1024)S(1)} %mul.170, ...), kind=kOutput, calls=%fused_computation.59 | convolution fusion | flops 4299682816 | bytes 16797696 | tf_op jit(solution)/shard_map/dot_general | solution.py:120
  346.7 32.8 %shard_map.273 = (bf16[512,1024]{1,0:T(8,128)(2,1)S(1)}, bf16[1536,1024]{1,0:T(8,128)(2,1)S(1)}, bf16[1536,1024]{1,0:T(8,128)(2,1)S(1)}) custom-call(bf16[512,1024]{1,0:T(8,128)(2,1)S(1)} %copy-done.2, bf16[1536,2048]{1,0:T(8,128)(2,1)} %copy-done.3, bf16[1536,2048]{1,0:T(8,128)(2,1)} %copy-done.3, bf16[512,1024]{1,0:T(8,128)(2,1)S(1)} %convolution_convert_fusion.6.change, ...), custom_call_target="tpu_custom_call" | custom-call | flops 26843545600 | bytes 16777216 | tf_op jit(solution)/shard_map/pallas_call | solution.py:291
  379.6 5.1 fusion.20
  384.7 5.5 convolution_add_fusion
  394.4 4.7 convolution_convert_fusion.3
  399.1 5.1 convolution_convert_fusion.4
  413.3 7.4 %convolution_convert_fusion.1 = bf16[1024,4096]{1,0:T(8,128)(2,1)} fusion(bf16[512,4096]{1,0:T(8,128)(2,1)S(1)} %copy-done.56, f32[512,1024]{1,0:T(8,128)S(1)} %copy-done.21, f32[1024]{0:T(1024)S(1)} %add.843, f32[1024]{0:T(1024)S(1)} %mul.170, f32[512]{0:T(512)S(1)} %add_rsqrt_fusion.1, f32[512]{0:T(512)S(1)} %broadcast_multiply_fusion.5), kind=kOutput, calls=%fused_computation.23 | convolution fusion | flops 4301783040 | bytes 14692352 | tf_op jit(solution)/shard_map/dot_general | solution.py:124
  420.7 13.2 %convolution_convert_fusion = bf16[4096,1024]{1,0:T(8,128)(2,1)} fusion(bf16[512,1024]{1,0:T(8,128)(2,1)S(1)} %copy-done.44, pred[512]{0:T(512)(128)(4,1)S(1)} %slice_compare_fusion, f32[512,4096]{1,0:T(8,128)} %copy-done.54, f32[4096]{0:T(1024)S(1)} %copy-done.53), kind=kOutput, calls=%fused_computation.22 | convolution fusion | flops 4320657408 | bytes 17842688 | tf_op jit(solution)/shard_map/dot_general | solution.py:124
  434.0 12.4 %select_convert_fusion = bf16[512,1024]{1,0:T(8,128)(2,1)} fusion(f32[512,1024]{1,0:T(8,128)S(1)} %copy-done.21, bf16[4096,1024]{1,0:T(8,128)(2,1)} %bitcast.104, f32[1024]{0:T(1024)S(1)} %add.851, pred[512]{0:T(512)(128)(4,1)S(1)} %slice_compare_fusion, f32[512,4096]{1,0:T(8,128)} %copy-done.54, f32[4096]{0:T(1024)S(1)} %copy-done.53), kind=kOutput, calls=%fused_computation.66 | convolution fusion | flops 4318035968 | bytes 19943936 | tf_op jit(solution)/shard_map/dot_general | solution.py:116
  447.7 5.2 fusion.15
  464.3 4.7 dynamic-slice_bitcast_fusion.1
  469.5 4.9 dynamic-slice_bitcast_fusion
  486.8 6.2 collective-permute-done.65
  498.5 4.4 collective-permute-done.66
  524.5 5.4 collective-permute-done.51
  529.9 5.4 collective-permute-done.52
  549.0 6.7 collective-permute-done.55
  557.7 9.4 %collective-permute-done.57 = bf16[2,2,32,3072]{3,2,1,0:T(8,128)(2,1)S(1)} collective-permute-done((bf16[2,2,32,3072]{3,2,1,0:T(8,128)(2,1)S(1)}, bf16[2,2,32,3072]{3,2,1,0:T(8,128)(2,1)S(1)}, u32[]{:S(2)}, u32[]{:S(2)}) %collective-permute-start.57) | collective-permute-done | bytes 786464 | tf_op jit(solution)/shard_map/ppermute | solution.py:43
  576.6 4.4 fusion.10
  584.8 5.7 collective-permute-done.59
  590.7 12.2 %collective-permute-done.71 = bf16[2,2,32,4096]{3,2,1,0:T(8,128)(2,1)} collective-permute-done((bf16[2,2,32,4096]{3,2,1,0:T(8,128)(2,1)S(1)}, bf16[2,2,32,4096]{3,2,1,0:T(8,128)(2,1)}, u32[]{:S(2)}, u32[]{:S(2)}) %collective-permute-start.71) | collective-permute-done | bytes 1048608 | tf_op jit(solution)/shard_map/ppermute | solution.py:43
  607.7 17.6 %collective-permute-done.79 = bf16[2,2,128,1024]{3,2,1,0:T(8,128)(2,1)S(1)} collective-permute-done((bf16[2,2,128,1024]{3,2,1,0:T(8,128)(2,1)S(1)}, bf16[2,2,128,1024]{3,2,1,0:T(8,128)(2,1)S(1)}, u32[]{:S(2)}, u32[]{:S(2)}) %collective-permute-start.79) | collective-permute-done | bytes 1048608 | tf_op jit(solution)/shard_map/ppermute | solution.py:43
  633.6 5.2 collective-permute-done.80
  639.4 5.2 collective-permute-done.75
  645.6 4.8 collective-permute-done.83
  651.3 4.8 collective-permute-done.76
  669.9 5.3 collective-permute-done.85
  (517 shorter events, 258.2 us)
Async XLA Ops:
  8.6 56.9 %collective-permute-start.2 = (bf16[32,3200]{1,0:T(8,128)(2,1)}, bf16[32,3200]{1,0:T(8,128)(2,1)}, u32[]{:S(2)}, u32[]{:S(2)}) collective-permute-start(bf16[32,3200]{1,0:T(8,128)(2,1)} %fusion.111), channel_id=1, source_target_pairs={{0,1},{1,2},{2,3},{3,0},{4,5},{5,6},{6,7},{7,4},{8,9},{9,10},{10,1... | collective-permute-start | bytes 614408 | tf_op jit(solution)/shard_map/ppermute | solution.py:43
  11.7 138.0 %collective-permute-start = (bf16[512,1024]{1,0:T(8,128)(2,1)}, bf16[512,1024]{1,0:T(8,128)(2,1)S(1)}, u32[]{:S(2)}, u32[]{:S(2)}) collective-permute-start(bf16[512,1024]{1,0:T(8,128)(2,1)} %param.17), channel_id=1, source_target_pairs={{0,1},{1,2},{2,3},{3,4},{4,5},{5,6},{6,7},{7,8},{8,9},{9,10},{10,1... | collective-permute-start | bytes 3145736 | tf_op jit(solution)/shard_map/ppermute | solution.py:46
  15.2 27.1 %collective-permute-start.13 = (bf16[32,1024]{1,0:T(8,128)(2,1)}, bf16[32,1024]{1,0:T(8,128)(2,1)S(1)}, u32[]{:S(2)}, u32[]{:S(2)}) collective-permute-start(bf16[32,1024]{1,0:T(8,128)(2,1)} %param.25), channel_id=1, source_target_pairs={{0,1},{1,2},{2,3},{3,0},{4,5},{5,6},{6,7},{7,4},{8,9},{9,10},{10,1... | collective-permute-start | bytes 196616 | tf_op jit(solution)/shard_map/ppermute | solution.py:43
  16.8 49.8 %collective-permute-start.35 = (bf16[128,1024]{1,0:T(8,128)(2,1)}, bf16[128,1024]{1,0:T(8,128)(2,1)}, u32[]{:S(2)}, u32[]{:S(2)}) collective-permute-start(bf16[128,1024]{1,0:T(8,128)(2,1)} %param.31), channel_id=1, source_target_pairs={{0,1},{1,2},{2,3},{3,0},{4,5},{5,6},{6,7},{7,4},{8,9},{9,10},{10,1... | collective-permute-start | bytes 786440 | tf_op jit(solution)/shard_map/ppermute | solution.py:43
  16.8 49.8 %collective-permute-start.24 = (bf16[32,4096]{1,0:T(8,128)(2,1)}, bf16[32,4096]{1,0:T(8,128)(2,1)}, u32[]{:S(2)}, u32[]{:S(2)}) collective-permute-start(bf16[32,4096]{1,0:T(8,128)(2,1)} %param.29), channel_id=1, source_target_pairs={{0,1},{1,2},{2,3},{3,0},{4,5},{5,6},{6,7},{7,4},{8,9},{9,10},{10,1... | collective-permute-start | bytes 786440 | tf_op jit(solution)/shard_map/ppermute | solution.py:43
  66.6 19.5 %collective-permute-start.36 = (bf16[128,1024]{1,0:T(8,128)(2,1)}, bf16[128,1024]{1,0:T(8,128)(2,1)S(1)}, u32[]{:S(2)}, u32[]{:S(2)}) collective-permute-start(bf16[128,1024]{1,0:T(8,128)(2,1)} %collective-permute-done.35), channel_id=1, source_target_pairs={{0,1},{1,2},{2,3},{3,0},{4,5},{5,6},{6,7},{7,4},{8,9},{9,10},{10,1... | collective-permute-start | bytes 786440 | tf_op jit(solution)/shard_map/ppermute | solution.py:43
  70.7 15.4 %collective-permute-start.25 = (bf16[32,4096]{1,0:T(8,128)(2,1)}, bf16[32,4096]{1,0:T(8,128)(2,1)S(1)}, u32[]{:S(2)}, u32[]{:S(2)}) collective-permute-start(bf16[32,4096]{1,0:T(8,128)(2,1)} %collective-permute-done.24), channel_id=1, source_target_pairs={{0,1},{1,2},{2,3},{3,0},{4,5},{5,6},{6,7},{7,4},{8,9},{9,10},{10,1... | collective-permute-start | bytes 786440 | tf_op jit(solution)/shard_map/ppermute | solution.py:43
  72.3 16.4 %collective-permute-start.17 = (bf16[2,2,32,1024]{3,2,1,0:T(8,128)(2,1)S(1)}, bf16[2,2,32,1024]{3,2,1,0:T(8,128)(2,1)S(1)}, u32[]{:S(2)}, u32[]{:S(2)}) collective-permute-start(bf16[2,2,32,1024]{3,2,1,0:T(8,128)(2,1)S(1)} %pad_maximum_fusion.8), channel_id=1, source_target_pairs={{0,4},{1,5},{2,6},{3,7},{4,0},{5,1},{6,2},{7,3},{8,12},{9,13},{10,... | collective-permute-start | bytes 786440 | tf_op jit(solution)/shard_map/ppermute | solution.py:43
  86.1 36.8 %collective-permute-start.21 = (bf16[2,2,32,1024]{3,2,1,0:T(8,128)(2,1)S(1)}, bf16[2,2,32,1024]{3,2,1,0:T(8,128)(2,1)S(1)}, u32[]{:S(2)}, u32[]{:S(2)}) collective-permute-start(bf16[2,2,32,1024]{3,2,1,0:T(8,128)(2,1)S(1)} %pad_maximum_fusion.9), channel_id=1, source_target_pairs={{0,4},{1,5},{2,6},{3,7},{4,0},{5,1},{6,2},{7,3},{8,12},{9,13},{10,... | collective-permute-start | bytes 786440 | tf_op jit(solution)/shard_map/ppermute | solution.py:43
  88.8 26.4 %collective-permute-start.37 = (bf16[128,1024]{1,0:T(8,128)(2,1)S(1)}, bf16[128,1024]{1,0:T(8,128)(2,1)S(1)}, u32[]{:S(2)}, u32[]{:S(2)}) collective-permute-start(bf16[128,1024]{1,0:T(8,128)(2,1)S(1)} %collective-permute-done.36), channel_id=1, source_target_pairs={{0,1},{1,2},{2,3},{3,0},{4,5},{5,6},{6,7},{7,4},{8,9},{9,10},{10,1... | collective-permute-start | bytes 786440 | tf_op jit(solution)/shard_map/ppermute | solution.py:43
  99.2 21.8 %collective-permute-start.19 = (bf16[2,2,32,1024]{3,2,1,0:T(8,128)(2,1)S(1)}, bf16[2,2,32,1024]{3,2,1,0:T(8,128)(2,1)S(1)}, u32[]{:S(2)}, u32[]{:S(2)}) collective-permute-start(bf16[2,2,32,1024]{3,2,1,0:T(8,128)(2,1)S(1)} %collective-permute-done.18), channel_id=1, source_target_pairs={{0,4},{1,5},{2,6},{3,7},{4,0},{5,1},{6,2},{7,3},{8,12},{9,13},{10,... | collective-permute-start | bytes 786440 | tf_op jit(solution)/shard_map/ppermute | solution.py:43
  108.9 14.7 %collective-permute-start.23 = (bf16[2,2,32,1024]{3,2,1,0:T(8,128)(2,1)S(1)}, bf16[2,2,32,1024]{3,2,1,0:T(8,128)(2,1)S(1)}, u32[]{:S(2)}, u32[]{:S(2)}) collective-permute-start(bf16[2,2,32,1024]{3,2,1,0:T(8,128)(2,1)S(1)} %collective-permute-done.22), channel_id=1, source_target_pairs={{0,4},{1,5},{2,6},{3,7},{4,0},{5,1},{6,2},{7,3},{8,12},{9,13},{10,... | collective-permute-start | bytes 786440 | tf_op jit(solution)/shard_map/ppermute | solution.py:43
  122.9 15.8 %collective-permute-start.38 = (bf16[2,128,1024]{2,1,0:T(8,128)(2,1)S(1)}, bf16[2,128,1024]{2,1,0:T(8,128)(2,1)S(1)}, u32[]{:S(2)}, u32[]{:S(2)}) collective-permute-start(bf16[2,128,1024]{2,1,0:T(8,128)(2,1)S(1)} %get-tuple-element.59), channel_id=1, source_target_pairs={{0,8},{1,9},{2,10},{3,11},{4,12},{5,13},{6,14},{7,15},{8,0},{9,1},... | collective-permute-start | bytes 1572872 | tf_op jit(solution)/shard_map/ppermute | solution.py:43
  123.6 21.0 %collective-permute-start.42 = (bf16[2,128,1024]{2,1,0:T(8,128)(2,1)S(1)}, bf16[2,128,1024]{2,1,0:T(8,128)(2,1)S(1)}, u32[]{:S(2)}, u32[]{:S(2)}) collective-permute-start(bf16[2,128,1024]{2,1,0:T(8,128)(2,1)S(1)} %get-tuple-element.58), channel_id=1, source_target_pairs={{0,16},{1,17},{2,18},{3,19},{4,20},{5,21},{6,22},{7,23},{8,24},{9,... | collective-permute-start | bytes 1572872 | tf_op jit(solution)/shard_map/ppermute | solution.py:43
  127.5 22.1 %collective-permute-start.27 = (bf16[2,32,4096]{2,1,0:T(8,128)(2,1)S(1)}, bf16[2,32,4096]{2,1,0:T(8,128)(2,1)S(1)}, u32[]{:S(2)}, u32[]{:S(2)}) collective-permute-start(bf16[2,32,4096]{2,1,0:T(8,128)(2,1)S(1)} %get-tuple-element.55), channel_id=1, source_target_pairs={{0,8},{1,9},{2,10},{3,11},{4,12},{5,13},{6,14},{7,15},{8,0},{9,1},... | collective-permute-start | bytes 1572872 | tf_op jit(solution)/shard_map/ppermute | solution.py:43
  133.4 22.5 %collective-permute-start.31 = (bf16[2,32,4096]{2,1,0:T(8,128)(2,1)}, bf16[2,32,4096]{2,1,0:T(8,128)(2,1)S(1)}, u32[]{:S(2)}, u32[]{:S(2)}) collective-permute-start(bf16[2,32,4096]{2,1,0:T(8,128)(2,1)} %get-tuple-element.54), channel_id=1, source_target_pairs={{0,16},{1,17},{2,18},{3,19},{4,20},{5,21},{6,22},{7,23},{8,24},{9,... | collective-permute-start | bytes 1572872 | tf_op jit(solution)/shard_map/ppermute | solution.py:43
  138.7 19.8 %collective-permute-start.6 = (bf16[2,2,32,3200]{3,2,1,0:T(8,128)(2,1)S(1)}, bf16[2,2,32,3200]{3,2,1,0:T(8,128)(2,1)S(1)}, u32[]{:S(2)}, u32[]{:S(2)}) collective-permute-start(bf16[2,2,32,3200]{3,2,1,0:T(8,128)(2,1)S(1)} %pad_maximum_fusion.6), channel_id=1, source_target_pairs={{0,4},{1,5},{2,6},{3,7},{4,0},{5,1},{6,2},{7,3},{8,12},{9,13},{10,... | collective-permute-start | bytes 2457608 | tf_op jit(solution)/shard_map/ppermute | solution.py:43
  144.6 35.6 %collective-permute-start.7 = (bf16[2,2,32,3200]{3,2,1,0:T(8,128)(2,1)S(1)}, bf16[2,2,32,3200]{3,2,1,0:T(8,128)(2,1)S(1)}, u32[]{:S(2)}, u32[]{:S(2)}) collective-permute-start(bf16[2,2,32,3200]{3,2,1,0:T(8,128)(2,1)S(1)} %pad_maximum_fusion.6), channel_id=1, source_target_pairs={{0,16},{1,17},{2,18},{3,19},{4,20},{5,21},{6,22},{7,23},{8,24},{9,... | collective-permute-start | bytes 2457608 | tf_op jit(solution)/shard_map/ppermute | solution.py:43
  149.6 85.2 %collective-permute-start.10 = (bf16[2,2,32,3200]{3,2,1,0:T(8,128)(2,1)S(1)}, bf16[2,2,32,3200]{3,2,1,0:T(8,128)(2,1)S(1)}, u32[]{:S(2)}, u32[]{:S(2)}) collective-permute-start(bf16[2,2,32,3200]{3,2,1,0:T(8,128)(2,1)S(1)} %pad_maximum_fusion.7), channel_id=1, source_target_pairs={{0,4},{1,5},{2,6},{3,7},{4,0},{5,1},{6,2},{7,3},{8,12},{9,13},{10,... | collective-permute-start | bytes 2457608 | tf_op jit(solution)/shard_map/ppermute | solution.py:43
  149.7 85.2 %collective-permute-start.11 = (bf16[2,2,32,3200]{3,2,1,0:T(8,128)(2,1)S(1)}, bf16[2,2,32,3200]{3,2,1,0:T(8,128)(2,1)S(1)}, u32[]{:S(2)}, u32[]{:S(2)}) collective-permute-start(bf16[2,2,32,3200]{3,2,1,0:T(8,128)(2,1)S(1)} %pad_maximum_fusion.7), channel_id=1, source_target_pairs={{0,8},{1,9},{2,10},{3,11},{4,12},{5,13},{6,14},{7,15},{8,0},{9,1},... | collective-permute-start | bytes 2457608 | tf_op jit(solution)/shard_map/ppermute | solution.py:43
  155.8 27.0 %collective-permute-start.1 = (bf16[512,1024]{1,0:T(8,128)(2,1)S(1)}, bf16[512,1024]{1,0:T(8,128)(2,1)S(1)}, u32[]{:S(2)}, u32[]{:S(2)}) collective-permute-start(bf16[512,1024]{1,0:T(8,128)(2,1)S(1)} %collective-permute-done), channel_id=1, source_target_pairs={{0,1},{1,2},{2,3},{3,4},{4,5},{5,6},{6,7},{7,8},{8,9},{9,10},{10,1... | collective-permute-start | bytes 3145736 | tf_op jit(solution)/shard_map/ppermute | solution.py:46
  158.5 28.4 %collective-permute-start.39 = (bf16[2,2,128,1024]{3,2,1,0:T(8,128)(2,1)S(1)}, bf16[2,2,128,1024]{3,2,1,0:T(8,128)(2,1)S(1)}, u32[]{:S(2)}, u32[]{:S(2)}) collective-permute-start(bf16[2,2,128,1024]{3,2,1,0:T(8,128)(2,1)S(1)} %pad_maximum_fusion.4), channel_id=1, source_target_pairs={{0,4},{1,5},{2,6},{3,7},{4,0},{5,1},{6,2},{7,3},{8,12},{9,13},{10,... | collective-permute-start | bytes 3145736 | tf_op jit(solution)/shard_map/ppermute | solution.py:43
  180.2 26.2 %collective-permute-start.40 = (bf16[2,2,128,1024]{3,2,1,0:T(8,128)(2,1)S(1)}, bf16[2,2,128,1024]{3,2,1,0:T(8,128)(2,1)}, u32[]{:S(2)}, u32[]{:S(2)}) collective-permute-start(bf16[2,2,128,1024]{3,2,1,0:T(8,128)(2,1)S(1)} %pad_maximum_fusion.4), channel_id=1, source_target_pairs={{0,16},{1,17},{2,18},{3,19},{4,20},{5,21},{6,22},{7,23},{8,24},{9,... | collective-permute-start | bytes 3145736 | tf_op jit(solution)/shard_map/ppermute | solution.py:43
  186.8 105.2 %collective-permute-start.43 = (bf16[2,2,128,1024]{3,2,1,0:T(8,128)(2,1)}, bf16[2,2,128,1024]{3,2,1,0:T(8,128)(2,1)}, u32[]{:S(2)}, u32[]{:S(2)}) collective-permute-start(bf16[2,2,128,1024]{3,2,1,0:T(8,128)(2,1)} %pad_maximum_fusion.5), channel_id=1, source_target_pairs={{0,4},{1,5},{2,6},{3,7},{4,0},{5,1},{6,2},{7,3},{8,12},{9,13},{10,... | collective-permute-start | bytes 3145736 | tf_op jit(solution)/shard_map/ppermute | solution.py:43
  188.9 94.6 %collective-permute-start.44 = (bf16[2,2,128,1024]{3,2,1,0:T(8,128)(2,1)}, bf16[2,2,128,1024]{3,2,1,0:T(8,128)(2,1)}, u32[]{:S(2)}, u32[]{:S(2)}) collective-permute-start(bf16[2,2,128,1024]{3,2,1,0:T(8,128)(2,1)} %pad_maximum_fusion.5), channel_id=1, source_target_pairs={{0,8},{1,9},{2,10},{3,11},{4,12},{5,13},{6,14},{7,15},{8,0},{9,1},... | collective-permute-start | bytes 3145736 | tf_op jit(solution)/shard_map/ppermute | solution.py:43
  206.4 25.7 %collective-permute-start.29 = (bf16[2,2,32,4096]{3,2,1,0:T(8,128)(2,1)S(1)}, bf16[2,2,32,4096]{3,2,1,0:T(8,128)(2,1)S(1)}, u32[]{:S(2)}, u32[]{:S(2)}) collective-permute-start(bf16[2,2,32,4096]{3,2,1,0:T(8,128)(2,1)S(1)} %pad_maximum_fusion.2), channel_id=1, source_target_pairs={{0,16},{1,17},{2,18},{3,19},{4,20},{5,21},{6,22},{7,23},{8,24},{9,... | collective-permute-start | bytes 3145736 | tf_op jit(solution)/shard_map/ppermute | solution.py:43
  234.4 65.6 %collective-permute-start.32 = (bf16[2,2,32,4096]{3,2,1,0:T(8,128)(2,1)}, bf16[2,2,32,4096]{3,2,1,0:T(8,128)(2,1)}, u32[]{:S(2)}, u32[]{:S(2)}) collective-permute-start(bf16[2,2,32,4096]{3,2,1,0:T(8,128)(2,1)} %pad_maximum_fusion.3), channel_id=1, source_target_pairs={{0,4},{1,5},{2,6},{3,7},{4,0},{5,1},{6,2},{7,3},{8,12},{9,13},{10,... | collective-permute-start | bytes 3145736 | tf_op jit(solution)/shard_map/ppermute | solution.py:43
  234.8 49.2 %collective-permute-start.33 = (bf16[2,2,32,4096]{3,2,1,0:T(8,128)(2,1)}, bf16[2,2,32,4096]{3,2,1,0:T(8,128)(2,1)}, u32[]{:S(2)}, u32[]{:S(2)}) collective-permute-start(bf16[2,2,32,4096]{3,2,1,0:T(8,128)(2,1)} %pad_maximum_fusion.3), channel_id=1, source_target_pairs={{0,8},{1,9},{2,10},{3,11},{4,12},{5,13},{6,14},{7,15},{8,0},{9,1},... | collective-permute-start | bytes 3145736 | tf_op jit(solution)/shard_map/ppermute | solution.py:43
  238.3 45.8 %collective-permute-start.41 = (bf16[2,2,128,1024]{3,2,1,0:T(8,128)(2,1)}, bf16[2,2,128,1024]{3,2,1,0:T(8,128)(2,1)}, u32[]{:S(2)}, u32[]{:S(2)}) collective-permute-start(bf16[2,2,128,1024]{3,2,1,0:T(8,128)(2,1)} %collective-permute-done.40), channel_id=1, source_target_pairs={{0,4},{1,5},{2,6},{3,7},{4,0},{5,1},{6,2},{7,3},{8,12},{9,13},{10,... | collective-permute-start | bytes 3145736 | tf_op jit(solution)/shard_map/ppermute | solution.py:43
  284.0 35.3 %collective-permute-start.45 = (bf16[2,2,128,1024]{3,2,1,0:T(8,128)(2,1)}, bf16[2,2,128,1024]{3,2,1,0:T(8,128)(2,1)S(1)}, u32[]{:S(2)}, u32[]{:S(2)}) collective-permute-start(bf16[2,2,128,1024]{3,2,1,0:T(8,128)(2,1)} %collective-permute-done.44), channel_id=1, source_target_pairs={{0,4},{1,5},{2,6},{3,7},{4,0},{5,1},{6,2},{7,3},{8,12},{9,13},{10,... | collective-permute-start | bytes 3145736 | tf_op jit(solution)/shard_map/ppermute | solution.py:43
  284.1 24.3 %collective-permute-start.34 = (bf16[2,2,32,4096]{3,2,1,0:T(8,128)(2,1)}, bf16[2,2,32,4096]{3,2,1,0:T(8,128)(2,1)S(1)}, u32[]{:S(2)}, u32[]{:S(2)}) collective-permute-start(bf16[2,2,32,4096]{3,2,1,0:T(8,128)(2,1)} %collective-permute-done.33), channel_id=1, source_target_pairs={{0,4},{1,5},{2,6},{3,7},{4,0},{5,1},{6,2},{7,3},{8,12},{9,13},{10,... | collective-permute-start | bytes 3145736 | tf_op jit(solution)/shard_map/ppermute | solution.py:43
  446.3 31.3 %collective-permute-start.46 = (bf16[512,1024]{1,0:T(8,128)(2,1)}, bf16[512,1024]{1,0:T(8,128)(2,1)}, u32[]{:S(2)}, u32[]{:S(2)}) collective-permute-start(bf16[512,1024]{1,0:T(8,128)(2,1)} %slice.671), channel_id=1, source_target_pairs={{1,0},{2,1},{3,2},{4,3},{5,4},{6,5},{7,6},{8,7},{9,8},{10,9},{11,1... | collective-permute-start | bytes 3145736 | tf_op jit(solution)/shard_map/ppermute | solution.py:49
  464.3 71.2 %collective-permute-start.54 = (bf16[2,2,4,32,3072]{4,3,2,1,0:T(8,128)(2,1)}, bf16[2,2,4,32,3072]{4,3,2,1,0:T(8,128)(2,1)}, u32[]{:S(2)}, u32[]{:S(2)}) collective-permute-start(bf16[2,2,4,32,3072]{4,3,2,1,0:T(8,128)(2,1)} %dynamic-slice_bitcast_fusion.2), channel_id=1, source_target_pairs={{0,4},{1,5},{2,6},{3,7},{4,0},{5,1},{6,2},{7,3},{8,12},{9,13},{10,... | collective-permute-start | bytes 9437192 | tf_op jit(solution)/shard_map/ppermute | solution.py:43
  469.0 100.2 %collective-permute-start.70 = (bf16[2,2,4,32,4096]{4,3,2,1,0:T(8,128)(2,1)}, bf16[2,2,4,32,4096]{4,3,2,1,0:T(8,128)(2,1)}, u32[]{:S(2)}, u32[]{:S(2)}) collective-permute-start(bf16[2,2,4,32,4096]{4,3,2,1,0:T(8,128)(2,1)} %dynamic-slice_bitcast_fusion.1), channel_id=1, source_target_pairs={{0,4},{1,5},{2,6},{3,7},{4,0},{5,1},{6,2},{7,3},{8,12},{9,13},{10,... | collective-permute-start | bytes 12582920 | tf_op jit(solution)/shard_map/ppermute | solution.py:43
  474.3 102.3 %collective-permute-start.78 = (bf16[2,2,4,128,1024]{4,3,2,1,0:T(8,128)(2,1)}, bf16[2,2,4,128,1024]{4,3,2,1,0:T(8,128)(2,1)}, u32[]{:S(2)}, u32[]{:S(2)}) collective-permute-start(bf16[2,2,4,128,1024]{4,3,2,1,0:T(8,128)(2,1)} %dynamic-slice_bitcast_fusion), channel_id=1, source_target_pairs={{0,4},{1,5},{2,6},{3,7},{4,0},{5,1},{6,2},{7,3},{8,12},{9,13},{10,... | collective-permute-start | bytes 12582920 | tf_op jit(solution)/shard_map/ppermute | solution.py:43
  479.9 27.7 %collective-permute-start.47 = (bf16[512,1024]{1,0:T(8,128)(2,1)S(1)}, bf16[512,1024]{1,0:T(8,128)(2,1)S(1)}, u32[]{:S(2)}, u32[]{:S(2)}) collective-permute-start(bf16[512,1024]{1,0:T(8,128)(2,1)S(1)} %fusion.18), channel_id=1, source_target_pairs={{1,0},{2,1},{3,2},{4,3},{5,4},{6,5},{7,6},{8,7},{9,8},{10,9},{11,1... | collective-permute-start | bytes 3145736 | tf_op jit(solution)/shard_map/ppermute | solution.py:49
  539.9 15.8 %collective-permute-start.55 = (bf16[2,2,32,3072]{3,2,1,0:T(8,128)(2,1)S(1)}, bf16[2,2,32,3072]{3,2,1,0:T(8,128)(2,1)S(1)}, u32[]{:S(2)}, u32[]{:S(2)}) collective-permute-start(bf16[2,2,32,3072]{3,2,1,0:T(8,128)(2,1)S(1)} %dynamic-slice_bitcast_fusion.9), channel_id=1, source_target_pairs={{0,8},{1,9},{2,10},{3,11},{4,12},{5,13},{6,14},{7,15},{8,0},{9,1},... | collective-permute-start | bytes 2359304 | tf_op jit(solution)/shard_map/ppermute | solution.py:43
  547.2 20.0 %collective-permute-start.57 = (bf16[2,2,32,3072]{3,2,1,0:T(8,128)(2,1)S(1)}, bf16[2,2,32,3072]{3,2,1,0:T(8,128)(2,1)S(1)}, u32[]{:S(2)}, u32[]{:S(2)}) collective-permute-start(bf16[2,2,32,3072]{3,2,1,0:T(8,128)(2,1)S(1)} %dynamic-slice_bitcast_fusion.8), channel_id=1, source_target_pairs={{0,16},{1,17},{2,18},{3,19},{4,20},{5,21},{6,22},{7,23},{8,24},{9,... | collective-permute-start | bytes 2359304 | tf_op jit(solution)/shard_map/ppermute | solution.py:43
  555.9 25.8 %collective-permute-start.56 = (bf16[2,32,3072]{2,1,0:T(8,128)(2,1)S(1)}, bf16[2,32,3072]{2,1,0:T(8,128)(2,1)S(1)}, u32[]{:S(2)}, u32[]{:S(2)}) collective-permute-start(bf16[2,32,3072]{2,1,0:T(8,128)(2,1)S(1)} %dynamic-slice_bitcast_fusion.15), channel_id=1, source_target_pairs={{0,16},{1,17},{2,18},{3,19},{4,20},{5,21},{6,22},{7,23},{8,24},{9,... | collective-permute-start | bytes 1179656 | tf_op jit(solution)/shard_map/ppermute | solution.py:43
  573.7 29.2 %collective-permute-start.71 = (bf16[2,2,32,4096]{3,2,1,0:T(8,128)(2,1)S(1)}, bf16[2,2,32,4096]{3,2,1,0:T(8,128)(2,1)}, u32[]{:S(2)}, u32[]{:S(2)}) collective-permute-start(bf16[2,2,32,4096]{3,2,1,0:T(8,128)(2,1)S(1)} %dynamic-slice_bitcast_fusion.6), channel_id=1, source_target_pairs={{0,8},{1,9},{2,10},{3,11},{4,12},{5,13},{6,14},{7,15},{8,0},{9,1},... | collective-permute-start | bytes 3145736 | tf_op jit(solution)/shard_map/ppermute | solution.py:43
  574.8 31.5 %collective-permute-start.73 = (bf16[2,2,32,4096]{3,2,1,0:T(8,128)(2,1)S(1)}, bf16[2,2,32,4096]{3,2,1,0:T(8,128)(2,1)S(1)}, u32[]{:S(2)}, u32[]{:S(2)}) collective-permute-start(bf16[2,2,32,4096]{3,2,1,0:T(8,128)(2,1)S(1)} %dynamic-slice_bitcast_fusion.5), channel_id=1, source_target_pairs={{0,16},{1,17},{2,18},{3,19},{4,20},{5,21},{6,22},{7,23},{8,24},{9,... | collective-permute-start | bytes 3145736 | tf_op jit(solution)/shard_map/ppermute | solution.py:43
  583.1 42.2 %collective-permute-start.79 = (bf16[2,2,128,1024]{3,2,1,0:T(8,128)(2,1)S(1)}, bf16[2,2,128,1024]{3,2,1,0:T(8,128)(2,1)S(1)}, u32[]{:S(2)}, u32[]{:S(2)}) collective-permute-start(bf16[2,2,128,1024]{3,2,1,0:T(8,128)(2,1)S(1)} %dynamic-slice_bitcast_fusion.4), channel_id=1, source_target_pairs={{0,8},{1,9},{2,10},{3,11},{4,12},{5,13},{6,14},{7,15},{8,0},{9,1},... | collective-permute-start | bytes 3145736 | tf_op jit(solution)/shard_map/ppermute | solution.py:43
  584.3 43.3 %collective-permute-start.81 = (bf16[2,2,128,1024]{3,2,1,0:T(8,128)(2,1)S(1)}, bf16[2,2,128,1024]{3,2,1,0:T(8,128)(2,1)S(1)}, u32[]{:S(2)}, u32[]{:S(2)}) collective-permute-start(bf16[2,2,128,1024]{3,2,1,0:T(8,128)(2,1)S(1)} %dynamic-slice_bitcast_fusion.3), channel_id=1, source_target_pairs={{0,16},{1,17},{2,18},{3,19},{4,20},{5,21},{6,22},{7,23},{8,24},{9,... | collective-permute-start | bytes 3145736 | tf_op jit(solution)/shard_map/ppermute | solution.py:43
  590.6 54.5 %collective-permute-start.60 = (bf16[32,3072]{1,0:T(8,128)(2,1)S(1)}, bf16[32,3072]{1,0:T(8,128)(2,1)S(1)}, u32[]{:S(2)}, u32[]{:S(2)}) collective-permute-start(bf16[32,3072]{1,0:T(8,128)(2,1)S(1)} %fusion.91), channel_id=1, source_target_pairs={{0,1},{1,2},{2,3},{3,0},{4,5},{5,6},{6,7},{7,4},{8,9},{9,10},{10,1... | collective-permute-start | bytes 589832 | tf_op jit(solution)/shard_map/ppermute | solution.py:43
  604.5 28.7 %collective-permute-start.72 = (bf16[2,32,4096]{2,1,0:T(8,128)(2,1)S(1)}, bf16[2,32,4096]{2,1,0:T(8,128)(2,1)S(1)}, u32[]{:S(2)}, u32[]{:S(2)}) collective-permute-start(bf16[2,32,4096]{2,1,0:T(8,128)(2,1)S(1)} %dynamic-slice_bitcast_fusion.13), channel_id=1, source_target_pairs={{0,16},{1,17},{2,18},{3,19},{4,20},{5,21},{6,22},{7,23},{8,24},{9,... | collective-permute-start | bytes 1572872 | tf_op jit(solution)/shard_map/ppermute | solution.py:43
  606.6 26.7 %collective-permute-start.74 = (bf16[2,32,4096]{2,1,0:T(8,128)(2,1)S(1)}, bf16[2,32,4096]{2,1,0:T(8,128)(2,1)S(1)}, u32[]{:S(2)}, u32[]{:S(2)}) collective-permute-start(bf16[2,32,4096]{2,1,0:T(8,128)(2,1)S(1)} %dynamic-slice_bitcast_fusion.12), channel_id=1, source_target_pairs={{0,8},{1,9},{2,10},{3,11},{4,12},{5,13},{6,14},{7,15},{8,0},{9,1},... | collective-permute-start | bytes 1572872 | tf_op jit(solution)/shard_map/ppermute | solution.py:43
  645.2 15.1 %collective-permute-start.61 = (bf16[32,3072]{1,0:T(8,128)(2,1)S(1)}, bf16[32,3072]{1,0:T(8,128)(2,1)S(1)}, u32[]{:S(2)}, u32[]{:S(2)}) collective-permute-start(bf16[32,3072]{1,0:T(8,128)(2,1)S(1)} %fusion.90), channel_id=1, source_target_pairs={{0,1},{1,2},{2,3},{3,0},{4,5},{5,6},{6,7},{7,4},{8,9},{9,10},{10,1... | collective-permute-start | bytes 589832 | tf_op jit(solution)/shard_map/ppermute | solution.py:43
  651.3 14.6 %collective-permute-start.84 = (bf16[128,1024]{1,0:T(8,128)(2,1)}, bf16[128,1024]{1,0:T(8,128)(2,1)}, u32[]{:S(2)}, u32[]{:S(2)}) collective-permute-start(bf16[128,1024]{1,0:T(8,128)(2,1)} %fusion.72), channel_id=1, source_target_pairs={{0,1},{1,2},{2,3},{3,0},{4,5},{5,6},{6,7},{7,4},{8,9},{9,10},{10,1... | collective-permute-start | bytes 786440 | tf_op jit(solution)/shard_map/ppermute | solution.py:43
  (102 other events, 1405.3 us)

commit v2 on v1

v2 whole, which is shorter than its diff:
```python
import functools

import functools

import jax
import jax.numpy as jnp
import numpy as np
from jax import lax
from jax.experimental import pallas as pl
from jax.experimental.pallas import tpu as pltpu
from jax.sharding import PartitionSpec as P

HEADS = 16
HEAD_DIM = 64
WINDOW = 1024
NDOCS = 32

ALL = ("y", "x", "core", "z")
norm_eps = 1e-05
bf16 = jnp.bfloat16
f32 = jnp.float32

MASKED = -1e30
TILE = 256
LANES = 128
SLOPE_LANE = NDOCS + 1
ROW_LANE = SLOPE_LANE + 6
SCALE = HEAD_DIM**-0.5
VMEM_LIMIT = 50 * 2**20
VMEM_ALL = 52 * 2**20
SHORT = pl.CostEstimate(flops=1, bytes_accessed=1, transcendentals=0)


def normalize(values):
    centred = values - jnp.mean(values, axis=-1, keepdims=True)
    inverse = lax.rsqrt(jnp.mean(centred * centred, axis=-1, keepdims=True) + norm_eps)
    return centred * inverse, inverse


def norm_back(change, normal, inverse, gain):
    scaled = change * gain
    mean_one = jnp.mean(scaled, axis=-1, keepdims=True)
    mean_two = jnp.mean(scaled * normal, axis=-1, keepdims=True)
    return inverse * (scaled - mean_one - normal * mean_two)


def dot_nn(left, right):
    return lax.dot_general(left, right, (((1,), (0,)), ((), ())), preferred_element_type=f32)


def dot_nt(left, right):
    return lax.dot_general(left, right, (((1,), (1,)), ((), ())), preferred_element_type=f32)


def dot_tn(left, right):
    return lax.dot_general(left, right, (((0,), (0,)), ((), ())), preferred_element_type=f32)


class Grid:
    def __init__(self):
        self.size = tuple(lax.axis_size(name) for name in ALL)
        self.here = tuple(lax.axis_index(name) for name in ALL)
        self.count = int(np.prod(self.size))
        self.linear = lax.axis_index(ALL)

    def shift(self, block, axis, distance=1):
        places = np.arange(self.count).reshape(self.size)
        ahead = np.roll(places, -distance, axis)
        return lax.ppermute(block, ALL, list(zip(places.ravel().tolist(), ahead.ravel().tolist())))

    def to_later(self, block):
        return lax.ppermute(block, ALL, [(i, i + 1) for i in range(self.count - 1)])

    def to_earlier(self, block):
        return lax.ppermute(block, ALL, [(i + 1, i) for i in range(self.count - 1)])


Y, X, CORE, Z = range(4)


def after(value, *earlier):
    anywhere = pl.BlockSpec(memory_space=pl.ANY)
    return pl.pallas_call(
        lambda *refs: None,
        in_specs=[anywhere] * (1 + len(earlier)),
        out_specs=anywhere,
        out_shape=jax.ShapeDtypeStruct(value.shape, value.dtype),
        input_output_aliases={0: 0},
        compiler_params=pltpu.CompilerParams(vmem_limit_bytes=2**17),
    )(value, *earlier)


def ring_gather(grid, block, axis):
    pieces = [block]
    for _ in range(grid.size[axis] - 1):
        pieces.append(grid.shift(pieces[-1], axis))
    return pieces


def direct_gather(grid, block, axis):
    return [block] + [grid.shift(block, axis, step) for step in range(1, grid.size[axis])]


def plane_gather(grid, line):
    half = len(line) // 2
    got = []
    for part, (one, two) in enumerate(((X, Y), (Y, X))):
        near = jnp.stack(ring_gather(grid, jnp.stack(line[part * half : (part + 1) * half]), one))
        for two_step, far in enumerate(ring_gather(grid, near, two)):
            got.append((part * half, one, two, two_step, far))
    return got


def plane_places(grid, got):
    ny, nx, _, nz = grid.size
    found = []
    for step, one, two, two_step, block in got:
        entries = []
        for one_step in range(block.shape[0]):
            back = {one: one_step, two: two_step}
            chip = (grid.here[Y] - back[Y]) % ny * nx + (grid.here[X] - back[X]) % nx
            entries.append([(chip, (grid.here[Z] - step - k) % nz) for k in range(block.shape[1])])
        found.append(entries)
    return found


def copy_blocks(moves, sems):
    copies = [pltpu.make_async_copy(source, target, sems.at[i]) for i, (source, target) in enumerate(moves)]
    for copy in copies:
        copy.start()
    for copy in copies:
        copy.wait()


def assemble(kernel, places, pieces, shapes, moves):
    anywhere = pl.BlockSpec(memory_space=pl.ANY)
    return pl.pallas_call(
        kernel,
        in_specs=[pl.BlockSpec(memory_space=pltpu.SMEM)] + [anywhere] * len(pieces),
        out_specs=[pl.BlockSpec(memory_space=pltpu.VMEM)] * len(shapes),
        out_shape=[jax.ShapeDtypeStruct(shape, bf16) for shape in shapes],
        scratch_shapes=[pltpu.SemaphoreType.DMA((moves,))],
        compiler_params=pltpu.CompilerParams(vmem_limit_bytes=VMEM_ALL),
        cost_estimate=SHORT,
    )(places, *pieces)


def joined_kernel(places, *refs):
    *pieces, whole, riders, sems = refs
    moves = []
    for piece in pieces:
        for near in range(piece.shape[0]):
            for step in range(piece.shape[1]):
                at = places[len(moves) // 4]
                for kind in range(3):
                    moves.append((piece.at[near, step, kind, :, pl.ds(0, whole.shape[-1])], whole.at[kind, at]))
                moves.append((piece.at[near, step, 0, :, pl.ds(whole.shape[-1], LANES)], riders.at[at]))
    copy_blocks(moves, sems)


def gather_joined(grid, line):
    got = plane_gather(grid, line)
    rows, width = line[0].shape[-2], line[0].shape[-1] - LANES
    pieces, places = [], []
    for (_, _, _, _, block), entries in zip(got, plane_places(grid, got)):
        for which, piece in ((grid.here[CORE], block), (1 - grid.here[CORE], grid.shift(block, CORE))):
            pieces.append(piece)
            places += [(chip * 2 + which) * grid.size[Z] + z for near in entries for chip, z in near]
    whole, riders = assemble(
        joined_kernel,
        jnp.stack(places).astype(jnp.int32),
        pieces,
        [(3, grid.count, rows, width), (grid.count, rows, LANES)],
        4 * len(places),
    )
    return whole.reshape(3, -1, width), riders


def up_kernel(places, lines, up, sems):
    width = lines.shape[-1]
    moves = []
    for entry in range(lines.shape[0]):
        for side in range(2):
            at = places[2 * entry + side]
            for half in range(2):
                moves.append((lines.at[entry, 2 * side + half], up.at[at, :, pl.ds(half * width, width)]))
    copy_blocks(moves, sems)


def whole_up(grid, lines, *earlier):
    count, _, rows, width = lines.shape
    nz, core = grid.size[Z], grid.here[CORE]
    places = [(entry // nz * 2 + which) * nz + entry % nz for entry in range(count) for which in (core, 1 - core)]
    places = after(jnp.stack(places).astype(jnp.int32), *earlier)
    (up,) = assemble(up_kernel, places, [lines], [(grid.count, rows, 2 * width)], 4 * count)
    return up.reshape(-1, 2 * width)


def add(left, right, kind=bf16):
    return (left.astype(f32) + right.astype(f32)).astype(kind)


def ring_reduce(grid, term, axis, kind=bf16):
    count = grid.size[axis]
    total = term(1)
    for step in range(2, count + 1):
        total = add(grid.shift(total, axis), term(step), kind)
    return total


def direct_reduce(grid, terms, axis, kind=f32):
    count, place = grid.size[axis], grid.here[axis]

    def term(step):
        return lax.dynamic_index_in_dim(terms, (place + step) % count, 0, keepdims=False)

    total = term(0).astype(f32)
    for step in range(1, count):
        total = total + grid.shift(term(step), axis, step).astype(f32)
    return total.astype(kind)


def down_kernel(left, right, out, total):
    out[...] = dot_tn(left[...], right[...]).astype(bf16)

    @pl.when(pl.program_id(0) == 0)
    def _():
        total[...] = jnp.sum(right[: right.shape[0] // 2].astype(f32), axis=0, keepdims=True)


def down_terms(hidden, change):
    tokens, units = hidden.shape
    width = change.shape[1]
    return pl.pallas_call(
        down_kernel,
        grid=(units // TILE,),
        in_specs=[
            pl.BlockSpec((tokens, TILE), lambda i: (0, i)),
            pl.BlockSpec((tokens, width), lambda i: (0, 0)),
        ],
        out_specs=[pl.BlockSpec((TILE, width), lambda i: (i, 0)), pl.BlockSpec((1, width), lambda i: (0, 0))],
        out_shape=[jax.ShapeDtypeStruct((units, width), bf16), jax.ShapeDtypeStruct((1, width), f32)],
        compiler_params=pltpu.CompilerParams(vmem_limit_bytes=VMEM_LIMIT),
        cost_estimate=SHORT,
    )(hidden, change)


def up_kernel_terms(own, other, right, *refs):
    refs[-1][...] = dot_tn(jnp.concatenate([own[...], other[...]], axis=0), right[...]).astype(bf16)


def up_terms(own, other, pre_change, earlier=()):
    rows, width = own.shape
    tokens, units = pre_change.shape
    wide = units // 2
    left = pl.BlockSpec((rows, TILE), lambda j, i: (0, i))
    return pl.pallas_call(
        up_kernel_terms,
        grid=(2, width // TILE),
        in_specs=[left, left, pl.BlockSpec((tokens, wide), lambda j, i: (0, j))]
        + [pl.BlockSpec(memory_space=pl.ANY)] * len(earlier),
        out_specs=pl.BlockSpec((TILE, wide), lambda j, i: (i, j)),
        out_shape=jax.ShapeDtypeStruct((width, units), bf16),
        compiler_params=pltpu.CompilerParams(vmem_limit_bytes=VMEM_LIMIT),
        cost_estimate=SHORT,
    )(own, other, pre_change, *earlier)


def add_kernel(split, left, right, *refs):
    if split == 0:
        refs[-1][...] = (left[...].astype(f32) + right[...].astype(f32)).astype(bf16)
    for i in range(split):
        refs[-split + i][...] = (left[i].astype(f32) + right[i].astype(f32)).astype(bf16)


def add_after(left, right, *earlier, split=False):
    held = pl.BlockSpec(memory_space=pltpu.VMEM)
    shape = jax.ShapeDtypeStruct(left.shape, bf16)
    if split:
        shape = [jax.ShapeDtypeStruct(left.shape[1:], bf16)] * left.shape[0]
    return pl.pallas_call(
        functools.partial(add_kernel, left.shape[0] if split else 0),
        in_specs=[held] * 2 + [pl.BlockSpec(memory_space=pl.ANY)] * len(earlier),
        out_specs=[held] * left.shape[0] if split else held,
        out_shape=shape,
        compiler_params=pltpu.CompilerParams(vmem_limit_bytes=VMEM_LIMIT),
        cost_estimate=SHORT,
    )(left, right, *earlier)


def product_kernel(left, right, *refs):
    refs[-1][...] = dot_nt(left[...], right[...]).astype(refs[-1].dtype)


def product_nt(left, right, kind, row_block=0, rows=None, earlier=()):
    rows = left.shape[0] if rows is None else rows
    depth, wide = left.shape[1], right.shape[0]
    return pl.pallas_call(
        product_kernel,
        grid=(wide // TILE,),
        in_specs=[
            pl.BlockSpec((rows, depth), lambda i: (row_block, 0)),
            pl.BlockSpec((TILE, depth), lambda i: (i, 0)),
        ]
        + [pl.BlockSpec(memory_space=pl.ANY)] * len(earlier),
        out_specs=pl.BlockSpec((rows, TILE), lambda i: (0, i)),
        out_shape=jax.ShapeDtypeStruct((rows, wide), kind),
        compiler_params=pltpu.CompilerParams(vmem_limit_bytes=VMEM_LIMIT),
        cost_estimate=SHORT,
    )(left, right, *earlier)


def product_nn_kernel(left, right, *refs):
    refs[-1][...] = dot_nn(left[...], right[...]).astype(refs[-1].dtype)


def product_nn(left, right, kind, row_block, rows, earlier=()):
    depth, wide = right.shape
    return pl.pallas_call(
        product_nn_kernel,
        grid=(wide // TILE,),
        in_specs=[
            pl.BlockSpec((rows, depth), lambda i: (row_block, 0)),
            pl.BlockSpec((depth, TILE), lambda i: (0, i)),
        ]
        + [pl.BlockSpec(memory_space=pl.ANY)] * len(earlier),
        out_specs=pl.BlockSpec((rows, TILE), lambda i: (0, i)),
        out_shape=jax.ShapeDtypeStruct((rows, wide), kind),
        compiler_params=pltpu.CompilerParams(vmem_limit_bytes=VMEM_LIMIT),
        cost_estimate=SHORT,
    )(left, right, *earlier)


def chunk_kernel(count, with_arrived, *refs):
    lefts, rights, (tokens, stats) = refs[:count], refs[count : 2 * count], refs[2 * count : 2 * count + 2]
    moved, gain_sum, shift_sum = refs[-3:]
    change = dot_nt(lefts[0][...], rights[0][...])
    for left, right in zip(lefts[1:], rights[1:]):
        change += dot_nt(left[...], right[...])
    normal = (tokens[...].astype(f32) - stats[:, :1]) * stats[:, 1:2]
    gain_sum[...] = jnp.sum(change * normal, axis=0, keepdims=True)
    shift_sum[...] = jnp.sum(change, axis=0, keepdims=True)
    if with_arrived:
        change += refs[2 * count + 2][...].astype(f32)
    moved[...] = change.astype(moved.dtype)


def chunk_back(pairs, chunk, kind, arrived=None, earlier=()):
    rows, width = chunk[0].shape
    tile = pl.BlockSpec((rows, TILE), lambda i: (0, i))
    sums = pl.BlockSpec((1, TILE), lambda i: (0, i))
    return pl.pallas_call(
        functools.partial(chunk_kernel, len(pairs), arrived is not None),
        grid=(width // TILE,),
        in_specs=[pl.BlockSpec((rows, left.shape[1]), lambda i, at=at: (at, 0)) for left, at, _ in pairs]
        + [pl.BlockSpec((TILE, right.shape[1]), lambda i: (i, 0)) for *_, right in pairs]
        + [tile, pl.BlockSpec((rows, LANES), lambda i: (0, 0))]
        + [tile] * (arrived is not None)
        + [pl.BlockSpec(memory_space=pl.ANY)] * len(earlier),
        out_specs=[tile, sums, sums],
        out_shape=[jax.ShapeDtypeStruct((rows, width), kind)] + [jax.ShapeDtypeStruct((1, width), f32)] * 2,
        compiler_params=pltpu.CompilerParams(vmem_limit_bytes=VMEM_LIMIT),
        cost_estimate=SHORT,
    )(
        *(left for left, *_ in pairs),
        *(right for *_, right in pairs),
        *chunk,
        *(() if arrived is None else (arrived,)),
        *earlier,
    )


def middle_kernel(pre_change, up, arrived, middle, gain, out_change, dense, *refs):
    middle_change, branch_change, context_change, gain_sum, shift_sum, branch_sum = refs[-6:]
    change = dot_nt(pre_change[...], up[...]) + arrived[...].astype(f32)
    normal, inverse = normalize(middle[...])
    moved = out_change[...].astype(f32) + norm_back(change, normal, inverse, gain[...])
    low = moved.astype(bf16)
    middle_change[...] = moved
    branch_change[...] = low
    context_change[...] = dot_nt(low, dense[...]).astype(bf16)
    first = pl.program_id(0) == 0
    for total, part in ((gain_sum, change * normal), (shift_sum, change), (branch_sum, low.astype(f32))):
        total[...] = jnp.where(first, 0.0, total[...]) + jnp.sum(part, axis=0, keepdims=True)


def middle_back(pre_change, up, arrived, middle, gain, out_change, dense, earlier=()):
    rows, width = middle.shape
    tile = pl.BlockSpec((TILE, width), lambda i: (i, 0))
    sums = pl.BlockSpec((1, width), lambda i: (0, 0))

    def whole(array):
        return pl.BlockSpec(array.shape, lambda i: (0, 0))

    return pl.pallas_call(
        middle_kernel,
        grid=(rows // TILE,),
        in_specs=[
            pl.BlockSpec((TILE, pre_change.shape[1]), lambda i: (i, 0)), whole(up), tile, tile, whole(gain), tile, whole(dense)
        ]
        + [pl.BlockSpec(memory_space=pl.ANY)] * len(earlier),
        out_specs=[tile, tile, tile, sums, sums, sums],
        out_shape=[
            jax.ShapeDtypeStruct((rows, width), f32),
            jax.ShapeDtypeStruct((rows, width), bf16),
            jax.ShapeDtypeStruct((rows, width), bf16),
        ]
        + [jax.ShapeDtypeStruct((1, width), f32)] * 3,
        compiler_params=pltpu.CompilerParams(vmem_limit_bytes=VMEM_LIMIT),
        cost_estimate=SHORT,
    )(pre_change, up, arrived, middle, gain, out_change, dense, *earlier)


def joined_kernel_terms(blocks, core, tokens_ext, context, query, key, value, branch, *refs):
    given_ahead, given_behind, kept_ahead, kept_behind = refs[-4:]
    left = tokens_ext[...]
    own = left[left.shape[0] - query.shape[0] :]
    rows = kept_ahead.shape[2]
    swapped = core[0] == 1
    for kind, (one, two) in enumerate(((own, query), (left, key), (left, value), (context[...], branch))):
        product = dot_tn(one, two[...])
        for part, (given, kept) in enumerate(((given_ahead, kept_ahead), (given_behind, kept_behind))):
            low, high = (product[(2 * side + part) * rows : (2 * side + part + 1) * rows] for side in range(2))
            given[0, kind] = jnp.where(swapped, low, high).astype(bf16)
            kept[0, kind] = jnp.where(swapped, high, low).astype(bf16)


def joined_terms(normed_ext, context, rights, chips_at, core, earlier=()):
    ext_rows, width = normed_ext.shape
    tok_rows = context.shape[0]
    count = len(chips_at)
    rows = width // count
    half = (1, 4, rows // 4, width)
    stacked = pl.BlockSpec(half, lambda i, at, core: (i, 0, 0, 0))

    def whole(array):
        return pl.BlockSpec(array.shape, lambda i, at, core: (0, 0))

    return pl.pallas_call(
        joined_kernel_terms,
        grid_spec=pltpu.PrefetchScalarGridSpec(
            num_scalar_prefetch=2,
            grid=(count,),
            in_specs=[
                pl.BlockSpec((ext_rows, rows), lambda i, at, core: (0, at[i])),
                pl.BlockSpec((tok_rows, rows), lambda i, at, core: (0, at[i])),
                *(whole(right) for right in rights),
                *[pl.BlockSpec(memory_space=pl.ANY)] * len(earlier),
            ],
            out_specs=[stacked] * 4,
        ),
        out_shape=[jax.ShapeDtypeStruct((count, *half[1:]), bf16)] * 4,
        compiler_params=pltpu.CompilerParams(vmem_limit_bytes=VMEM_LIMIT),
        cost_estimate=SHORT,
    )(
        jnp.stack(chips_at).astype(jnp.int32), jnp.reshape(core, (1,)).astype(jnp.int32), normed_ext, context, *rights, *earlier
    )


def split_kernel(nx, ahead, arrived_ahead, behind, arrived_behind, *refs):
    ny = ahead.shape[0]
    outs = refs[-nx - ny :]
    for back_y in range(ny):
        for back_x in range(nx):
            outs[back_x][back_y] = (ahead[back_y, back_x].astype(f32) + arrived_ahead[back_y, back_x].astype(f32)).astype(bf16)
            outs[nx + back_y][back_x] = (
                behind[back_y, back_x].astype(f32) + arrived_behind[back_y, back_x].astype(f32)
            ).astype(bf16)


def split_terms(ahead, arrived_ahead, behind, arrived_behind, ny, nx, earlier=()):
    arrays = [array.reshape(ny, nx, *array.shape[1:]) for array in (ahead, arrived_ahead, behind, arrived_behind)]
    shape = arrays[0].shape[2:]
    kinds = shape[0]
    rest = shape[1:]
    return pl.pallas_call(
        functools.partial(split_kernel, nx),
        grid=(kinds,),
        in_specs=[pl.BlockSpec((ny, nx, 1, *rest), lambda i: (0, 0, i, 0, 0))] * 4
        + [pl.BlockSpec(memory_space=pl.ANY)] * len(earlier),
        out_specs=[pl.BlockSpec((ny, 1, *rest), lambda i: (0, i, 0, 0))] * nx
        + [pl.BlockSpec((nx, 1, *rest), lambda i: (0, i, 0, 0))] * ny,
        out_shape=[jax.ShapeDtypeStruct((ny, *shape), bf16)] * nx + [jax.ShapeDtypeStruct((nx, *shape), bf16)] * ny,
        compiler_params=pltpu.CompilerParams(vmem_limit_bytes=VMEM_LIMIT),
        cost_estimate=SHORT,
    )(*arrays, *earlier)


def reduce_scatter_small(grid, terms):
    terms = terms.reshape(*grid.size, terms.shape[1])
    for axis, dim in ((CORE, 2), (X, 1), (Y, 0)):
        def term(step, terms=terms, axis=axis, dim=dim):
            return lax.dynamic_index_in_dim(terms, (grid.here[axis] - step) % grid.size[axis], dim, keepdims=False)

        terms = ring_reduce(grid, term, axis, f32)
    return direct_reduce(grid, terms, Z, f32)


def thirds(values):
    high = values.astype(bf16)
    rest = values - high.astype(f32)
    middle = rest.astype(bf16)
    return high, middle, (rest - middle.astype(f32)).astype(bf16)


def slope_lanes():
    lanes = np.zeros((HEADS // 2, 8, LANES), np.float32)
    for h in range(HEADS):
        rest = np.float32(2.0 ** (-8.0 * (h + 1) / HEADS))
        for part in range(3):
            piece = np.float32(rest.astype(bf16))
            rest = np.float32(rest - piece)
            lanes[h // 2, h % 2, SLOPE_LANE + part] = piece
            lanes[h // 2, h % 2, SLOPE_LANE + 3 + part] = piece
    return lanes


def side_lanes(seg_ext, tok_rows):
    lane = jnp.arange(LANES, dtype=jnp.int32)
    doc = lane[None, :] <= NDOCS
    seg_query = seg_ext[seg_ext.shape[0] - tok_rows :]
    query_side = jnp.where(doc & (lane[None, :] == seg_query[:, None]), 1.0, 0.0).astype(bf16)
    key_pos = jnp.arange(seg_ext.shape[0], dtype=jnp.int32)[:, None]
    key_side = jnp.where(doc & (lane[None, :] != seg_ext[:, None]), MASKED, 0.0)
    key_side = jnp.where((lane >= SLOPE_LANE) & (lane < SLOPE_LANE + 3), (key_pos // TILE * TILE).astype(f32), key_side)
    key_side = jnp.where((lane >= SLOPE_LANE + 3) & (lane < ROW_LANE), (key_pos % TILE).astype(f32), key_side)
    key_side = jnp.where((lane >= ROW_LANE) & (lane < ROW_LANE + 3), 1.0, key_side)
    return query_side, key_side.astype(bf16)


def key_tiles(tile):
    wide = WINDOW // TILE
    edges = [(tile + step) * TILE for step in (0, 1, wide, wide + 1)]
    return [slice(edges[i], edges[i + 1]) for i in range(3)]


def attend_kernel(query, key, value, query_side, key_side, slope, context, log_total):
    pair = pl.program_id(0)
    lane = lax.broadcasted_iota(jnp.int32, (TILE, LANES), 1)
    causal = lax.broadcasted_iota(jnp.int32, (TILE, TILE), 0) >= lax.broadcasted_iota(jnp.int32, (TILE, TILE), 1)
    keys = jnp.concatenate([key[...], key_side[...]], axis=1)
    for tile in range(query.shape[0] // TILE):
        rows = slice(tile * TILE, (tile + 1) * TILE)
        first, middle, last = key_tiles(tile)
        scaled = query[rows, :] * jnp.asarray(SCALE, bf16)
        outs, logs = [], []
        for half in range(2):
            mine = (lane >= HEAD_DIM) == (half == 1)
            side = query_side[rows, :] + slope[0, half : half + 1, :].astype(bf16)
            queries = jnp.concatenate([jnp.where(mine, scaled, jnp.zeros_like(scaled)), side], axis=1)
            inner = dot_nt(queries, keys[middle])
            outer = jnp.where(causal, dot_nt(queries, keys[last]), dot_nt(queries, keys[first]))
            top = jnp.maximum(jnp.max(inner, axis=1, keepdims=True), jnp.max(outer, axis=1, keepdims=True))
            inner = jnp.exp(inner - top)
            outer = jnp.exp(outer - top)
            total = jnp.sum(inner, axis=1, keepdims=True) + jnp.sum(outer, axis=1, keepdims=True)
            summed = dot_nn(inner.astype(bf16), value[middle, :])
            summed += dot_nn(jnp.where(causal, outer, 0.0).astype(bf16), value[last, :])
            summed += dot_nn(jnp.where(causal, 0.0, outer).astype(bf16), value[first, :])
            outs.append(summed / total)
            logs.append(top + jnp.log(total))
        context[rows, :] = jnp.where(lane < HEAD_DIM, outs[0], outs[1]).astype(bf16)
        before = jnp.where(pair == 0, jnp.zeros((TILE, LANES), f32), log_total[rows, :])
        log_total[rows, :] = jnp.where(lane == 2 * pair, logs[0], jnp.where(lane == 2 * pair + 1, logs[1], before))


def attend(queries, keys, values, query_side, key_side, slopes):
    tok_rows, width = queries.shape
    key_rows = keys.shape[0]
    steps = HEADS // 2
    return pl.pallas_call(
        attend_kernel,
        grid=(steps,),
        in_specs=[
            pl.BlockSpec((tok_rows, LANES), lambda p: (0, p)),
            pl.BlockSpec((key_rows, LANES), lambda p: (0, p)),
            pl.BlockSpec((key_rows, LANES), lambda p: (0, p)),
            pl.BlockSpec((tok_rows, LANES), lambda p: (0, 0)),
            pl.BlockSpec((key_rows, LANES), lambda p: (0, 0)),
            pl.BlockSpec((1, 8, LANES), lambda p: (p, 0, 0)),
        ],
        out_specs=[
            pl.BlockSpec((tok_rows, LANES), lambda p: (0, p)),
            pl.BlockSpec((tok_rows, LANES), lambda p: (0, 0)),
        ],
        out_shape=[
            jax.ShapeDtypeStruct((tok_rows, width), bf16),
            jax.ShapeDtypeStruct((tok_rows, LANES), f32),
        ],
        compiler_params=pltpu.CompilerParams(vmem_limit_bytes=VMEM_ALL),
        cost_estimate=SHORT,
    )(queries, keys, values, query_side, key_side, slopes)


def attend_back_kernel(
    query, key, value, change, context, log_total, query_side, key_side, slope, *refs, first_pair,
):
    query_change, key_change, value_change, key_sum, value_sum = refs[-5:]
    pair = first_pair + pl.program_id(0)
    lane = lax.broadcasted_iota(jnp.int32, (TILE, LANES), 1)
    causal = lax.broadcasted_iota(jnp.int32, (TILE, TILE), 0) <= lax.broadcasted_iota(jnp.int32, (TILE, TILE), 1)
    keys = jnp.concatenate([key[...], key_side[...]], axis=1)
    values = jnp.concatenate([value[...], key_side[...]], axis=1)
    keys_across = key[...].T
    key_sum[...] = jnp.zeros_like(key_sum)
    value_sum[...] = jnp.zeros_like(value_sum)

    def row_lanes(column):
        high, middle, low = thirds(column)
        lanes = jnp.where(lane == ROW_LANE + 2, low, jnp.zeros((TILE, LANES), bf16))
        return jnp.where(lane == ROW_LANE, high, jnp.where(lane == ROW_LANE + 1, middle, lanes))

    for tile in range(query.shape[0] // TILE):
        rows = slice(tile * TILE, (tile + 1) * TILE)
        first, middle, last = key_tiles(tile)
        scaled = query[rows, :] * jnp.asarray(SCALE, bf16)
        changed = change[rows, :]
        product = changed.astype(f32) * context[rows, :].astype(f32)
        logs = log_total[rows, :]
        parts = []
        for half in range(2):
            mine = (lane >= HEAD_DIM) == (half == 1)
            asked = jnp.where(mine, scaled, jnp.zeros_like(scaled))
            moved = jnp.where(mine, changed, jnp.zeros_like(changed))
            log_row = jnp.sum(jnp.where(lane == 2 * pair + half, logs, 0.0), axis=1, keepdims=True)
            inner_row = jnp.sum(jnp.where(mine, product, 0.0), axis=1, keepdims=True)
            side = query_side[rows, :] + slope[0, half : half + 1, :].astype(bf16) + row_lanes(-log_row)
            queries = jnp.concatenate([asked, side], axis=1)
            changes = jnp.concatenate([moved, row_lanes(-inner_row)], axis=1)
            prob = jnp.exp(dot_nt(keys[middle], queries))
            prob_edge = jnp.exp(jnp.where(causal, dot_nt(keys[last], queries), dot_nt(keys[first], queries)))
            score = (prob * dot_nt(values[middle], changes)).astype(bf16)
            score_edge = prob_edge * jnp.where(causal, dot_nt(values[last], changes), dot_nt(values[first], changes))
            score_last = jnp.where(causal, score_edge, 0.0).astype(bf16)
            score_first = jnp.where(causal, 0.0, score_edge).astype(bf16)
            value_sum[middle, :] += dot_nn(prob.astype(bf16), moved)
            value_sum[last, :] += dot_nn(jnp.where(causal, prob_edge, 0.0).astype(bf16), moved)
            value_sum[first, :] += dot_nn(jnp.where(causal, 0.0, prob_edge).astype(bf16), moved)
            key_sum[middle, :] += dot_nn(score, asked)
            key_sum[last, :] += dot_nn(score_last, asked)
            key_sum[first, :] += dot_nn(score_first, asked)
            parts.append(
                dot_nn(keys_across[:, middle], score)
                + dot_nn(keys_across[:, last], score_last)
                + dot_nn(keys_across[:, first], score_first)
            )
        entry = lax.broadcasted_iota(jnp.int32, (LANES, TILE), 0)
        query_change[rows, :] = (jnp.where(entry < HEAD_DIM, parts[0], parts[1]).T * SCALE).astype(bf16)
    key_change[...] = key_sum[...].astype(bf16)
    value_change[...] = value_sum[...].astype(bf16)


def attend_back(queries, keys, values, change, context, log_total, query_side, key_side, slopes, first_pair, count, others=()):
    tok_rows, width = queries.shape
    key_rows = keys.shape[0]
    steps = HEADS // 2
    by_query = pl.BlockSpec((tok_rows, LANES), lambda p: (0, first_pair + p))
    by_key = pl.BlockSpec((key_rows, LANES), lambda p: (0, first_pair + p))
    return pl.pallas_call(
        functools.partial(attend_back_kernel, first_pair=first_pair),
        grid=(count,),
        in_specs=[
            by_query,
            by_key,
            by_key,
            by_query,
            by_query,
            pl.BlockSpec((tok_rows, LANES), lambda p: (0, 0)),
            pl.BlockSpec((tok_rows, LANES), lambda p: (0, 0)),
            pl.BlockSpec((key_rows, LANES), lambda p: (0, 0)),
            pl.BlockSpec((1, 8, LANES), lambda p: (first_pair + p, 0, 0)),
        ]
        + [pl.BlockSpec(memory_space=pl.ANY)] * len(others),
        out_specs=[by_query, by_key, by_key],
        out_shape=[
            jax.ShapeDtypeStruct((tok_rows, width), bf16),
            jax.ShapeDtypeStruct((key_rows, width), bf16),
            jax.ShapeDtypeStruct((key_rows, width), bf16),
        ],
        input_output_aliases={9 + i: i for i in range(len(others))},
        scratch_shapes=[pltpu.VMEM((key_rows, LANES), f32), pltpu.VMEM((key_rows, LANES), f32)],
        compiler_params=pltpu.CompilerParams(vmem_limit_bytes=VMEM_ALL),
        cost_estimate=SHORT,
    )(queries, keys, values, change, context, log_total, query_side, key_side, slopes, *others)


def segment_ids(lengths, valid_count, positions):
    doc_ends = jnp.cumsum(lengths)
    passed = jnp.sum((doc_ends[None, :] <= positions[:, None]).astype(jnp.int32), axis=1)
    inside = jnp.where(positions < valid_count[0], passed, NDOCS)
    return jnp.where(positions < 0, -1, inside)


ROOT = float(np.sqrt(2.0 / np.pi))


def gelu_parts(values):
    square = values * values
    rise = 0.5 * jnp.tanh(values * (square * (ROOT * 0.044715) + ROOT)) + 0.5
    bend = values * (square * (6.0 * ROOT * 0.044715) + 2.0 * ROOT)
    return values * rise, rise + bend * (rise - rise * rise)


def hidden_kernel(chips, core, own, other, up_kept, up_given, bias, hidden, slope, sides):
    rows, width = own.shape
    wide = width // (2 * chips)

    @pl.when(pl.program_id(0) == 0)
    def _():
        first = core[0] == 0
        for chip in range(chips):
            start, to = 2 * chip * wide, slice(chip * wide, (chip + 1) * wide)
            for part, tokens in enumerate((own, other)):
                low, high = tokens[:, start : start + wide], tokens[:, start + wide : start + 2 * wide]
                sides[0, part * rows : (part + 1) * rows, to] = jnp.where(first, low, high)
                sides[1, part * rows : (part + 1) * rows, to] = jnp.where(first, high, low)

    kept = up_kept[...].reshape(width // 2, TILE)
    given = up_given[...].reshape(width // 2, TILE)
    for start in range(0, 2 * rows, TILE):
        product = dot_nn(sides[0, start : start + TILE], kept) + dot_nn(sides[1, start : start + TILE], given)
        value, rise = gelu_parts(product + bias[...])
        hidden[start : start + TILE, :] = value.astype(bf16)
        slope[start : start + TILE, :] = rise.astype(bf16)


def hidden_units(chips, core, own, other, lines, bias):
    rows, depth = own.shape
    count, _, height, width = lines.shape
    units = 2 * width
    steps = width // TILE
    columns = pl.BlockSpec((2 * rows, TILE), lambda i, at: (0, i))
    whole = pl.BlockSpec((rows, depth), lambda i, at: (0, 0))

    def block(side):
        return pl.BlockSpec((count, 1, height, TILE), lambda i, at: (0, 2 * side + i // steps, 0, i % steps))

    return pl.pallas_call(
        functools.partial(hidden_kernel, chips),
        grid_spec=pltpu.PrefetchScalarGridSpec(
            num_scalar_prefetch=1,
            grid=(units // TILE,),
            in_specs=[whole, whole, block(0), block(1), pl.BlockSpec((1, TILE), lambda i, at: (0, i))],
            out_specs=[columns, columns],
            scratch_shapes=[pltpu.VMEM((2, 2 * rows, depth // 2), bf16)],
        ),
        out_shape=[jax.ShapeDtypeStruct((2 * rows, units), bf16)] * 2,
        compiler_params=pltpu.CompilerParams(vmem_limit_bytes=VMEM_LIMIT),
        cost_estimate=SHORT,
    )(jnp.reshape(core, (1,)).astype(jnp.int32), own, other, lines, lines, bias)


def pre_change_kernel(change, down, slope, *refs):
    pre_change, total = refs[-2:]
    moved = (dot_nt(change[...], down[...]) * slope[...].astype(f32)).astype(bf16)
    pre_change[...] = moved
    total[...] = jnp.sum(moved.astype(f32), axis=0, keepdims=True)


def hidden_back(change, down, slope, earlier=()):
    tokens, depth = change.shape
    units = down.shape[0]
    columns = pl.BlockSpec((tokens, TILE), lambda i: (0, i))
    return pl.pallas_call(
        pre_change_kernel,
        grid=(units // TILE,),
        in_specs=[
            pl.BlockSpec((tokens, depth), lambda i: (0, 0)),
            pl.BlockSpec((TILE, depth), lambda i: (i, 0)),
            columns,
        ]
        + [pl.BlockSpec(memory_space=pl.ANY)] * len(earlier),
        out_specs=[columns, pl.BlockSpec((1, TILE), lambda i: (0, i))],
        out_shape=[jax.ShapeDtypeStruct((tokens, units), bf16), jax.ShapeDtypeStruct((1, units), f32)],
        compiler_params=pltpu.CompilerParams(vmem_limit_bytes=VMEM_LIMIT),
        cost_estimate=SHORT,
    )(change, down, slope, *earlier)


def projection_kernel(kinds, others, tokens, gain, shift, *refs):
    mats, shifts = refs[:kinds], refs[kinds : 2 * kinds]
    normed, stats, *outs, held = refs[2 * kinds + others :]

    @pl.when(pl.program_id(0) == 0)
    def _():
        values = tokens[...].astype(f32)
        mean = jnp.mean(values, axis=-1, keepdims=True)
        centred = values - mean
        inverse = lax.rsqrt(jnp.mean(centred * centred, axis=-1, keepdims=True) + norm_eps)
        low = (centred * inverse * gain[...] + shift[...]).astype(bf16)
        normed[...] = low
        held[...] = low
        lane = lax.broadcasted_iota(jnp.int32, stats.shape, 1)
        stats[...] = jnp.where(lane == 0, mean, inverse)

    for mat, add, out in zip(mats, shifts, outs):
        out[...] = (dot_nn(held[...], mat[...]) + add[...]).astype(bf16)


def project(tokens, gain, shift, mats, shifts, chunk, chunks, others=()):
    rows, width = tokens.shape
    kinds = len(mats)
    ext_rows = chunks * rows
    fixed = pl.BlockSpec((rows, width), lambda i: (0, 0))
    row = pl.BlockSpec((1, width), lambda i: (0, 0))
    placed = pl.BlockSpec((rows, TILE), lambda i: (chunk, i))
    out_specs = [pl.BlockSpec((rows, width), lambda i: (chunk, 0)), pl.BlockSpec((rows, LANES), lambda i: (0, 0)), placed, placed]
    out_shape = [jax.ShapeDtypeStruct((ext_rows, width), bf16), jax.ShapeDtypeStruct((rows, LANES), f32)]
    out_shape += [jax.ShapeDtypeStruct((ext_rows, width), bf16)] * 2
    if kinds == 3:
        out_specs.append(pl.BlockSpec((rows, TILE), lambda i: (0, i)))
        out_shape.append(jax.ShapeDtypeStruct((rows, width), bf16))
    aliases = {3 + 2 * kinds + i: place for i, place in enumerate((0, 2, 3)[: len(others)])}
    return pl.pallas_call(
        functools.partial(projection_kernel, kinds, len(others)),
        grid=(width // TILE,),
        in_specs=[fixed, row, row]
        + [pl.BlockSpec((width, TILE), lambda i: (0, i))] * kinds
        + [pl.BlockSpec((1, TILE), lambda i: (0, i))] * kinds
        + [pl.BlockSpec(memory_space=pl.ANY)] * len(others),
        out_specs=out_specs,
        out_shape=out_shape,
        scratch_shapes=[pltpu.VMEM((rows, width), bf16)],
        input_output_aliases=aliases,
        compiler_params=pltpu.CompilerParams(vmem_limit_bytes=VMEM_LIMIT),
        cost_estimate=SHORT,
    )(tokens, gain, shift, *mats, *shifts, *others)


def pack_kernel(weight, *refs):
    *vectors, packed, rider = refs
    width = packed.shape[-1] - LANES
    for kind in range(3):
        for pair in range(HEADS // 2):
            at = [((2 * pair + half) * 3 + kind) * HEAD_DIM for half in range(2)]
            packed[kind, :, pair * LANES : (pair + 1) * LANES] = jnp.concatenate(
                [weight[:, start : start + HEAD_DIM] for start in at], axis=1
            )
        packed[kind, :, width:] = jnp.zeros((packed.shape[1], LANES), bf16)
    rider[...] = jnp.zeros_like(rider)
    for i, vector in enumerate(vectors):
        rider[i : i + 1, : vector.shape[1]] = vector[...].astype(f32)
    packed[0, :, width:] = rider[...].astype(bf16)


def pack_joined(weight, vectors):
    rows, wide = weight.shape
    return pl.pallas_call(
        pack_kernel,
        out_shape=jax.ShapeDtypeStruct((3, rows, wide // 3 + LANES), bf16),
        scratch_shapes=[pltpu.VMEM((rows, LANES), f32)],
    )(weight, *(v[None] for v in vectors))


def unpack_kernel(riders, *refs):
    *vectors, query, value = refs
    for i, vector in enumerate(vectors):
        wide = vector.shape[1] // riders.shape[0]
        for device in range(riders.shape[0]):
            vector[:, device * wide : (device + 1) * wide] = riders[device, i : i + 1, :wide].astype(f32)
    for pair in range(HEADS // 2):
        for offset, out in ((0, query), (HEAD_DIM, value)):
            start = 4 * HEAD_DIM * pair + offset
            halves = [vectors[2][:, at : at + HEAD_DIM] for at in (start, start + 2 * HEAD_DIM)]
            out[:, pair * LANES : (pair + 1) * LANES] = jnp.concatenate(halves, axis=1)


def unpack_vectors(riders, counts):
    sizes = [riders.shape[0] * count for count in counts] + [HEADS * HEAD_DIM] * 2
    return pl.pallas_call(
        unpack_kernel,
        out_shape=[jax.ShapeDtypeStruct((1, size), f32) for size in sizes],
        cost_estimate=SHORT,
    )(riders)


def from_kinds(columns):
    rows = columns.shape[0]
    return columns.reshape(rows, 3, HEADS, HEAD_DIM).swapaxes(1, 2).reshape(rows, 3 * HEADS * HEAD_DIM)


def on_device(
    tokens,
    cotangent,
    lengths,
    valid_count,
    first_gain,
    first_shift,
    joined_weight,
    joined_bias,
    dense_weight,
    dense_bias,
    second_gain,
    second_shift,
    up_weight,
    up_bias,
    down_weight,
    down_bias,
):
    grid = Grid()
    tok_rows, width = tokens.shape
    hops = WINDOW // tok_rows
    shard_rows = joined_weight.shape[0]

    y, x, core, z = grid.here
    ny, nx, _, nz = grid.size
    chips = ny * nx
    up_rows, ff = up_weight.shape
    ff_core = ff // 2

    def core_columns(block, which):
        wide = block.shape[1] // chips // 2
        return jnp.concatenate(
            [lax.dynamic_slice_in_dim(block, (2 * chip + which) * wide, wide, 1) for chip in range(chips)], axis=1
        )

    vectors = (first_gain, first_shift, joined_bias, dense_bias, second_gain, second_shift, up_bias, down_bias)
    counts = [v.shape[0] for v in vectors]
    joined_line = direct_gather(grid, pack_joined(joined_weight, vectors), Z)
    (query_mat, key_mat, value_mat), riders = gather_joined(grid, joined_line)
    gain_one, shift_one, _, dense_vec, gain_two, shift_two, up_vec, down_vec, query_vec, value_vec = unpack_vectors(
        riders, counts
    )

    up_kept, up_given = (core_columns(up_weight, which) for which in (core, 1 - core))
    up_blocks = [half for side in (up_kept, grid.shift(up_given, CORE)) for half in (side[:, :width], side[:, width:])]
    lines = ("y", "x", "z")
    up_shard = after(jnp.stack([*up_blocks, dense_weight]), *joined_line[1:])
    up_lines = lax.all_gather(up_shard, lines, axis=0)
    down_mat = lax.all_gather(after(down_weight, *joined_line[1:]), lines, axis=0, tiled=True)

    before = [after(tokens, *joined_line[1:])]
    for _ in range(hops):
        before.append(grid.to_later(before[-1]))
    first_pos = grid.linear * tok_rows - WINDOW
    positions = first_pos + jnp.arange(WINDOW + tok_rows, dtype=jnp.int32)
    seg_ext = segment_ids(lengths, valid_count, positions)
    query_side, key_side = side_lanes(seg_ext, tok_rows)
    slopes = jnp.asarray(slope_lanes())
    live_rows = (positions[WINDOW:] < valid_count[0])[:, None]
    change_low = jnp.where(live_rows, cotangent, jnp.zeros_like(cotangent))
    change_both = jnp.concatenate([change_low, grid.shift(change_low, CORE)], axis=0)

    values = tokens.astype(f32)
    mats, shifts = (key_mat, value_mat), (jnp.zeros_like(value_vec), value_vec)
    normed_ext, stats, keys, all_values, queries = project(
        tokens, gain_one, shift_one, (*mats, query_mat), (*shifts, query_vec), hops, hops + 1
    )
    chunks = [(tokens, stats)]
    for hop in range(1, hops + 1):
        normed_ext, stats, keys, all_values = project(
            before[hop], gain_one, shift_one, mats, shifts, hops - hop, hops + 1, (normed_ext, keys, all_values)
        )
        chunks.insert(0, (before[hop], stats))
    context, log_total = attend(queries, keys, all_values, query_side, key_side, after(slopes, change_both))
    dense_part = after(up_lines[:, 4].reshape(-1, width), context)
    dense_other = grid.shift(dense_part, CORE)
    dense_sides = [jnp.where(core == which, dense_part, dense_other).reshape(chips, -1, width) for which in range(2)]
    dense_mat = jnp.stack(dense_sides, axis=1).reshape(-1, width)
    middle = values + dot_nn(context, dense_mat) + dense_vec
    normal_two, inverse_two = normalize(middle)
    normed_two = (normal_two * gain_two + shift_two).astype(bf16)
    normed_other = grid.shift(normed_two, CORE)
    hidden, slope = hidden_units(chips, core, normed_two, normed_other, up_lines, core_columns(up_vec, core))
    up_mat = whole_up(grid, up_lines, hidden)

    def far_sums(part, terms, *earlier):
        axis = (Y, X)[part]
        moving = terms[0]
        for step in range(1, grid.size[axis]):
            moving = add_after(grid.shift(moving, axis), terms[step], *earlier)
        return moving

    out_change = change_low.astype(f32)
    down_sums, down_vec_grad = down_terms(hidden, change_both)
    down_plane = lax.psum_scatter(down_sums, ("y", "x"), scatter_dimension=0, tiled=True)
    pre_change, up_core_grad = hidden_back(change_both, down_mat, slope, (down_sums,))
    given = product_nt(pre_change, up_mat, bf16, 1, tok_rows)
    up_sums = up_terms(normed_two, normed_other, pre_change, (given,))
    up_plane = lax.psum_scatter(up_sums, ("y", "x"), scatter_dimension=0, tiled=True)
    middle_change, branch_change, context_change, gain_two_grad, shift_two_grad, dense_vec_grad = middle_back(
        pre_change, up_mat, grid.shift(given, CORE), middle, gain_two, change_low, dense_mat, (up_sums,)
    )
    halves = HEADS // 4
    changes = attend_back(
        queries, keys, all_values, context_change, context, log_total, query_side, key_side, slopes, 0, halves
    )
    down_plane = after(down_plane, changes[0]).reshape(nz, -1, width)
    query_change, key_change, value_change = attend_back(
        queries, keys, all_values, context_change, context, log_total, query_side, key_side, after(slopes, down_plane),
        halves, halves, changes,
    )
    backs = [(back_y, back_x) for back_y in range(1, ny + 1) for back_x in range(1, nx + 1)]

    down_grad = direct_reduce(grid, down_plane, Z)
    chips_at = [(y - back_y) % ny * nx + (x - back_x) % nx for back_y, back_x in backs]
    rights = (query_change, key_change, value_change, branch_change)
    joined_given = joined_terms(normed_ext, context, rights, chips_at, core, (down_grad,))
    pairs = [(key_change, key_mat), (value_change, value_mat)]
    returned, *sums = chunk_back(
        [(left, 0, right) for left, right in pairs], chunks[0], bf16, None, joined_given[:1]
    )
    chunk_sums = [sums]
    joined_kept = split_terms(
        joined_given[2], grid.shift(joined_given[0], CORE), joined_given[3], grid.shift(joined_given[1], CORE), ny, nx, (returned,)
    )
    own_change, *sums = chunk_back(
        [(left, hops, right) for left, right in pairs] + [(query_change, 0, query_mat)], chunks[-1], f32, None, joined_kept
    )
    chunk_sums.append(sums)
    done = own_change
    for chunk in range(1, hops):
        arrived = grid.to_earlier(returned)
        returned, *sums = chunk_back(
            [(left, chunk, right) for left, right in pairs], chunks[chunk], bf16, arrived, (done,)
        )
        chunk_sums.append(sums)
        done = returned
    joined_near = []
    for terms, axis in ((joined_kept[:nx], X), (joined_kept[nx:], Y)):
        total = terms[0]
        for step in range(1, grid.size[axis]):
            total = add_after(grid.shift(total, axis), terms[step], done, split=step == grid.size[axis] - 1)
        joined_near.append(total)
    nears = [*joined_near[0], *joined_near[1]]
    up_rows_both = after(up_plane, *nears).reshape(2, nz, up_rows, ff_core).swapaxes(0, 1)
    up_sum = direct_reduce(grid, up_rows_both, Z)
    up_mine = lax.dynamic_index_in_dim(up_sum, core, 0, keepdims=False)
    up_other = grid.shift(lax.dynamic_index_in_dim(up_sum, 1 - core, 0, keepdims=False), CORE)
    returned = grid.to_earlier(returned)
    joined_far = [far_sums(part, joined_near[part], returned, up_sum) for part in range(2)]
    both = [half.reshape(4, nz // 2, -1, width) for half in joined_far]
    owned_rows = direct_reduce(grid, jnp.concatenate(both, axis=1).swapaxes(0, 1), Z)
    dense_grad = owned_rows[3]
    joined_grad = jnp.concatenate(list(owned_rows[:3]), axis=1)
    returned = returned.astype(f32)

    def interleave(mine, other):
        first, second = jnp.where(core == 0, mine, other), jnp.where(core == 0, other, mine)
        wide = mine.shape[1] // chips
        cuts = [slice(chip * wide, (chip + 1) * wide) for chip in range(chips)]
        return jnp.concatenate([side[:, cut] for cut in cuts for side in (first, second)], axis=1)

    up_grad = interleave(up_mine, up_other)
    branch_given = product_nn(hidden, down_mat, bf16, 1, tok_rows, nears)
    branch_two = product_nn(hidden, down_mat, f32, 0, tok_rows, nears) + grid.shift(branch_given, CORE).astype(f32)
    layer_output = jnp.where(live_rows, middle + (branch_two + down_vec), 0.0).astype(bf16)
    gain_one_grad, shift_one_grad = (sum(total).reshape(-1) for total in zip(*chunk_sums))
    joined_vec_grad = jnp.stack(
        [
            jnp.sum(query_change.astype(f32), axis=0).reshape(HEADS, HEAD_DIM),
            jnp.sum(value_change.astype(f32), axis=0).reshape(HEADS, HEAD_DIM),
        ],
        axis=1,
    ).reshape(-1)
    input_grad = (middle_change + norm_back(own_change + returned, *normalize(values), gain_one)).astype(bf16)
    up_parts = up_core_grad.reshape(chips, 1, -1)
    up_vec_grad = jnp.concatenate(
        [jnp.where(core == which, up_parts, jnp.zeros_like(up_parts)) for which in range(2)], axis=1
    ).reshape(-1)
    vector_grads = (
        gain_one_grad, shift_one_grad, joined_vec_grad, dense_vec_grad, gain_two_grad, shift_two_grad, up_vec_grad,
        down_vec_grad,
    )
    cuts = np.cumsum([0] + counts)
    vector_rows = jnp.concatenate([v.reshape(grid.count, -1) for v in vector_grads], axis=1)
    owned = reduce_scatter_small(grid, after(vector_rows, *nears))
    owned = [owned[cuts[i] : cuts[i + 1]] for i in range(len(counts))]
    return (
        layer_output,
        input_grad,
        owned[0],
        owned[1],
        from_kinds(joined_grad),
        owned[2],
        dense_grad,
        owned[3],
        owned[4],
        owned[5],
        up_grad,
        owned[6],
        down_grad,
        owned[7],
    )


def solution(mesh):
    blocks, heads = mesh.devices.shape
    split = jax.sharding.Mesh(mesh.devices.reshape(2, blocks // 4, 2, heads), ALL)
    rows, vector, same = P(ALL, None), P(ALL), P()
    return jax.shard_map(
        on_device,
        mesh=split,
        in_specs=(
            rows, rows, same, same, vector, vector, rows, vector, rows, vector, vector, vector, rows, vector, rows, vector
        ),
        out_specs=(rows, rows, vector, vector, rows, vector, rows, vector, vector, vector, rows, vector, rows, vector),
        check_vma=False,
    )
```

time: 685 us -> 486 us (0.71)
  waiting for transfers between devices: 274 us -> 111 us
  Pallas kernels: 54.8 us -> 210 us
  matrix products: 103 us -> 1.37 us
  local copies, waits for them, and re-layouts: 110 us -> 49 us
  other arithmetic: 58.8 us -> 31 us
  starting transfers between devices: 72.6 us -> 59 us
  between operations: 3.92 us -> 16 us
    ppermute x86 -> x43, waiting for transfers between devices: 274 us -> 91.3 us  [the longest x39 82.5 us: shift(): lax.ppermute(block, ALL, list(zip(places.ravel().tolist(), ahead.ravel()....]
    pallas_call x1 -> x36, Pallas kernels: 32.8 us -> 189 us  [the longest x2 34.7 us: attend_back(): pl.pallas_call(functools.partial(attend_back_kernel, first_pair=first_pai...]
    dot_general x12 -> x0, matrix products: 70.5 us -> none  [the longest x6 35.6 us: dot_tn(): lax.dot_general(left, right, (((0,), (0,)), ((), ())), preferred_element_...]
    dynamic_update_slice x79 -> x0, local copies, waits for them, and re-layouts: 52.5 us -> none  [the longest x64 43.2 us: gather(): lax.dynamic_update_slice(whole, block[near_step][None, None, None], (at[Y...]
    dot_general x5 -> x1, matrix products: 32.1 us -> 1.37 us  [dot_nn(): lax.dot_general(left, right, (((1,), (0,)), ((), ())), preferred_element_...]
    convert_element_type x32 -> x3, other arithmetic: 32.8 us -> 5.48 us  [the longest x1 3.22 us: on_device(): jnp.where(live_rows, middle + (branch_two + down_vec), 0.0).astype(bf16)]
    all_gather x0 -> x2, waiting for transfers between devices: none -> 19.4 us  [the longest x1 19.4 us: on_device(): lax.all_gather(after(down_weight, *joined_line[1:]), lines, axis=0, tiled...]
    unnamed x126 -> x175, local copies, waits for them, and re-layouts: 11.8 us -> 28.3 us
  transfers between devices with their start and end apart: 86 -> 47, of which waited for: 41 -> 18; matrix products, arithmetic and copies ran while one was open for 24% -> 11% of each run, Pallas kernels for 3% -> 44%
where the time goes in v2:
time: 486 us; the launch traced here: 478 us
  Pallas kernels  210 us (43%)
  waiting for transfers between devices  111 us (23%)
  starting transfers between devices  59 us (12%)
  local copies, waits for them, and re-layouts  49 us (10%)
  other arithmetic  31 us (6%)
  between operations  16 us (3%)
    ppermute x39, waiting for transfers between devices, shift(): lax.ppermute(block, ALL, list(zip(places.ravel().tolist(), ahead.ravel()....  82.5 us
    ppermute x39, starting transfers between devices, shift(): lax.ppermute(block, ALL, list(zip(places.ravel().tolist(), ahead.ravel()....  46.8 us
    pallas_call x2, Pallas kernels, attend_back(): pl.pallas_call(functools.partial(attend_back_kernel, first_pair=first_pai...  34.7 us
    unnamed x175, local copies, waits for them, and re-layouts  28.3 us
    pallas_call x3, Pallas kernels, project(): pl.pallas_call(functools.partial(projection_kernel, kinds, len(others)),...  21.3 us
    pallas_call x1, Pallas kernels, attend(): pl.pallas_call(attend_kernel, grid=(steps,), in_specs=[pl.BlockSpec((tok_...  21.2 us
    pallas_call x3, Pallas kernels, chunk_back(): pl.pallas_call(functools.partial(chunk_kernel, len(pairs), arrived is not...  20.6 us
    all_gather x1, waiting for transfers between devices, on_device(): lax.all_gather(after(down_weight, *joined_line[1:]), lines, axis=0, tiled...  19.4 us
  transfers between devices with their start and end apart: 47, of which 18 were waited for; matrix products, arithmetic and copies ran while one was open for 11% of the time, Pallas kernels for 44%

profile of v2, /device:TPU:0, one launch (start us, length us, event | category | flops | bytes accessed | tf_op | source)
XLA Modules:
  0.0 478.3 jit_solution(8662749802565914730)
XLA Ops:
  10.7 5.0 %collective-permute-start.6 = (bf16[3,32,1152]{2,1,0:T(8,128)(2,1)}, bf16[3,32,1152]{2,1,0:T(8,128)(2,1)S(1)}, u32[]{:S(2)}, u32[]{:S(2)}) collective-permute-start(bf16[3,32,1152]{2,1,0:T(8,128)(2,1)} %shard_map.272), channel_id=1, source_target_pairs={{0,3},{1,0},{2,1},{3,2},{4,7},{5,4},{6,5},{7,6},{8,11},{9,8},{10,9... | collective-permute-start | bytes 663560 | tf_op jit(solution)/shard_map/ppermute | solution.py:69
  21.9 12.8 %collective-permute-done.5.refs_2_ = bf16[3,32,1152]{2,1,0:T(8,128)(2,1)S(1)} collective-permute-done((bf16[3,32,1152]{2,1,0:T(8,128)(2,1)}, bf16[3,32,1152]{2,1,0:T(8,128)(2,1)S(1)}, u32[]{:S(2)}, u32[]{:S(2)}) %collective-permute-start.5) | collective-permute-done | bytes 221216 | tf_op jit(solution)/shard_map/ppermute | solution.py:69
  40.7 8.1 %collective-permute-done.7 = bf16[2,3,32,1152]{3,2,1,0:T(8,128)(2,1)S(1)} collective-permute-done((bf16[2,3,32,1152]{3,2,1,0:T(8,128)(2,1)S(1)}, bf16[2,3,32,1152]{3,2,1,0:T(8,128)(2,1)S(1)}, u32[]{:S(2)}, u32[]{:S(2)}) %collective-permute-start.7) | collective-permute-done | bytes 442400 | tf_op jit(solution)/shard_map/ppermute | solution.py:69
  54.3 4.0 collective-permute-start.11
  60.4 26.8 %collective-permute-done.9.refs_6_ = bf16[2,2,3,32,1152]{4,3,2,1,0:T(8,128)(2,1)} collective-permute-done((bf16[2,2,3,32,1152]{4,3,2,1,0:T(8,128)(2,1)}, bf16[2,2,3,32,1152]{4,3,2,1,0:T(8,128)(2,1)}, u32[]{:S(2)}, u32[]{:S(2)}) %collective-permute-start.9) | collective-permute-done | bytes 884768 | tf_op jit(solution)/shard_map/ppermute | solution.py:69
  88.9 5.3 %collective-permute-start.12 = (bf16[512,1024]{1,0:T(8,128)(2,1)}, bf16[512,1024]{1,0:T(8,128)(2,1)S(1)}, u32[]{:S(2)}, u32[]{:S(2)}) collective-permute-start(bf16[512,1024]{1,0:T(8,128)(2,1)} %collective-permute-done.11.tokens.refs_4_), channel_id=1, source_target_pairs={{0,1},{1,2},{2,3},{3,4},{4,5},{5,6},{6,7},{7,8},{8,9},{9,10},{10,1... | collective-permute-start | bytes 3145736 | tf_op jit(solution)/shard_map/ppermute | solution.py:72
  94.2 2.8 select_convert_fusion.1.key_side
  100.2 7.3 %shard_map.273 = (bf16[3,32,32,1024]{3,2,1,0:T(8,128)(2,1)}, bf16[32,32,128]{2,1,0:T(8,128)(2,1)S(1)}) custom-call(s32[32]{0:T(128)S(1)} %stack.305.places, bf16[2,2,3,32,1152]{4,3,2,1,0:T(8,128)(2,1)S(1)} %pad_maximum_fusion.2.refs_0_, bf16[2,2,3,32,1152]{4,3,2,1,0:T(8,128)(2,1)} %collective-permute-done.2.refs_1_, ...), custom_call_target="tpu_custom_call" | custom-call | flops 1 | bytes 1 | tf_op jit(solution)/shard_map/pallas_call | solution.py:137
  110.0 5.9 %fusion.49 = (bf16[1,32,32,1024]{3,2,1,0:T(8,128)(2,1)}, bf16[1,32,32,1024]{3,2,1,0:T(8,128)(2,1)}, bf16[1,32,32,1024]{3,2,1,0:T(8,128)(2,1)}) fusion(bf16[3,32,32,1024]{3,2,1,0:T(8,128)(2,1)} %get-tuple-element.82), kind=kLoop, calls=%fused_computation.157 | loop fusion | bytes 12582912 | tf_op jit(solution)/shard_map/unstack | solution.py:920
  115.9 7.8 %shard_map.275 = (bf16[1536,1024]{1,0:T(8,128)(2,1)}, f32[512,128]{1,0:T(8,128)S(1)}, bf16[1536,1024]{1,0:T(8,128)(2,1)}, bf16[1536,1024]{1,0:T(8,128)(2,1)}, bf16[512,1024]{1,0:T(8,128)(2,1)S(1)}) custom-call(bf16[512,1024]{1,0:T(8,128)(2,1)S(1)} %copy-done.2, f32[1,1024]{1,0:T(1,128)S(1)} %copy-done.49, f32[1,1024]{1,0:T(1,128)S(1)} %copy-done.50, ...), custom_call_target="tpu_custom_call" | custom-call | flops 1 | bytes 1 | tf_op jit(solution)/shard_map/pallas_call | solution.py:814
  124.4 6.9 %shard_map.277 = (bf16[1536,1024]{1,0:T(8,128)(2,1)}, f32[512,128]{1,0:T(8,128)S(1)}, bf16[1536,1024]{1,0:T(8,128)(2,1)}, bf16[1536,1024]{1,0:T(8,128)(2,1)}) custom-call(bf16[512,1024]{1,0:T(8,128)(2,1)} %collective-permute-done.11.tokens.refs_4_, f32[1,1024]{1,0:T(1,128)S(1)} %copy-done.49, ...), custom_call_target="tpu_custom_call", output_to_operand_aliasing={{0}: (7, {}), {2}: (8, {}), {3}: (9, {})} | custom-call | flops 1 | bytes 1 | tf_op jit(solution)/shard_map/pallas_call | solution.py:814
  131.3 3.0 collective-permute-done.12.tokens.refs_4_
  134.3 6.6 %shard_map.278 = (bf16[1536,1024]{1,0:T(8,128)(2,1)}, f32[512,128]{1,0:T(8,128)S(1)}, bf16[1536,1024]{1,0:T(8,128)(2,1)}, bf16[1536,1024]{1,0:T(8,128)(2,1)}) custom-call(bf16[512,1024]{1,0:T(8,128)(2,1)S(1)} %collective-permute-done.12.tokens.refs_4_, f32[1,1024]{1,0:T(1,128)S(1)} %copy-done.49, ...), custom_call_target="tpu_custom_call", output_to_operand_aliasing={{0}: (7, {}), {2}: (8, {}), {3}: (9, {})} | custom-call | flops 1 | bytes 1 | tf_op jit(solution)/shard_map/pallas_call | solution.py:814
  141.6 21.2 %shard_map.280 = (bf16[512,1024]{1,0:T(8,128)(2,1)S(1)}, f32[512,128]{1,0:T(8,128)S(1)}) custom-call(bf16[512,1024]{1,0:T(8,128)(2,1)} %copy-done.7, bf16[1536,1024]{1,0:T(8,128)(2,1)} %get-tuple-element.92.key, bf16[1536,1024]{1,0:T(8,128)(2,1)} %get-tuple-element.93.value, bf16[512,128]{1,0:T(8,128)(2,1)S(1)} %select_convert_fusion.2.query_side, ...), custom_call_target="tpu_custom_call" | custom-call | flops 1 | bytes 1 | tf_op jit(solution)/shard_map/pallas_call | solution.py:571
  165.3 2.8 collective-permute-done.15
  173.5 2.5 collective-permute-done.16.other
  176.0 13.3 %shard_map.283 = (bf16[1024,2048]{1,0:T(8,128)(2,1)}, bf16[1024,2048]{1,0:T(8,128)(2,1)}) custom-call(s32[1]{0:T(128)} %bitcast.66.core, bf16[512,1024]{1,0:T(8,128)(2,1)S(1)} %add_convert_fusion.own, bf16[512,1024]{1,0:T(8,128)(2,1)S(1)} %collective-permute-done.16.other, bf16[16,5,32,1024]{3,2,1,0:T(8,128)(2,1)} %bitcast.234, ...), custom_call_target="tpu_custom_call" | custom-call | flops 1 | bytes 1 | tf_op jit(solution)/shard_map/pallas_call | solution.py:738
  189.3 9.6 %shard_map.285 = (bf16[2048,1024]{1,0:T(8,128)(2,1)}, f32[1,1024]{1,0:T(1,128)S(1)}) custom-call(bf16[1024,2048]{1,0:T(8,128)(2,1)} %get-tuple-element.99.left.refs_1_, bf16[1024,1024]{1,0:T(8,128)(2,1)S(1)} %copy-done.4), custom_call_target="tpu_custom_call" | custom-call | flops 1 | bytes 1 | tf_op jit(solution)/shard_map/pallas_call | solution.py:234
  201.9 5.3 %shard_map.288 = bf16[32,32,2048]{2,1,0:T(8,128)(2,1)} custom-call(s32[32]{0:T(128)S(1)} %shard_map.287.places, bf16[16,5,32,1024]{3,2,1,0:T(8,128)(2,1)} %bitcast.236), custom_call_target="tpu_custom_call" | custom-call | flops 1 | bytes 1 | tf_op jit(solution)/shard_map/pallas_call | solution.py:137
  207.2 19.4 %all-gather.4.cloned.1.call-done.down.right = bf16[2048,1024]{1,0:T(8,128)(2,1)} async-done(((bf16[128,1024]{1,0:T(8,128)(2,1)}), bf16[2048,1024]{1,0:T(8,128)(2,1)}) %all-gather.4.cloned.1.call-update) | async-done | bytes 4194320 | tf_op jit(solution)/shard_map/all_gather | solution.py:930
  226.7 10.5 %shard_map.286 = (bf16[1024,2048]{1,0:T(8,128)(2,1)}, f32[1,2048]{1,0:T(1,128)S(1)}) custom-call(bf16[1024,1024]{1,0:T(8,128)(2,1)S(1)} %copy-done.4, bf16[2048,1024]{1,0:T(8,128)(2,1)} %all-gather.4.cloned.1.call-done.down.right, bf16[1024,2048]{1,0:T(8,128)(2,1)} %get-tuple-element.101.slope, bf16[2048,1024]{1,0:T(8,128)(2,1)} %get-tuple-element.102.refs_0_), custom_call_target="tpu_custom_call" | custom-call | flops 1 | bytes 1 | tf_op jit(solution)/shard_map/pallas_call | solution.py:764
  237.2 5.8 %shard_map.289.refs_0_ = bf16[512,1024]{1,0:T(8,128)(2,1)S(1)} custom-call(bf16[1024,2048]{1,0:T(8,128)(2,1)} %get-tuple-element.103.left.right.pre_change, bf16[1024,2048]{1,0:T(8,128)(2,1)} %bitcast.237), custom_call_target="tpu_custom_call" | custom-call | flops 1 | bytes 1 | tf_op jit(solution)/shard_map/pallas_call | solution.py:298
  243.1 10.1 %shard_map.290.refs_0_ = bf16[1024,2048]{1,0:T(8,128)(2,1)} custom-call(bf16[512,1024]{1,0:T(8,128)(2,1)S(1)} %copy-done.10, bf16[512,1024]{1,0:T(8,128)(2,1)S(1)} %copy-done.23, bf16[1024,2048]{1,0:T(8,128)(2,1)} %get-tuple-element.103.left.right.pre_change, bf16[512,1024]{1,0:T(8,128)(2,1)S(1)} %shard_map.289.refs_0_), custom_call_target="tpu_custom_call" | custom-call | flops 1 | bytes 1 | tf_op jit(solution)/shard_map/pallas_call | solution.py:257
  253.4 2.6 collective-permute-done.17.arrived
  255.9 9.5 %shard_map.291 = (f32[512,1024]{1,0:T(8,128)}, bf16[512,1024]{1,0:T(8,128)(2,1)S(1)}, bf16[512,1024]{1,0:T(8,128)(2,1)S(1)}, f32[1,1024]{1,0:T(1,128)S(1)}, f32[...) custom-call(bf16[1024,2048]{1,0:T(8,128)(2,1)} %get-tuple-element.103.left.right.pre_change, bf16[1024,2048]{1,0:T(8,128)(2,1)} %bitcast.238, ...), custom_call_target="tpu_custom_call" | custom-call | flops 1 | bytes 1 | tf_op jit(solution)/shard_map/pallas_call | solution.py:395
  269.2 17.0 %shard_map.292 = (bf16[512,1024]{1,0:T(8,128)(2,1)S(1)}, bf16[1536,1024]{1,0:T(8,128)(2,1)}, bf16[1536,1024]{1,0:T(8,128)(2,1)}) custom-call(bf16[512,1024]{1,0:T(8,128)(2,1)} %copy-done.7, bf16[1536,1024]{1,0:T(8,128)(2,1)} %get-tuple-element.92.key, bf16[1536,1024]{1,0:T(8,128)(2,1)} %get-tuple-element.93.value, bf16[512,1024]{1,0:T(8,128)(2,1)} %copy-done.15, ...), custom_call_target="tpu_custom_call" | custom-call | flops 1 | bytes 1 | tf_op jit(solution)/shard_map/pallas_call | solution.py:659
  296.2 17.7 %shard_map.295 = (bf16[512,1024]{1,0:T(8,128)(2,1)S(1)}, bf16[1536,1024]{1,0:T(8,128)(2,1)}, bf16[1536,1024]{1,0:T(8,128)(2,1)}) custom-call(bf16[512,1024]{1,0:T(8,128)(2,1)} %copy-done.7, bf16[1536,1024]{1,0:T(8,128)(2,1)} %get-tuple-element.92.key, ...), custom_call_target="tpu_custom_call", output_to_operand_aliasing={{0}: (9, {}), {1}: (10, {}), {2}: (11, {})} | custom-call | flops 1 | bytes 1 | tf_op jit(solution)/shard_map/pallas_call | solution.py:659
  316.5 14.9 %shard_map.296 = (bf16[4,4,64,1024]{3,2,1,0:T(8,128)(2,1)}, bf16[4,4,64,1024]{3,2,1,0:T(8,128)(2,1)}, bf16[4,4,64,1024]{3,2,1,0:T(8,128)(2,1)}, bf16[4,4,64,1024]{3,2,1,0:T(8,128)(2,1)}) custom-call(s32[4]{0:T(128)S(1)} %pad_add_fusion.blocks, s32[1]{0:T(128)} %bitcast.66.core, bf16[1536,1024]{1,0:T(8,128)(2,1)} %get-tuple-element.100.tokens_ext, ...), custom_call_target="tpu_custom_call" | custom-call | flops 1 | bytes 1 | tf_op jit(solution)/shard_map/pallas_call | solution.py:439
  332.1 6.4 %shard_map.297 = (bf16[512,1024]{1,0:T(8,128)(2,1)}, f32[1,1024]{1,0:T(1,128)S(1)}, f32[1,1024]{1,0:T(1,128)S(1)}) custom-call(bf16[1536,1024]{1,0:T(8,128)(2,1)} %get-tuple-element.110.key.refs_0_, bf16[1536,1024]{1,0:T(8,128)(2,1)} %get-tuple-element.111.value.refs_1_, bf16[1024,1024]{1,0:T(8,128)(2,1)} %bitcast.206, bf16[1024,1024]{1,0:T(8,128)(2,1)} %bitcast.230, ...), custom_call_target="tpu_custom_call" | custom-call | flops 1 | bytes 1 | tf_op jit(solution)/shard_map/pallas_call | solution.py:352
  340.9 5.8 %shard_map.298 = (bf16[2,4,64,1024]{3,2,1,0:T(8,128)(2,1)}, bf16[2,4,64,1024]{3,2,1,0:T(8,128)(2,1)S(1)}, bf16[2,4,64,1024]{3,2,1,0:T(8,128)(2,1)}, bf16[2,4,64,1024]{3,2,1,0:T(8,128)(2,1)}) custom-call(bf16[2,2,4,64,1024]{4,3,2,1,0:T(8,128)(2,1)} %bitcast.245, bf16[2,2,4,64,1024]{4,3,2,1,0:T(8,128)(2,1)} %bitcast.112.arrived_ahead, ...), custom_call_target="tpu_custom_call" | custom-call | flops 1 | bytes 1 | tf_op jit(solution)/shard_map/pallas_call | solution.py:476
  347.6 3.1 collective-permute-start.23
  355.8 7.8 %shard_map.299 = (f32[512,1024]{1,0:T(8,128)}, f32[1,1024]{1,0:T(1,128)S(1)}, f32[1,1024]{1,0:T(1,128)S(1)}) custom-call(bf16[1536,1024]{1,0:T(8,128)(2,1)} %get-tuple-element.110.key.refs_0_, bf16[1536,1024]{1,0:T(8,128)(2,1)} %get-tuple-element.111.value.refs_1_, bf16[512,1024]{1,0:T(8,128)(2,1)S(1)} %get-tuple-element.109.query.refs_2_, ...), custom_call_target="tpu_custom_call" | custom-call | flops 1 | bytes 1 | tf_op jit(solution)/shard_map/pallas_call | solution.py:352
  365.8 6.5 %shard_map.300 = (bf16[512,1024]{1,0:T(8,128)(2,1)}, f32[1,1024]{1,0:T(1,128)S(1)}, f32[1,1024]{1,0:T(1,128)S(1)}) custom-call(bf16[1536,1024]{1,0:T(8,128)(2,1)} %get-tuple-element.110.key.refs_0_, bf16[1536,1024]{1,0:T(8,128)(2,1)} %get-tuple-element.111.value.refs_1_, bf16[1024,1024]{1,0:T(8,128)(2,1)} %bitcast.208, bf16[1024,1024]{1,0:T(8,128)(2,1)} %bitcast.232, ...), custom_call_target="tpu_custom_call" | custom-call | flops 1 | bytes 1 | tf_op jit(solution)/shard_map/pallas_call | solution.py:352
  380.3 6.9 %collective-permute-start.34 = (bf16[4,64,1024]{2,1,0:T(8,128)(2,1)}, bf16[4,64,1024]{2,1,0:T(8,128)(2,1)}, u32[]{:S(2)}, u32[]{:S(2)}) collective-permute-start(bf16[4,64,1024]{2,1,0:T(8,128)(2,1)} %get-tuple-element.127.refs_0_.refs_1_), channel_id=1, source_target_pairs={{0,16},{1,17},{2,18},{3,19},{4,20},{5,21},{6,22},{7,23},{8,24},{9,... | collective-permute-start | bytes 1572872 | tf_op jit(solution)/shard_map/ppermute | solution.py:69
  395.3 3.5 collective-permute-done.27.refs_0_
  399.7 3.3 collective-permute-start.29
  403.0 3.8 collective-permute-start.37
  408.8 5.5 %shard_map.304 = bf16[512,1024]{1,0:T(8,128)(2,1)S(1)} custom-call(bf16[1024,2048]{1,0:T(8,128)(2,1)} %get-tuple-element.99.left.refs_1_, bf16[2048,1024]{1,0:T(8,128)(2,1)} %all-gather.4.cloned.1.call-done.down.right, bf16[4,64,1024]{2,1,0:T(8,128)(2,1)} %get-tuple-element.127.refs_0_.refs_1_, ...), custom_call_target="tpu_custom_call" | custom-call | flops 1 | bytes 1 | tf_op jit(solution)/shard_map/pallas_call | solution.py:319
  414.3 6.5 %shard_map.303 = f32[512,1024]{1,0:T(8,128)} custom-call(bf16[1024,2048]{1,0:T(8,128)(2,1)} %get-tuple-element.99.left.refs_1_, bf16[2048,1024]{1,0:T(8,128)(2,1)} %all-gather.4.cloned.1.call-done.down.right, bf16[4,64,1024]{2,1,0:T(8,128)(2,1)} %get-tuple-element.127.refs_0_.refs_1_, bf16[4,64,1024]{2,1,0:T(8,128)(2,1)S(1)} %get-tuple-element.128.refs_1_.refs_2_.right, ...), custom_call_target="tpu_custom_call" | custom-call | flops 1 | bytes 1 | tf_op jit(solution)/shard_map/pallas_call | solution.py:319
  423.0 3.3 collective-permute-start.33
  426.2 4.3 collective-permute-done.36
  432.2 2.8 collective-permute-done.32
  439.4 3.1 collective-permute-start.41
  442.5 7.3 %collective-permute-done.39 = bf16[4,32,1024]{2,1,0:T(8,128)(2,1)S(1)} collective-permute-done((bf16[4,32,1024]{2,1,0:T(8,128)(2,1)S(1)}, bf16[4,32,1024]{2,1,0:T(8,128)(2,1)S(1)}, u32[]{:S(2)}, u32[]{:S(2)}) %collective-permute-start.39) | collective-permute-done | bytes 262176 | tf_op jit(solution)/shard_map/ppermute | solution.py:69
  449.7 9.3 %collective-permute-done.40 = bf16[4,32,1024]{2,1,0:T(8,128)(2,1)S(1)} collective-permute-done((bf16[4,32,1024]{2,1,0:T(8,128)(2,1)S(1)}, bf16[4,32,1024]{2,1,0:T(8,128)(2,1)S(1)}, u32[]{:S(2)}, u32[]{:S(2)}) %collective-permute-start.40) | collective-permute-done | bytes 262176 | tf_op jit(solution)/shard_map/ppermute | solution.py:69
  462.8 2.9 maximum_bitcast_fusion
  465.7 2.6 reshape.298
  468.3 3.2 select_convert_fusion
  (359 shorter events, 100.2 us)
Async XLA Ops:
  7.2 156.3 %all-gather.6.cloned.1.call-start = ((), (), s32[]{:S(2)}) async-start(), calls=%async_computation.5 | async-start | bytes 5570560 | tf_op jit(solution)/shard_map/all_gather | solution.py:929
  10.7 11.2 %collective-permute-start.6 = (bf16[3,32,1152]{2,1,0:T(8,128)(2,1)}, bf16[3,32,1152]{2,1,0:T(8,128)(2,1)S(1)}, u32[]{:S(2)}, u32[]{:S(2)}) collective-permute-start(bf16[3,32,1152]{2,1,0:T(8,128)(2,1)} %shard_map.272), channel_id=1, source_target_pairs={{0,3},{1,0},{2,1},{3,2},{4,7},{5,4},{6,5},{7,6},{8,11},{9,8},{10,9... | collective-permute-start | bytes 663560 | tf_op jit(solution)/shard_map/ppermute | solution.py:69
  15.7 19.0 %collective-permute-start.5 = (bf16[3,32,1152]{2,1,0:T(8,128)(2,1)}, bf16[3,32,1152]{2,1,0:T(8,128)(2,1)S(1)}, u32[]{:S(2)}, u32[]{:S(2)}) collective-permute-start(bf16[3,32,1152]{2,1,0:T(8,128)(2,1)} %shard_map.272), channel_id=1, source_target_pairs={{0,2},{1,3},{2,0},{3,1},{4,6},{5,7},{6,4},{7,5},{8,10},{9,11},{10,... | collective-permute-start | bytes 663560 | tf_op jit(solution)/shard_map/ppermute | solution.py:69
  15.7 19.0 %collective-permute-start = (bf16[3,32,1152]{2,1,0:T(8,128)(2,1)}, bf16[3,32,1152]{2,1,0:T(8,128)(2,1)S(1)}, u32[]{:S(2)}, u32[]{:S(2)}) collective-permute-start(bf16[3,32,1152]{2,1,0:T(8,128)(2,1)} %shard_map.272), channel_id=1, source_target_pairs={{0,1},{1,2},{2,3},{3,0},{4,5},{5,6},{6,7},{7,4},{8,9},{9,10},{10,1... | collective-permute-start | bytes 663560 | tf_op jit(solution)/shard_map/ppermute | solution.py:69
  17.7 1.4 collective-permute-start.14
  34.8 191.9 %all-gather.4.cloned.1.call-start = ((), (), s32[]{:S(2)}) async-start(), calls=%async_computation.2 | async-start | bytes 4456448 | tf_op jit(solution)/shard_map/all_gather | solution.py:930
  35.6 250.6 %reduce-scatter.3.cloned.1.call-start = ((), (), s32[]{:S(2)}) async-start(), calls=%async_computation.3 | async-start | bytes 5242880 | tf_op jit(solution)/shard_map/reduce_scatter | solution.py:976
  36.4 12.5 %collective-permute-start.7 = (bf16[2,3,32,1152]{3,2,1,0:T(8,128)(2,1)S(1)}, bf16[2,3,32,1152]{3,2,1,0:T(8,128)(2,1)S(1)}, u32[]{:S(2)}, u32[]{:S(2)}) collective-permute-start(bf16[2,3,32,1152]{3,2,1,0:T(8,128)(2,1)S(1)} %get-tuple-element.171), channel_id=1, source_target_pairs={{0,16},{1,17},{2,18},{3,19},{4,20},{5,21},{6,22},{7,23},{8,24},{9,... | collective-permute-start | bytes 1327112 | tf_op jit(solution)/shard_map/ppermute | solution.py:69
  38.0 14.5 %collective-permute-start.1 = (bf16[2,3,32,1152]{3,2,1,0:T(8,128)(2,1)S(1)}, bf16[2,3,32,1152]{3,2,1,0:T(8,128)(2,1)S(1)}, u32[]{:S(2)}, u32[]{:S(2)}) collective-permute-start(bf16[2,3,32,1152]{3,2,1,0:T(8,128)(2,1)S(1)} %get-tuple-element.173), channel_id=1, source_target_pairs={{0,8},{1,9},{2,10},{3,11},{4,12},{5,13},{6,14},{7,15},{8,0},{9,1},... | collective-permute-start | bytes 1327112 | tf_op jit(solution)/shard_map/ppermute | solution.py:69
  40.7 19.1 %collective-permute-start.13 = (bf16[512,1024]{1,0:T(8,128)(2,1)}, bf16[512,1024]{1,0:T(8,128)(2,1)}, u32[]{:S(2)}, u32[]{:S(2)}) collective-permute-start(bf16[512,1024]{1,0:T(8,128)(2,1)} %broadcast_select_fusion.out_change), channel_id=1, source_target_pairs={{0,4},{1,5},{2,6},{3,7},{4,0},{5,1},{6,2},{7,3},{8,12},{9,13},{10,... | collective-permute-start | bytes 3145736 | tf_op jit(solution)/shard_map/ppermute | solution.py:69
  49.9 37.3 %collective-permute-start.9 = (bf16[2,2,3,32,1152]{4,3,2,1,0:T(8,128)(2,1)}, bf16[2,2,3,32,1152]{4,3,2,1,0:T(8,128)(2,1)}, u32[]{:S(2)}, u32[]{:S(2)}) collective-permute-start(bf16[2,2,3,32,1152]{4,3,2,1,0:T(8,128)(2,1)} %pad_maximum_fusion.3.refs_4_), channel_id=1, source_target_pairs={{0,8},{1,9},{2,10},{3,11},{4,12},{5,13},{6,14},{7,15},{8,0},{9,1},... | collective-permute-start | bytes 2654216 | tf_op jit(solution)/shard_map/ppermute | solution.py:69
  52.6 34.5 %collective-permute-start.3 = (bf16[2,2,3,32,1152]{4,3,2,1,0:T(8,128)(2,1)S(1)}, bf16[2,2,3,32,1152]{4,3,2,1,0:T(8,128)(2,1)}, u32[]{:S(2)}, u32[]{:S(2)}) collective-permute-start(bf16[2,2,3,32,1152]{4,3,2,1,0:T(8,128)(2,1)S(1)} %pad_maximum_fusion.2.refs_0_), channel_id=1, source_target_pairs={{0,16},{1,17},{2,18},{3,19},{4,20},{5,21},{6,22},{7,23},{8,24},{9,... | collective-permute-start | bytes 2654216 | tf_op jit(solution)/shard_map/ppermute | solution.py:69
  54.3 34.5 %collective-permute-start.11 = (bf16[512,1024]{1,0:T(8,128)(2,1)S(1)}, bf16[512,1024]{1,0:T(8,128)(2,1)}, u32[]{:S(2)}, u32[]{:S(2)}) collective-permute-start(bf16[512,1024]{1,0:T(8,128)(2,1)S(1)} %shard_map.276), channel_id=1, source_target_pairs={{0,1},{1,2},{2,3},{3,4},{4,5},{5,6},{6,7},{7,8},{8,9},{9,10},{10,1... | collective-permute-start | bytes 3145736 | tf_op jit(solution)/shard_map/ppermute | solution.py:72
  59.8 40.4 %collective-permute-start.8 = (bf16[2,2,3,32,1152]{4,3,2,1,0:T(8,128)(2,1)}, bf16[2,2,3,32,1152]{4,3,2,1,0:T(8,128)(2,1)}, u32[]{:S(2)}, u32[]{:S(2)}) collective-permute-start(bf16[2,2,3,32,1152]{4,3,2,1,0:T(8,128)(2,1)} %pad_maximum_fusion.3.refs_4_), channel_id=1, source_target_pairs={{0,4},{1,5},{2,6},{3,7},{4,0},{5,1},{6,2},{7,3},{8,12},{9,13},{10,... | collective-permute-start | bytes 2654216 | tf_op jit(solution)/shard_map/ppermute | solution.py:69
  59.9 40.3 %collective-permute-start.2 = (bf16[2,2,3,32,1152]{4,3,2,1,0:T(8,128)(2,1)S(1)}, bf16[2,2,3,32,1152]{4,3,2,1,0:T(8,128)(2,1)}, u32[]{:S(2)}, u32[]{:S(2)}) collective-permute-start(bf16[2,2,3,32,1152]{4,3,2,1,0:T(8,128)(2,1)S(1)} %pad_maximum_fusion.2.refs_0_), channel_id=1, source_target_pairs={{0,4},{1,5},{2,6},{3,7},{4,0},{5,1},{6,2},{7,3},{8,12},{9,13},{10,... | collective-permute-start | bytes 2654216 | tf_op jit(solution)/shard_map/ppermute | solution.py:69
  87.1 13.0 %collective-permute-start.10 = (bf16[2,2,3,32,1152]{4,3,2,1,0:T(8,128)(2,1)}, bf16[2,2,3,32,1152]{4,3,2,1,0:T(8,128)(2,1)}, u32[]{:S(2)}, u32[]{:S(2)}) collective-permute-start(bf16[2,2,3,32,1152]{4,3,2,1,0:T(8,128)(2,1)} %collective-permute-done.9.refs_6_), channel_id=1, source_target_pairs={{0,4},{1,5},{2,6},{3,7},{4,0},{5,1},{6,2},{7,3},{8,12},{9,13},{10,... | collective-permute-start | bytes 2654216 | tf_op jit(solution)/shard_map/ppermute | solution.py:69
  87.1 13.0 %collective-permute-start.4 = (bf16[2,2,3,32,1152]{4,3,2,1,0:T(8,128)(2,1)}, bf16[2,2,3,32,1152]{4,3,2,1,0:T(8,128)(2,1)}, u32[]{:S(2)}, u32[]{:S(2)}) collective-permute-start(bf16[2,2,3,32,1152]{4,3,2,1,0:T(8,128)(2,1)} %collective-permute-done.3.refs_2_), channel_id=1, source_target_pairs={{0,4},{1,5},{2,6},{3,7},{4,0},{5,1},{6,2},{7,3},{8,12},{9,13},{10,... | collective-permute-start | bytes 2654216 | tf_op jit(solution)/shard_map/ppermute | solution.py:69
  88.9 52.8 %copy-start.28 = (bf16[512,128]{1,0:T(8,128)(2,1)}, bf16[512,128]{1,0:T(8,128)(2,1)S(1)}, u32[]{:S(2)}) copy-start(bf16[512,128]{1,0:T(8,128)(2,1)S(1)} %select_convert_fusion.2.query_side) | copy-start | bytes 393220
  88.9 45.4 %collective-permute-start.12 = (bf16[512,1024]{1,0:T(8,128)(2,1)}, bf16[512,1024]{1,0:T(8,128)(2,1)S(1)}, u32[]{:S(2)}, u32[]{:S(2)}) collective-permute-start(bf16[512,1024]{1,0:T(8,128)(2,1)} %collective-permute-done.11.tokens.refs_4_), channel_id=1, source_target_pairs={{0,1},{1,2},{2,3},{3,4},{4,5},{5,6},{6,7},{7,8},{8,9},{9,10},{10,1... | collective-permute-start | bytes 3145736 | tf_op jit(solution)/shard_map/ppermute | solution.py:72
  165.2 2.9 collective-permute-start.15
  173.3 2.7 collective-permute-start.16
  199.6 191.3 %reduce-scatter.5.cloned.1.call-start = ((), (), s32[]{:S(2)}) async-start(), calls=%async_computation.4 | async-start | bytes 5242880 | tf_op jit(solution)/shard_map/reduce_scatter | solution.py:980
  253.2 2.7 collective-permute-start.17
  288.3 25.6 %collective-permute-start.18 = (bf16[128,1024]{1,0:T(8,128)(2,1)}, bf16[128,1024]{1,0:T(8,128)(2,1)}, u32[]{:S(2)}, u32[]{:S(2)}) collective-permute-start(bf16[128,1024]{1,0:T(8,128)(2,1)} %get-tuple-element.161), channel_id=1, source_target_pairs={{0,1},{1,2},{2,3},{3,0},{4,5},{5,6},{6,7},{7,4},{8,9},{9,10},{10,1... | collective-permute-start | bytes 786440 | tf_op jit(solution)/shard_map/ppermute | solution.py:69
  289.6 24.2 %collective-permute-start.20 = (bf16[128,1024]{1,0:T(8,128)(2,1)}, bf16[128,1024]{1,0:T(8,128)(2,1)}, u32[]{:S(2)}, u32[]{:S(2)}) collective-permute-start(bf16[128,1024]{1,0:T(8,128)(2,1)} %get-tuple-element.162), channel_id=1, source_target_pairs={{0,3},{1,0},{2,1},{3,2},{4,7},{5,4},{6,5},{7,6},{8,11},{9,8},{10,9... | collective-permute-start | bytes 786440 | tf_op jit(solution)/shard_map/ppermute | solution.py:69
  292.1 23.1 %collective-permute-start.19 = (bf16[128,1024]{1,0:T(8,128)(2,1)}, bf16[128,1024]{1,0:T(8,128)(2,1)}, u32[]{:S(2)}, u32[]{:S(2)}) collective-permute-start(bf16[128,1024]{1,0:T(8,128)(2,1)} %get-tuple-element.163), channel_id=1, source_target_pairs={{0,2},{1,3},{2,0},{3,1},{4,6},{5,7},{6,4},{7,5},{8,10},{9,11},{10,... | collective-permute-start | bytes 786440 | tf_op jit(solution)/shard_map/ppermute | solution.py:69
  331.4 9.5 %collective-permute-start.22 = (bf16[4,4,64,1024]{3,2,1,0:T(8,128)(2,1)}, bf16[4,4,64,1024]{3,2,1,0:T(8,128)(2,1)}, u32[]{:S(2)}, u32[]{:S(2)}) collective-permute-start(bf16[4,4,64,1024]{3,2,1,0:T(8,128)(2,1)} %get-tuple-element.116), channel_id=1, source_target_pairs={{0,4},{1,5},{2,6},{3,7},{4,0},{5,1},{6,2},{7,3},{8,12},{9,13},{10,... | collective-permute-start | bytes 6291464 | tf_op jit(solution)/shard_map/ppermute | solution.py:69
  331.4 9.5 %collective-permute-start.21 = (bf16[4,4,64,1024]{3,2,1,0:T(8,128)(2,1)}, bf16[4,4,64,1024]{3,2,1,0:T(8,128)(2,1)}, u32[]{:S(2)}, u32[]{:S(2)}) collective-permute-start(bf16[4,4,64,1024]{3,2,1,0:T(8,128)(2,1)} %get-tuple-element.114.refs_6_), channel_id=1, source_target_pairs={{0,4},{1,5},{2,6},{3,7},{4,0},{5,1},{6,2},{7,3},{8,12},{9,13},{10,... | collective-permute-start | bytes 6291464 | tf_op jit(solution)/shard_map/ppermute | solution.py:69
  338.5 27.3 %collective-permute-start.24 = (bf16[512,1024]{1,0:T(8,128)(2,1)}, bf16[512,1024]{1,0:T(8,128)(2,1)S(1)}, u32[]{:S(2)}, u32[]{:S(2)}) collective-permute-start(bf16[512,1024]{1,0:T(8,128)(2,1)} %get-tuple-element.118.refs_0_), channel_id=1, source_target_pairs={{1,0},{2,1},{3,2},{4,3},{5,4},{6,5},{7,6},{8,7},{9,8},{10,9},{11,1... | collective-permute-start | bytes 3145736 | tf_op jit(solution)/shard_map/ppermute | solution.py:75
  347.6 29.3 %collective-permute-start.23 = (bf16[2,4,64,1024]{3,2,1,0:T(8,128)(2,1)}, bf16[2,4,64,1024]{3,2,1,0:T(8,128)(2,1)}, u32[]{:S(2)}, u32[]{:S(2)}) collective-permute-start(bf16[2,4,64,1024]{3,2,1,0:T(8,128)(2,1)} %get-tuple-element.119.refs_8_), channel_id=1, source_target_pairs={{0,8},{1,9},{2,10},{3,11},{4,12},{5,13},{6,14},{7,15},{8,0},{9,1},... | collective-permute-start | bytes 3145736 | tf_op jit(solution)/shard_map/ppermute | solution.py:69
  350.7 36.5 %collective-permute-start.25 = (bf16[2,4,64,1024]{3,2,1,0:T(8,128)(2,1)}, bf16[2,4,64,1024]{3,2,1,0:T(8,128)(2,1)}, u32[]{:S(2)}, u32[]{:S(2)}) collective-permute-start(bf16[2,4,64,1024]{3,2,1,0:T(8,128)(2,1)} %get-tuple-element.123.refs_10_), channel_id=1, source_target_pairs={{0,16},{1,17},{2,18},{3,19},{4,20},{5,21},{6,22},{7,23},{8,24},{9,... | collective-permute-start | bytes 3145736 | tf_op jit(solution)/shard_map/ppermute | solution.py:69
  372.3 26.6 %collective-permute-start.27 = (bf16[512,1024]{1,0:T(8,128)(2,1)}, bf16[512,1024]{1,0:T(8,128)(2,1)S(1)}, u32[]{:S(2)}, u32[]{:S(2)}) collective-permute-start(bf16[512,1024]{1,0:T(8,128)(2,1)} %get-tuple-element.126.refs_0_), channel_id=1, source_target_pairs={{1,0},{2,1},{3,2},{4,3},{5,4},{6,5},{7,6},{8,7},{9,8},{10,9},{11,1... | collective-permute-start | bytes 3145736 | tf_op jit(solution)/shard_map/ppermute | solution.py:75
  380.3 56.7 %collective-permute-start.34 = (bf16[4,64,1024]{2,1,0:T(8,128)(2,1)}, bf16[4,64,1024]{2,1,0:T(8,128)(2,1)}, u32[]{:S(2)}, u32[]{:S(2)}) collective-permute-start(bf16[4,64,1024]{2,1,0:T(8,128)(2,1)} %get-tuple-element.127.refs_0_.refs_1_), channel_id=1, source_target_pairs={{0,16},{1,17},{2,18},{3,19},{4,20},{5,21},{6,22},{7,23},{8,24},{9,... | collective-permute-start | bytes 1572872 | tf_op jit(solution)/shard_map/ppermute | solution.py:69
  390.8 8.9 %collective-permute-start.28 = (f32[2,2,4,384]{3,2,1,0:T(4,128)S(1)}, f32[2,2,4,384]{3,2,1,0:T(4,128)S(1)}, u32[]{:S(2)}, u32[]{:S(2)}) collective-permute-start(f32[2,2,4,384]{3,2,1,0:T(4,128)S(1)} %dynamic-slice_bitcast_fusion.7), channel_id=1, source_target_pairs={{0,4},{1,5},{2,6},{3,7},{4,0},{5,1},{6,2},{7,3},{8,12},{9,13},{10,... | collective-permute-start | bytes 73736 | tf_op jit(solution)/shard_map/ppermute | solution.py:69
  399.7 7.1 %collective-permute-start.29 = (f32[2,4,384]{2,1,0:T(4,128)S(1)}, f32[2,4,384]{2,1,0:T(4,128)S(1)}, u32[]{:S(2)}, u32[]{:S(2)}) collective-permute-start(f32[2,4,384]{2,1,0:T(4,128)S(1)} %dynamic-slice_bitcast_fusion.8), channel_id=1, source_target_pairs={{0,8},{1,9},{2,10},{3,11},{4,12},{5,13},{6,14},{7,15},{8,0},{9,1},... | collective-permute-start | bytes 36872 | tf_op jit(solution)/shard_map/ppermute | solution.py:69
  403.0 19.3 %collective-permute-start.35 = (bf16[2,32,2048]{2,1,0:T(8,128)(2,1)S(1)}, bf16[2,32,2048]{2,1,0:T(8,128)(2,1)S(1)}, u32[]{:S(2)}, u32[]{:S(2)}) collective-permute-start(bf16[2,32,2048]{2,1,0:T(8,128)(2,1)S(1)} %get-tuple-element.158), channel_id=1, source_target_pairs={{0,1},{1,2},{2,3},{3,0},{4,5},{5,6},{6,7},{7,4},{8,9},{9,10},{10,1... | collective-permute-start | bytes 786440 | tf_op jit(solution)/shard_map/ppermute | solution.py:69
  403.0 20.0 %collective-permute-start.37 = (bf16[2,32,2048]{2,1,0:T(8,128)(2,1)S(1)}, bf16[2,32,2048]{2,1,0:T(8,128)(2,1)S(1)}, u32[]{:S(2)}, u32[]{:S(2)}) collective-permute-start(bf16[2,32,2048]{2,1,0:T(8,128)(2,1)S(1)} %get-tuple-element.159), channel_id=1, source_target_pairs={{0,3},{1,0},{2,1},{3,2},{4,7},{5,4},{6,5},{7,6},{8,11},{9,8},{10,9... | collective-permute-start | bytes 786440 | tf_op jit(solution)/shard_map/ppermute | solution.py:69
  406.8 23.7 %collective-permute-start.36 = (bf16[2,32,2048]{2,1,0:T(8,128)(2,1)S(1)}, bf16[2,32,2048]{2,1,0:T(8,128)(2,1)S(1)}, u32[]{:S(2)}, u32[]{:S(2)}) collective-permute-start(bf16[2,32,2048]{2,1,0:T(8,128)(2,1)S(1)} %get-tuple-element.160), channel_id=1, source_target_pairs={{0,2},{1,3},{2,0},{3,1},{4,6},{5,7},{6,4},{7,5},{8,10},{9,11},{10,... | collective-permute-start | bytes 786440 | tf_op jit(solution)/shard_map/ppermute | solution.py:69
  406.9 14.0 %collective-permute-start.30 = (f32[4,384]{1,0:T(4,128)S(1)}, f32[4,384]{1,0:T(4,128)S(1)}, u32[]{:S(2)}, u32[]{:S(2)}) collective-permute-start(f32[4,384]{1,0:T(4,128)S(1)} %fusion.40), channel_id=1, source_target_pairs={{0,16},{1,17},{2,18},{3,19},{4,20},{5,21},{6,22},{7,23},{8,24},{9,... | collective-permute-start | bytes 18440 | tf_op jit(solution)/shard_map/ppermute | solution.py:69
  420.8 16.0 %collective-permute-start.38 = (bf16[4,64,1024]{2,1,0:T(8,128)(2,1)S(1)}, bf16[4,64,1024]{2,1,0:T(8,128)(2,1)S(1)}, u32[]{:S(2)}, u32[]{:S(2)}) collective-permute-start(bf16[4,64,1024]{2,1,0:T(8,128)(2,1)S(1)} %copy-done.13), channel_id=1, source_target_pairs={{0,8},{1,9},{2,10},{3,11},{4,12},{5,13},{6,14},{7,15},{8,0},{9,1},... | collective-permute-start | bytes 1572872 | tf_op jit(solution)/shard_map/ppermute | solution.py:69
  422.4 9.3 %collective-permute-start.31 = (f32[384]{0:T(512)S(1)}, f32[384]{0:T(512)S(1)}, u32[]{:S(2)}, u32[]{:S(2)}) collective-permute-start(f32[384]{0:T(512)S(1)} %get-tuple-element.146), channel_id=1, source_target_pairs={{0,1},{1,2},{2,3},{3,0},{4,5},{5,6},{6,7},{7,4},{8,9},{9,10},{10,1... | collective-permute-start | bytes 4616 | tf_op jit(solution)/shard_map/ppermute | solution.py:69
  423.0 8.8 %collective-permute-start.33 = (f32[384]{0:T(512)S(1)}, f32[384]{0:T(512)S(1)}, u32[]{:S(2)}, u32[]{:S(2)}) collective-permute-start(f32[384]{0:T(512)S(1)} %get-tuple-element.147), channel_id=1, source_target_pairs={{0,3},{1,0},{2,1},{3,2},{4,7},{5,4},{6,5},{7,6},{8,11},{9,8},{10,9... | collective-permute-start | bytes 4616 | tf_op jit(solution)/shard_map/ppermute | solution.py:69
  430.5 4.5 collective-permute-start.32
  431.6 36.6 %collective-permute-start.26 = (bf16[512,1024]{1,0:T(8,128)(2,1)S(1)}, bf16[512,1024]{1,0:T(8,128)(2,1)}, u32[]{:S(2)}, u32[]{:S(2)}) collective-permute-start(bf16[512,1024]{1,0:T(8,128)(2,1)S(1)} %shard_map.304), channel_id=1, source_target_pairs={{0,4},{1,5},{2,6},{3,7},{4,0},{5,1},{6,2},{7,3},{8,12},{9,13},{10,... | collective-permute-start | bytes 3145736 | tf_op jit(solution)/shard_map/ppermute | solution.py:69
  431.8 5.0 %collective-permute-start.42 = (f32[32,2048]{1,0:T(8,128)S(1)}, f32[32,2048]{1,0:T(8,128)S(1)}, u32[]{:S(2)}, u32[]{:S(2)}) collective-permute-start(f32[32,2048]{1,0:T(8,128)S(1)} %dynamic-slice_bitcast_fusion), channel_id=1, source_target_pairs={{0,4},{1,5},{2,6},{3,7},{4,0},{5,1},{6,2},{7,3},{8,12},{9,13},{10,... | collective-permute-start | bytes 786440 | tf_op jit(solution)/shard_map/ppermute | solution.py:69
  438.6 11.2 %collective-permute-start.39 = (bf16[4,32,1024]{2,1,0:T(8,128)(2,1)S(1)}, bf16[4,32,1024]{2,1,0:T(8,128)(2,1)S(1)}, u32[]{:S(2)}, u32[]{:S(2)}) collective-permute-start(bf16[4,32,1024]{2,1,0:T(8,128)(2,1)S(1)} %get-tuple-element.155), channel_id=1, source_target_pairs={{0,1},{1,2},{2,3},{3,0},{4,5},{5,6},{6,7},{7,4},{8,9},{9,10},{10,1... | collective-permute-start | bytes 786440 | tf_op jit(solution)/shard_map/ppermute | solution.py:69
  438.6 20.4 %collective-permute-start.40 = (bf16[4,32,1024]{2,1,0:T(8,128)(2,1)S(1)}, bf16[4,32,1024]{2,1,0:T(8,128)(2,1)S(1)}, u32[]{:S(2)}, u32[]{:S(2)}) collective-permute-start(bf16[4,32,1024]{2,1,0:T(8,128)(2,1)S(1)} %get-tuple-element.156), channel_id=1, source_target_pairs={{0,2},{1,3},{2,0},{3,1},{4,6},{5,7},{6,4},{7,5},{8,10},{9,11},{10,... | collective-permute-start | bytes 786440 | tf_op jit(solution)/shard_map/ppermute | solution.py:69
  439.4 19.6 %collective-permute-start.41 = (bf16[4,32,1024]{2,1,0:T(8,128)(2,1)S(1)}, bf16[4,32,1024]{2,1,0:T(8,128)(2,1)S(1)}, u32[]{:S(2)}, u32[]{:S(2)}) collective-permute-start(bf16[4,32,1024]{2,1,0:T(8,128)(2,1)S(1)} %get-tuple-element.157), channel_id=1, source_target_pairs={{0,3},{1,0},{2,1},{3,2},{4,7},{5,4},{6,5},{7,6},{8,11},{9,8},{10,9... | collective-permute-start | bytes 786440 | tf_op jit(solution)/shard_map/ppermute | solution.py:69
  (80 other events, 547.1 us)
Sparse Core Ops, SparseCore 0:
  34.9 115.5 all-gather.5
  153.9 72.7 all-gather.3
  229.6 51.2 reduce-scatter.2
  284.1 52.7 reduce-scatter.4

commit v3 on v2

--- a/solution.py
+++ b/solution.py
@@ -22,6 +22,7 @@
 
 MASKED = -1e30
 TILE = 256
+WIDE = 512
 LANES = 128
 SLOPE_LANE = NDOCS + 1
 ROW_LANE = SLOPE_LANE + 6
@@ -146,15 +147,16 @@
 
 
 def joined_kernel(places, *refs):
-    *pieces, whole, riders, sems = refs
+    *pieces, query, key, value, riders, sems = refs
+    width = query.shape[-1]
     moves = []
     for piece in pieces:
         for near in range(piece.shape[0]):
             for step in range(piece.shape[1]):
                 at = places[len(moves) // 4]
-                for kind in range(3):
-                    moves.append((piece.at[near, step, kind, :, pl.ds(0, whole.shape[-1])], whole.at[kind, at]))
-                moves.append((piece.at[near, step, 0, :, pl.ds(whole.shape[-1], LANES)], riders.at[at]))
+                for kind, whole in enumerate((query, key, value)):
+                    moves.append((piece.at[near, step, kind, :, pl.ds(0, width)], whole.at[at]))
+                moves.append((piece.at[near, step, 0, :, pl.ds(width, LANES)], riders.at[at]))
     copy_blocks(moves, sems)
 
 
@@ -166,14 +168,14 @@
         for which, piece in ((grid.here[CORE], block), (1 - grid.here[CORE], grid.shift(block, CORE))):
             pieces.append(piece)
             places += [(chip * 2 + which) * grid.size[Z] + z for near in entries for chip, z in near]
-    whole, riders = assemble(
+    *mats, riders = assemble(
         joined_kernel,
         jnp.stack(places).astype(jnp.int32),
         pieces,
-        [(3, grid.count, rows, width), (grid.count, rows, LANES)],
+        [(grid.count, rows, width)] * 3 + [(grid.count, rows, LANES)],
         4 * len(places),
     )
-    return whole.reshape(3, -1, width), riders
+    return *(mat.reshape(-1, width) for mat in mats), riders
 
 
 def up_kernel(places, lines, up, sems):
@@ -208,16 +210,32 @@
     return total
 
 
-def direct_reduce(grid, terms, axis, kind=f32):
+def sum_kernel(count, *refs):
+    total = refs[0][...].astype(f32)
+    for ref in refs[1:count]:
+        total += ref[...].astype(f32)
+    refs[-1][...] = total
+
+
+def sum_after(arrays, *earlier):
+    held = pl.BlockSpec(memory_space=pltpu.VMEM)
+    return pl.pallas_call(
+        functools.partial(sum_kernel, len(arrays)),
+        in_specs=[held] * len(arrays) + [pl.BlockSpec(memory_space=pl.ANY)] * len(earlier),
+        out_specs=held,
+        out_shape=jax.ShapeDtypeStruct(arrays[0].shape, f32),
+        compiler_params=pltpu.CompilerParams(vmem_limit_bytes=2**23),
+        cost_estimate=SHORT,
+    )(*arrays, *earlier)
+
+
+def direct_reduce(grid, terms, axis, earlier=()):
     count, place = grid.size[axis], grid.here[axis]
 
     def term(step):
         return lax.dynamic_index_in_dim(terms, (place + step) % count, 0, keepdims=False)
 
-    total = term(0).astype(f32)
-    for step in range(1, count):
-        total = total + grid.shift(term(step), axis, step).astype(f32)
-    return total.astype(kind)
+    return sum_after([term(0)] + [grid.shift(term(step), axis, step) for step in range(1, count)], *earlier)
 
 
 def down_kernel(left, right, out, total):
@@ -246,20 +264,20 @@
 
 
 def up_kernel_terms(own, other, right, *refs):
-    refs[-1][...] = dot_tn(jnp.concatenate([own[...], other[...]], axis=0), right[...]).astype(bf16)
+    rows = own.shape[0]
+    refs[-1][...] = (dot_tn(own[...], right[:rows]) + dot_tn(other[...], right[rows:])).astype(bf16)
 
 
 def up_terms(own, other, pre_change, earlier=()):
     rows, width = own.shape
     tokens, units = pre_change.shape
-    wide = units // 2
-    left = pl.BlockSpec((rows, TILE), lambda j, i: (0, i))
+    left = pl.BlockSpec((rows, width), lambda i: (0, 0))
     return pl.pallas_call(
         up_kernel_terms,
-        grid=(2, width // TILE),
-        in_specs=[left, left, pl.BlockSpec((tokens, wide), lambda j, i: (0, j))]
+        grid=(units // WIDE,),
+        in_specs=[left, left, pl.BlockSpec((tokens, WIDE), lambda i: (0, i))]
         + [pl.BlockSpec(memory_space=pl.ANY)] * len(earlier),
-        out_specs=pl.BlockSpec((TILE, wide), lambda j, i: (i, j)),
+        out_specs=pl.BlockSpec((width, WIDE), lambda i: (0, i)),
         out_shape=jax.ShapeDtypeStruct((width, units), bf16),
         compiler_params=pltpu.CompilerParams(vmem_limit_bytes=VMEM_LIMIT),
         cost_estimate=SHORT,
@@ -297,13 +315,13 @@
     depth, wide = left.shape[1], right.shape[0]
     return pl.pallas_call(
         product_kernel,
-        grid=(wide // TILE,),
+        grid=(wide // WIDE,),
         in_specs=[
             pl.BlockSpec((rows, depth), lambda i: (row_block, 0)),
-            pl.BlockSpec((TILE, depth), lambda i: (i, 0)),
+            pl.BlockSpec((WIDE, depth), lambda i: (i, 0)),
         ]
         + [pl.BlockSpec(memory_space=pl.ANY)] * len(earlier),
-        out_specs=pl.BlockSpec((rows, TILE), lambda i: (0, i)),
+        out_specs=pl.BlockSpec((rows, WIDE), lambda i: (0, i)),
         out_shape=jax.ShapeDtypeStruct((rows, wide), kind),
         compiler_params=pltpu.CompilerParams(vmem_limit_bytes=VMEM_LIMIT),
         cost_estimate=SHORT,
@@ -493,7 +511,11 @@
             return lax.dynamic_index_in_dim(terms, (grid.here[axis] - step) % grid.size[axis], dim, keepdims=False)
 
         terms = ring_reduce(grid, term, axis, f32)
-    return direct_reduce(grid, terms, Z, f32)
+    total = lax.dynamic_index_in_dim(terms, grid.here[Z], 0, keepdims=False)
+    for step in range(1, grid.size[Z]):
+        term = lax.dynamic_index_in_dim(terms, (grid.here[Z] + step) % grid.size[Z], 0, keepdims=False)
+        total = total + grid.shift(term, Z, step)
+    return total
 
 
 def thirds(values):
@@ -715,8 +737,8 @@
                 sides[0, part * rows : (part + 1) * rows, to] = jnp.where(first, low, high)
                 sides[1, part * rows : (part + 1) * rows, to] = jnp.where(first, high, low)
 
-    kept = up_kept[...].reshape(width // 2, TILE)
-    given = up_given[...].reshape(width // 2, TILE)
+    kept = up_kept[...].reshape(width // 2, WIDE)
+    given = up_given[...].reshape(width // 2, WIDE)
     for start in range(0, 2 * rows, TILE):
         product = dot_nn(sides[0, start : start + TILE], kept) + dot_nn(sides[1, start : start + TILE], given)
         value, rise = gelu_parts(product + bias[...])
@@ -728,19 +750,19 @@
     rows, depth = own.shape
     count, _, height, width = lines.shape
     units = 2 * width
-    steps = width // TILE
-    columns = pl.BlockSpec((2 * rows, TILE), lambda i, at: (0, i))
+    steps = width // WIDE
+    columns = pl.BlockSpec((2 * rows, WIDE), lambda i, at: (0, i))
     whole = pl.BlockSpec((rows, depth), lambda i, at: (0, 0))
 
     def block(side):
-        return pl.BlockSpec((count, 1, height, TILE), lambda i, at: (0, 2 * side + i // steps, 0, i % steps))
+        return pl.BlockSpec((count, 1, height, WIDE), lambda i, at: (0, 2 * side + i // steps, 0, i % steps))
 
     return pl.pallas_call(
         functools.partial(hidden_kernel, chips),
         grid_spec=pltpu.PrefetchScalarGridSpec(
             num_scalar_prefetch=1,
-            grid=(units // TILE,),
-            in_specs=[whole, whole, block(0), block(1), pl.BlockSpec((1, TILE), lambda i, at: (0, i))],
+            grid=(units // WIDE,),
+            in_specs=[whole, whole, block(0), block(1), pl.BlockSpec((1, WIDE), lambda i, at: (0, i))],
             out_specs=[columns, columns],
             scratch_shapes=[pltpu.VMEM((2, 2 * rows, depth // 2), bf16)],
         ),
@@ -760,17 +782,17 @@
 def hidden_back(change, down, slope, earlier=()):
     tokens, depth = change.shape
     units = down.shape[0]
-    columns = pl.BlockSpec((tokens, TILE), lambda i: (0, i))
+    columns = pl.BlockSpec((tokens, WIDE), lambda i: (0, i))
     return pl.pallas_call(
         pre_change_kernel,
-        grid=(units // TILE,),
+        grid=(units // WIDE,),
         in_specs=[
             pl.BlockSpec((tokens, depth), lambda i: (0, 0)),
-            pl.BlockSpec((TILE, depth), lambda i: (i, 0)),
+            pl.BlockSpec((WIDE, depth), lambda i: (i, 0)),
             columns,
         ]
         + [pl.BlockSpec(memory_space=pl.ANY)] * len(earlier),
-        out_specs=[columns, pl.BlockSpec((1, TILE), lambda i: (0, i))],
+        out_specs=[columns, pl.BlockSpec((1, WIDE), lambda i: (0, i))],
         out_shape=[jax.ShapeDtypeStruct((tokens, units), bf16), jax.ShapeDtypeStruct((1, units), f32)],
         compiler_params=pltpu.CompilerParams(vmem_limit_bytes=VMEM_LIMIT),
         cost_estimate=SHORT,
@@ -803,20 +825,20 @@
     ext_rows = chunks * rows
     fixed = pl.BlockSpec((rows, width), lambda i: (0, 0))
     row = pl.BlockSpec((1, width), lambda i: (0, 0))
-    placed = pl.BlockSpec((rows, TILE), lambda i: (chunk, i))
+    placed = pl.BlockSpec((rows, WIDE), lambda i: (chunk, i))
     out_specs = [pl.BlockSpec((rows, width), lambda i: (chunk, 0)), pl.BlockSpec((rows, LANES), lambda i: (0, 0)), placed, placed]
     out_shape = [jax.ShapeDtypeStruct((ext_rows, width), bf16), jax.ShapeDtypeStruct((rows, LANES), f32)]
     out_shape += [jax.ShapeDtypeStruct((ext_rows, width), bf16)] * 2
     if kinds == 3:
-        out_specs.append(pl.BlockSpec((rows, TILE), lambda i: (0, i)))
+        out_specs.append(pl.BlockSpec((rows, WIDE), lambda i: (0, i)))
         out_shape.append(jax.ShapeDtypeStruct((rows, width), bf16))
     aliases = {3 + 2 * kinds + i: place for i, place in enumerate((0, 2, 3)[: len(others)])}
     return pl.pallas_call(
         functools.partial(projection_kernel, kinds, len(others)),
-        grid=(width // TILE,),
+        grid=(width // WIDE,),
         in_specs=[fixed, row, row]
-        + [pl.BlockSpec((width, TILE), lambda i: (0, i))] * kinds
-        + [pl.BlockSpec((1, TILE), lambda i: (0, i))] * kinds
+        + [pl.BlockSpec((width, WIDE), lambda i: (0, i))] * kinds
+        + [pl.BlockSpec((1, WIDE), lambda i: (0, i))] * kinds
         + [pl.BlockSpec(memory_space=pl.ANY)] * len(others),
         out_specs=out_specs,
         out_shape=out_shape,
@@ -874,9 +896,31 @@
     )(riders)
 
 
-def from_kinds(columns):
-    rows = columns.shape[0]
-    return columns.reshape(rows, 3, HEADS, HEAD_DIM).swapaxes(1, 2).reshape(rows, 3 * HEADS * HEAD_DIM)
+def finish_kernel(count, *refs):
+    terms, (joined, dense) = refs[:count], refs[-2:]
+    total = terms[0][...].astype(f32)
+    for term in terms[1:]:
+        total += term[...].astype(f32)
+    dense[...] = total[3]
+    for first in range(0, 3 * HEADS, 2):
+        halves = []
+        for at in (first, first + 1):
+            start = at // 3 * HEAD_DIM
+            halves.append(total[at % 3, :, start : start + HEAD_DIM])
+        joined[:, first * HEAD_DIM : (first + 2) * HEAD_DIM] = jnp.concatenate(halves, axis=1)
+
+
+def finish_joined(own, arrived, earlier=()):
+    _, rows, width = own.shape
+    held = pl.BlockSpec(memory_space=pltpu.VMEM)
+    return pl.pallas_call(
+        functools.partial(finish_kernel, 1 + len(arrived)),
+        in_specs=[held] * (1 + len(arrived)) + [pl.BlockSpec(memory_space=pl.ANY)] * len(earlier),
+        out_specs=[held, held],
+        out_shape=[jax.ShapeDtypeStruct((rows, 3 * width), f32), jax.ShapeDtypeStruct((rows, width), f32)],
+        compiler_params=pltpu.CompilerParams(vmem_limit_bytes=2**23),
+        cost_estimate=SHORT,
+    )(own, *arrived, *earlier)
 
 
 def on_device(
@@ -917,7 +961,7 @@
     vectors = (first_gain, first_shift, joined_bias, dense_bias, second_gain, second_shift, up_bias, down_bias)
     counts = [v.shape[0] for v in vectors]
     joined_line = direct_gather(grid, pack_joined(joined_weight, vectors), Z)
-    (query_mat, key_mat, value_mat), riders = gather_joined(grid, joined_line)
+    query_mat, key_mat, value_mat, riders = gather_joined(grid, joined_line)
     gain_one, shift_one, _, dense_vec, gain_two, shift_two, up_vec, down_vec, query_vec, value_vec = unpack_vectors(
         riders, counts
     )
@@ -1024,15 +1068,21 @@
         joined_near.append(total)
     nears = [*joined_near[0], *joined_near[1]]
     up_rows_both = after(up_plane, *nears).reshape(2, nz, up_rows, ff_core).swapaxes(0, 1)
-    up_sum = direct_reduce(grid, up_rows_both, Z)
+    returned = grid.to_earlier(returned)
+    branch_given = product_nn(hidden, down_mat, bf16, 1, tok_rows, nears)
+    branch_kept = product_nn(hidden, down_mat, f32, 0, tok_rows, (branch_given,))
+    joined_far = [far_sums(part, joined_near[part], returned, branch_kept) for part in range(2)]
+    both = [half.reshape(4, nz // 2, -1, width) for half in joined_far]
+    both = jnp.concatenate(both, axis=1)
+
+    def line_term(step):
+        return lax.dynamic_index_in_dim(both, (z + step) % nz, 1, keepdims=False)
+
+    arrived = [grid.shift(line_term(step), Z, step) for step in range(1, nz)]
+    joined_grad, dense_grad = finish_joined(line_term(0), arrived)
+    up_sum = direct_reduce(grid, up_rows_both, Z, arrived)
     up_mine = lax.dynamic_index_in_dim(up_sum, core, 0, keepdims=False)
     up_other = grid.shift(lax.dynamic_index_in_dim(up_sum, 1 - core, 0, keepdims=False), CORE)
-    returned = grid.to_earlier(returned)
-    joined_far = [far_sums(part, joined_near[part], returned, up_sum) for part in range(2)]
-    both = [half.reshape(4, nz // 2, -1, width) for half in joined_far]
-    owned_rows = direct_reduce(grid, jnp.concatenate(both, axis=1).swapaxes(0, 1), Z)
-    dense_grad = owned_rows[3]
-    joined_grad = jnp.concatenate(list(owned_rows[:3]), axis=1)
     returned = returned.astype(f32)
 
     def interleave(mine, other):
@@ -1042,8 +1092,7 @@
         return jnp.concatenate([side[:, cut] for cut in cuts for side in (first, second)], axis=1)
 
     up_grad = interleave(up_mine, up_other)
-    branch_given = product_nn(hidden, down_mat, bf16, 1, tok_rows, nears)
-    branch_two = product_nn(hidden, down_mat, f32, 0, tok_rows, nears) + grid.shift(branch_given, CORE).astype(f32)
+    branch_two = branch_kept + grid.shift(branch_given, CORE).astype(f32)
     layer_output = jnp.where(live_rows, middle + (branch_two + down_vec), 0.0).astype(bf16)
     gain_one_grad, shift_one_grad = (sum(total).reshape(-1) for total in zip(*chunk_sums))
     joined_vec_grad = jnp.stack(
@@ -1071,7 +1120,7 @@
         input_grad,
         owned[0],
         owned[1],
-        from_kinds(joined_grad),
+        joined_grad,
         owned[2],
         dense_grad,
         owned[3],

time: 486 us -> 466 us (0.959)
  starting transfers between devices: 59 us -> 69.8 us
  local copies, waits for them, and re-layouts: 49 us -> 40.4 us
  other arithmetic: 31 us -> 23.5 us
  Pallas kernels: 210 us -> 205 us
  waiting for transfers between devices: 111 us -> 106 us
    ppermute x39, waiting for transfers between devices: 82.5 us -> 43 us  [shift(): lax.ppermute(block, ALL, list(zip(places.ravel().tolist(), ahead.ravel()....]
    all_gather x1, waiting for transfers between devices: 19.4 us -> 36.3 us  [on_device(): lax.all_gather(after(down_weight, *joined_line[1:]), lines, axis=0, tiled...]
    ppermute x2, waiting for transfers between devices: 2.96 us -> 17.7 us  [to_later(): return lax.ppermute(block, ALL, [(i, i + 1) for i in range(self.count - 1)])]
    ppermute x39, starting transfers between devices: 46.8 us -> 58.3 us  [shift(): lax.ppermute(block, ALL, list(zip(places.ravel().tolist(), ahead.ravel()....]
    another operation x2 -> x1, local copies, waits for them, and re-layouts: 5.96 us -> 0.09 us  [the longest x1 5.88 us: on_device(): (query_mat, key_mat, value_mat), riders = gather_joined(grid, joined_line)]
    pallas_call x3 -> x6, Pallas kernels: 26.5 us -> 24.8 us  [the longest x1 8.74 us: hidden_back(): pl.pallas_call(pre_change_kernel, grid=(units // WIDE,), in_specs=[pl.Blo...]
  transfers between devices with their start and end apart: 47 -> 47, of which waited for: 18 -> 18; matrix products, arithmetic and copies ran while one was open for 11% -> 7% of each run, Pallas kernels for 44% -> 44%
where the time goes in v3:
time: 466 us; the launch traced here: 462 us
  Pallas kernels  205 us (44%)
  waiting for transfers between devices  106 us (23%)
  starting transfers between devices  69.8 us (15%)
  local copies, waits for them, and re-layouts  40.4 us (9%)
  other arithmetic  23.5 us (5%)
  between operations  15.9 us (3%)
    ppermute x39, starting transfers between devices, shift(): lax.ppermute(block, ALL, list(zip(places.ravel().tolist(), ahead.ravel()....  58.3 us
    ppermute x39, waiting for transfers between devices, shift(): lax.ppermute(block, ALL, list(zip(places.ravel().tolist(), ahead.ravel()....  43 us
    all_gather x1, waiting for transfers between devices, on_device(): lax.all_gather(after(down_weight, *joined_line[1:]), lines, axis=0, tiled...  36.3 us
    pallas_call x2, Pallas kernels, attend_back(): pl.pallas_call(functools.partial(attend_back_kernel, first_pair=first_pai...  34.1 us
    unnamed x175, local copies, waits for them, and re-layouts  31.8 us
    pallas_call x1, Pallas kernels, attend(): pl.pallas_call(attend_kernel, grid=(steps,), in_specs=[pl.BlockSpec((tok_...  21.1 us
    pallas_call x3, Pallas kernels, chunk_back(): pl.pallas_call(functools.partial(chunk_kernel, len(pairs), arrived is not...  20.5 us
    pallas_call x3, Pallas kernels, project(): pl.pallas_call(functools.partial(projection_kernel, kinds, len(others)),...  19.4 us
  transfers between devices with their start and end apart: 47, of which 18 were waited for; matrix products, arithmetic and copies ran while one was open for 7% of the time, Pallas kernels for 44%

profile of v3, /device:TPU:0, one launch (start us, length us, event | category | flops | bytes accessed | tf_op | source)
XLA Modules:
  0.0 461.6 jit_solution(18341094553505421145)
XLA Ops:
  10.7 5.0 %collective-permute-start.6 = (bf16[3,32,1152]{2,1,0:T(8,128)(2,1)}, bf16[3,32,1152]{2,1,0:T(8,128)(2,1)S(1)}, u32[]{:S(2)}, u32[]{:S(2)}) collective-permute-start(bf16[3,32,1152]{2,1,0:T(8,128)(2,1)} %shard_map.272), channel_id=1, source_target_pairs={{0,3},{1,0},{2,1},{3,2},{4,7},{5,4},{6,5},{7,6},{8,11},{9,8},{10,9... | collective-permute-start | bytes 663560 | tf_op jit(solution)/shard_map/ppermute | solution.py:70
  21.9 12.8 %collective-permute-done.5.refs_2_ = bf16[3,32,1152]{2,1,0:T(8,128)(2,1)S(1)} collective-permute-done((bf16[3,32,1152]{2,1,0:T(8,128)(2,1)}, bf16[3,32,1152]{2,1,0:T(8,128)(2,1)S(1)}, u32[]{:S(2)}, u32[]{:S(2)}) %collective-permute-start.5) | collective-permute-done | bytes 221216 | tf_op jit(solution)/shard_map/ppermute | solution.py:70
  40.8 3.9 collective-permute-start.11
  44.7 5.0 %collective-permute-done.7 = bf16[2,3,32,1152]{3,2,1,0:T(8,128)(2,1)S(1)} collective-permute-done((bf16[2,3,32,1152]{3,2,1,0:T(8,128)(2,1)S(1)}, bf16[2,3,32,1152]{3,2,1,0:T(8,128)(2,1)S(1)}, u32[]{:S(2)}, u32[]{:S(2)}) %collective-permute-start.7) | collective-permute-done | bytes 442400 | tf_op jit(solution)/shard_map/ppermute | solution.py:70
  51.6 3.3 collective-permute-done.1
  56.0 17.7 %collective-permute-done.11.tokens.refs_4_ = bf16[512,1024]{1,0:T(8,128)(2,1)} collective-permute-done((bf16[512,1024]{1,0:T(8,128)(2,1)S(1)}, bf16[512,1024]{1,0:T(8,128)(2,1)}, u32[]{:S(2)}, u32[]{:S(2)}) %collective-permute-start.11) | collective-permute-done | bytes 1048608 | tf_op jit(solution)/shard_map/ppermute | solution.py:73
  73.8 4.7 %collective-permute-start.12 = (bf16[512,1024]{1,0:T(8,128)(2,1)}, bf16[512,1024]{1,0:T(8,128)(2,1)S(1)}, u32[]{:S(2)}, u32[]{:S(2)}) collective-permute-start(bf16[512,1024]{1,0:T(8,128)(2,1)} %collective-permute-done.11.tokens.refs_4_), channel_id=1, source_target_pairs={{0,1},{1,2},{2,3},{3,4},{4,5},{5,6},{6,7},{7,8},{8,9},{9,10},{10,1... | collective-permute-start | bytes 3145736 | tf_op jit(solution)/shard_map/ppermute | solution.py:73
  79.6 3.5 collective-permute-done.9.refs_6_
  85.1 2.4 select_convert_fusion.1.key_side
  90.6 7.4 %shard_map.273 = (bf16[32,32,1024]{2,1,0:T(8,128)(2,1)}, bf16[32,32,1024]{2,1,0:T(8,128)(2,1)}, bf16[32,32,1024]{2,1,0:T(8,128)(2,1)}, bf16[32,32,128]{2,1,0:T(8,128)(2,1)S(1)}) custom-call(s32[32]{0:T(128)S(1)} %stack.305.places, bf16[2,2,3,32,1152]{4,3,2,1,0:T(8,128)(2,1)S(1)} %pad_maximum_fusion.2.refs_0_, ...), custom_call_target="tpu_custom_call" | custom-call | flops 1 | bytes 1 | tf_op jit(solution)/shard_map/pallas_call | solution.py:138
  103.2 7.1 %shard_map.275 = (bf16[1536,1024]{1,0:T(8,128)(2,1)}, f32[512,128]{1,0:T(8,128)S(1)}, bf16[1536,1024]{1,0:T(8,128)(2,1)}, bf16[1536,1024]{1,0:T(8,128)(2,1)}, bf16[512,1024]{1,0:T(8,128)(2,1)S(1)}) custom-call(bf16[512,1024]{1,0:T(8,128)(2,1)S(1)} %copy-done.2, f32[1,1024]{1,0:T(1,128)S(1)} %copy-done.45, f32[1,1024]{1,0:T(1,128)S(1)} %copy-done.47, ...), custom_call_target="tpu_custom_call" | custom-call | flops 1 | bytes 1 | tf_op jit(solution)/shard_map/pallas_call | solution.py:836
  111.0 6.3 %shard_map.277 = (bf16[1536,1024]{1,0:T(8,128)(2,1)}, f32[512,128]{1,0:T(8,128)S(1)}, bf16[1536,1024]{1,0:T(8,128)(2,1)}, bf16[1536,1024]{1,0:T(8,128)(2,1)}) custom-call(bf16[512,1024]{1,0:T(8,128)(2,1)} %collective-permute-done.11.tokens.refs_4_, f32[1,1024]{1,0:T(1,128)S(1)} %copy-done.46, ...), custom_call_target="tpu_custom_call", output_to_operand_aliasing={{0}: (7, {}), {2}: (8, {}), {3}: (9, {})} | custom-call | flops 1 | bytes 1 | tf_op jit(solution)/shard_map/pallas_call | solution.py:836
  117.3 6.0 %shard_map.278 = (bf16[1536,1024]{1,0:T(8,128)(2,1)}, f32[512,128]{1,0:T(8,128)S(1)}, bf16[1536,1024]{1,0:T(8,128)(2,1)}, bf16[1536,1024]{1,0:T(8,128)(2,1)}) custom-call(bf16[512,1024]{1,0:T(8,128)(2,1)S(1)} %collective-permute-done.12.tokens.refs_4_, f32[1,1024]{1,0:T(1,128)S(1)} %copy-done.46, ...), custom_call_target="tpu_custom_call", output_to_operand_aliasing={{0}: (7, {}), {2}: (8, {}), {3}: (9, {})} | custom-call | flops 1 | bytes 1 | tf_op jit(solution)/shard_map/pallas_call | solution.py:836
  124.0 21.1 %shard_map.280 = (bf16[512,1024]{1,0:T(8,128)(2,1)S(1)}, f32[512,128]{1,0:T(8,128)S(1)}) custom-call(bf16[512,1024]{1,0:T(8,128)(2,1)} %copy-done.9, bf16[1536,1024]{1,0:T(8,128)(2,1)} %get-tuple-element.98.key, bf16[1536,1024]{1,0:T(8,128)(2,1)} %get-tuple-element.99.value, bf16[512,128]{1,0:T(8,128)(2,1)S(1)} %select_convert_fusion.2.query_side, ...), custom_call_target="tpu_custom_call" | custom-call | flops 1 | bytes 1 | tf_op jit(solution)/shard_map/pallas_call | solution.py:593
  145.8 2.9 all-gather.6.cloned.1.call-done
  150.8 2.4 collective-permute-done.15
  158.8 2.3 collective-permute-done.16.other
  161.0 11.6 %shard_map.283 = (bf16[1024,2048]{1,0:T(8,128)(2,1)}, bf16[1024,2048]{1,0:T(8,128)(2,1)}) custom-call(s32[1]{0:T(128)} %bitcast.66.core, bf16[512,1024]{1,0:T(8,128)(2,1)S(1)} %add_convert_fusion.own, bf16[512,1024]{1,0:T(8,128)(2,1)S(1)} %collective-permute-done.16.other, bf16[16,5,32,1024]{3,2,1,0:T(8,128)(2,1)} %bitcast.224, ...), custom_call_target="tpu_custom_call" | custom-call | flops 1 | bytes 1 | tf_op jit(solution)/shard_map/pallas_call | solution.py:760
  172.6 9.6 %shard_map.285 = (bf16[2048,1024]{1,0:T(8,128)(2,1)}, f32[1,1024]{1,0:T(1,128)S(1)}) custom-call(bf16[1024,2048]{1,0:T(8,128)(2,1)} %get-tuple-element.105.left.refs_1_, bf16[1024,1024]{1,0:T(8,128)(2,1)S(1)} %copy-done.4), custom_call_target="tpu_custom_call" | custom-call | flops 1 | bytes 1 | tf_op jit(solution)/shard_map/pallas_call | solution.py:252
  183.1 2.2 copy-done.1
  185.3 5.4 %shard_map.288 = bf16[32,32,2048]{2,1,0:T(8,128)(2,1)} custom-call(s32[32]{0:T(128)S(1)} %shard_map.287.places, bf16[16,5,32,1024]{3,2,1,0:T(8,128)(2,1)} %bitcast.226), custom_call_target="tpu_custom_call" | custom-call | flops 1 | bytes 1 | tf_op jit(solution)/shard_map/pallas_call | solution.py:138
  190.7 36.3 %all-gather.4.cloned.1.call-done.down.right = bf16[2048,1024]{1,0:T(8,128)(2,1)} async-done(((bf16[128,1024]{1,0:T(8,128)(2,1)}), bf16[2048,1024]{1,0:T(8,128)(2,1)}) %all-gather.4.cloned.1.call-update) | async-done | bytes 4194320 | tf_op jit(solution)/shard_map/all_gather | solution.py:974
  226.9 8.7 %shard_map.286 = (bf16[1024,2048]{1,0:T(8,128)(2,1)}, f32[1,2048]{1,0:T(1,128)S(1)}) custom-call(bf16[1024,1024]{1,0:T(8,128)(2,1)S(1)} %copy-done.4, bf16[2048,1024]{1,0:T(8,128)(2,1)} %all-gather.4.cloned.1.call-done.down.right, bf16[1024,2048]{1,0:T(8,128)(2,1)} %get-tuple-element.107.slope, bf16[2048,1024]{1,0:T(8,128)(2,1)} %get-tuple-element.108.refs_0_), custom_call_target="tpu_custom_call" | custom-call | flops 1 | bytes 1 | tf_op jit(solution)/shard_map/pallas_call | solution.py:786
  235.7 5.0 %shard_map.289.refs_0_ = bf16[512,1024]{1,0:T(8,128)(2,1)S(1)} custom-call(bf16[1024,2048]{1,0:T(8,128)(2,1)} %get-tuple-element.109.left.right.pre_change, bf16[1024,2048]{1,0:T(8,128)(2,1)} %bitcast.227), custom_call_target="tpu_custom_call" | custom-call | flops 1 | bytes 1 | tf_op jit(solution)/shard_map/pallas_call | solution.py:316
  240.7 8.0 %shard_map.290.refs_0_ = bf16[1024,2048]{1,0:T(8,128)(2,1)} custom-call(bf16[512,1024]{1,0:T(8,128)(2,1)S(1)} %copy-done.12, bf16[512,1024]{1,0:T(8,128)(2,1)S(1)} %copy-done.22, bf16[1024,2048]{1,0:T(8,128)(2,1)} %get-tuple-element.109.left.right.pre_change, bf16[512,1024]{1,0:T(8,128)(2,1)S(1)} %shard_map.289.refs_0_), custom_call_target="tpu_custom_call" | custom-call | flops 1 | bytes 1 | tf_op jit(solution)/shard_map/pallas_call | solution.py:275
  248.9 2.6 collective-permute-done.17.arrived
  251.5 9.4 %shard_map.291 = (f32[512,1024]{1,0:T(8,128)}, bf16[512,1024]{1,0:T(8,128)(2,1)S(1)}, bf16[512,1024]{1,0:T(8,128)(2,1)S(1)}, f32[1,1024]{1,0:T(1,128)S(1)}, f32[...) custom-call(bf16[1024,2048]{1,0:T(8,128)(2,1)} %get-tuple-element.109.left.right.pre_change, bf16[1024,2048]{1,0:T(8,128)(2,1)} %bitcast.228, ...), custom_call_target="tpu_custom_call" | custom-call | flops 1 | bytes 1 | tf_op jit(solution)/shard_map/pallas_call | solution.py:413
  264.6 16.8 %shard_map.292 = (bf16[512,1024]{1,0:T(8,128)(2,1)S(1)}, bf16[1536,1024]{1,0:T(8,128)(2,1)}, bf16[1536,1024]{1,0:T(8,128)(2,1)}) custom-call(bf16[512,1024]{1,0:T(8,128)(2,1)} %copy-done.9, bf16[1536,1024]{1,0:T(8,128)(2,1)} %get-tuple-element.98.key, bf16[1536,1024]{1,0:T(8,128)(2,1)} %get-tuple-element.99.value, bf16[512,1024]{1,0:T(8,128)(2,1)} %copy-done.16, ...), custom_call_target="tpu_custom_call" | custom-call | flops 1 | bytes 1 | tf_op jit(solution)/shard_map/pallas_call | solution.py:681
  283.7 3.1 collective-permute-start.20
  292.0 17.3 %shard_map.295 = (bf16[512,1024]{1,0:T(8,128)(2,1)S(1)}, bf16[1536,1024]{1,0:T(8,128)(2,1)}, bf16[1536,1024]{1,0:T(8,128)(2,1)}) custom-call(bf16[512,1024]{1,0:T(8,128)(2,1)} %copy-done.9, bf16[1536,1024]{1,0:T(8,128)(2,1)} %get-tuple-element.98.key, ...), custom_call_target="tpu_custom_call", output_to_operand_aliasing={{0}: (9, {}), {1}: (10, {}), {2}: (11, {})} | custom-call | flops 1 | bytes 1 | tf_op jit(solution)/shard_map/pallas_call | solution.py:681
  313.2 14.8 %shard_map.297 = (bf16[4,4,64,1024]{3,2,1,0:T(8,128)(2,1)}, bf16[4,4,64,1024]{3,2,1,0:T(8,128)(2,1)}, bf16[4,4,64,1024]{3,2,1,0:T(8,128)(2,1)}, bf16[4,4,64,1024]{3,2,1,0:T(8,128)(2,1)}) custom-call(s32[4]{0:T(128)S(1)} %pad_add_fusion.blocks, s32[1]{0:T(128)} %bitcast.66.core, bf16[1536,1024]{1,0:T(8,128)(2,1)} %get-tuple-element.106.tokens_ext, ...), custom_call_target="tpu_custom_call" | custom-call | flops 1 | bytes 1 | tf_op jit(solution)/shard_map/pallas_call | solution.py:457
  328.8 6.3 %shard_map.298 = (bf16[512,1024]{1,0:T(8,128)(2,1)}, f32[1,1024]{1,0:T(1,128)S(1)}, f32[1,1024]{1,0:T(1,128)S(1)}) custom-call(bf16[1536,1024]{1,0:T(8,128)(2,1)} %get-tuple-element.116.key.refs_0_, bf16[1536,1024]{1,0:T(8,128)(2,1)} %get-tuple-element.117.value.refs_1_, bf16[1024,1024]{1,0:T(8,128)(2,1)} %bitcast.200, bf16[1024,1024]{1,0:T(8,128)(2,1)} %bitcast.220, ...), custom_call_target="tpu_custom_call" | custom-call | flops 1 | bytes 1 | tf_op jit(solution)/shard_map/pallas_call | solution.py:370
  337.6 5.7 %shard_map.299 = (bf16[2,4,64,1024]{3,2,1,0:T(8,128)(2,1)}, bf16[2,4,64,1024]{3,2,1,0:T(8,128)(2,1)S(1)}, bf16[2,4,64,1024]{3,2,1,0:T(8,128)(2,1)}, bf16[2,4,64,1024]{3,2,1,0:T(8,128)(2,1)}) custom-call(bf16[2,2,4,64,1024]{4,3,2,1,0:T(8,128)(2,1)} %bitcast.235, bf16[2,2,4,64,1024]{4,3,2,1,0:T(8,128)(2,1)} %bitcast.112.arrived_ahead, ...), custom_call_target="tpu_custom_call" | custom-call | flops 1 | bytes 1 | tf_op jit(solution)/shard_map/pallas_call | solution.py:494
  344.3 3.9 collective-permute-start.23
  353.2 7.7 %shard_map.300 = (f32[512,1024]{1,0:T(8,128)}, f32[1,1024]{1,0:T(1,128)S(1)}, f32[1,1024]{1,0:T(1,128)S(1)}) custom-call(bf16[1536,1024]{1,0:T(8,128)(2,1)} %get-tuple-element.116.key.refs_0_, bf16[1536,1024]{1,0:T(8,128)(2,1)} %get-tuple-element.117.value.refs_1_, bf16[512,1024]{1,0:T(8,128)(2,1)S(1)} %get-tuple-element.115.query.refs_2_, ...), custom_call_target="tpu_custom_call" | custom-call | flops 1 | bytes 1 | tf_op jit(solution)/shard_map/pallas_call | solution.py:370
  362.4 6.5 %shard_map.301 = (bf16[512,1024]{1,0:T(8,128)(2,1)}, f32[1,1024]{1,0:T(1,128)S(1)}, f32[1,1024]{1,0:T(1,128)S(1)}) custom-call(bf16[1536,1024]{1,0:T(8,128)(2,1)} %get-tuple-element.116.key.refs_0_, bf16[1536,1024]{1,0:T(8,128)(2,1)} %get-tuple-element.117.value.refs_1_, bf16[1024,1024]{1,0:T(8,128)(2,1)} %bitcast.202, bf16[1024,1024]{1,0:T(8,128)(2,1)} %bitcast.222, ...), custom_call_target="tpu_custom_call" | custom-call | flops 1 | bytes 1 | tf_op jit(solution)/shard_map/pallas_call | solution.py:370
  370.5 2.5 convert_reduce_fusion
  376.8 7.7 %collective-permute-start.34 = (bf16[4,64,1024]{2,1,0:T(8,128)(2,1)}, bf16[4,64,1024]{2,1,0:T(8,128)(2,1)}, u32[]{:S(2)}, u32[]{:S(2)}) collective-permute-start(bf16[4,64,1024]{2,1,0:T(8,128)(2,1)} %get-tuple-element.133.refs_0_.refs_1_), channel_id=1, source_target_pairs={{0,16},{1,17},{2,18},{3,19},{4,20},{5,21},{6,22},{7,23},{8,24},{9,... | collective-permute-start | bytes 1572872 | tf_op jit(solution)/shard_map/ppermute | solution.py:70
  391.9 3.4 collective-permute-done.27.refs_0_
  396.2 4.2 collective-permute-start.29
  400.4 2.9 collective-permute-start.41
  403.2 5.5 %shard_map.304.refs_0_ = bf16[512,1024]{1,0:T(8,128)(2,1)S(1)} custom-call(bf16[1024,2048]{1,0:T(8,128)(2,1)} %get-tuple-element.105.left.refs_1_, bf16[2048,1024]{1,0:T(8,128)(2,1)} %all-gather.4.cloned.1.call-done.down.right, bf16[4,64,1024]{2,1,0:T(8,128)(2,1)} %get-tuple-element.133.refs_0_.refs_1_, ...), custom_call_target="tpu_custom_call" | custom-call | flops 1 | bytes 1 | tf_op jit(solution)/shard_map/pallas_call | solution.py:337
  408.8 5.5 %shard_map.305.refs_1_ = f32[512,1024]{1,0:T(8,128)S(1)} custom-call(bf16[1024,2048]{1,0:T(8,128)(2,1)} %get-tuple-element.105.left.refs_1_, bf16[2048,1024]{1,0:T(8,128)(2,1)} %all-gather.4.cloned.1.call-done.down.right, bf16[512,1024]{1,0:T(8,128)(2,1)S(1)} %shard_map.304.refs_0_), custom_call_target="tpu_custom_call" | custom-call | flops 1 | bytes 1 | tf_op jit(solution)/shard_map/pallas_call | solution.py:337
  419.9 3.3 collective-permute-start.38
  427.7 6.2 %collective-permute-start.31 = (f32[384]{0:T(512)S(1)}, f32[384]{0:T(512)S(1)}, u32[]{:S(2)}, u32[]{:S(2)}) collective-permute-start(f32[384]{0:T(512)S(1)} %get-tuple-element.154), channel_id=1, source_target_pairs={{0,1},{1,2},{2,3},{3,0},{4,5},{5,6},{6,7},{7,4},{8,9},{9,10},{10,1... | collective-permute-start | bytes 4616 | tf_op jit(solution)/shard_map/ppermute | solution.py:70
  433.9 4.9 %collective-permute-done.38.refs_3_.refs_6_ = bf16[4,32,1024]{2,1,0:T(8,128)(2,1)S(1)} collective-permute-done((bf16[4,32,1024]{2,1,0:T(8,128)(2,1)S(1)}, bf16[4,32,1024]{2,1,0:T(8,128)(2,1)S(1)}, u32[]{:S(2)}, u32[]{:S(2)}) %collective-permute-start.38) | collective-permute-done | bytes 262176 | tf_op jit(solution)/shard_map/ppermute | solution.py:70
  438.8 8.3 %collective-permute-start.32 = (f32[384]{0:T(512)S(1)}, f32[384]{0:T(512)S(1)}, u32[]{:S(2)}, u32[]{:S(2)}) collective-permute-start(f32[384]{0:T(512)S(1)} %get-tuple-element.156), channel_id=1, source_target_pairs={{0,2},{1,3},{2,0},{3,1},{4,6},{5,7},{6,4},{7,5},{8,10},{9,11},{10,... | collective-permute-start | bytes 4616 | tf_op jit(solution)/shard_map/ppermute | solution.py:70
  447.1 3.1 collective-permute-done.37.refs_2_.refs_5_
  (352 shorter events, 93.4 us)
Async XLA Ops:
  7.2 141.6 %all-gather.6.cloned.1.call-start = ((), (), s32[]{:S(2)}) async-start(), calls=%async_computation.5 | async-start | bytes 5570560 | tf_op jit(solution)/shard_map/all_gather | solution.py:973
  10.7 11.2 %collective-permute-start.6 = (bf16[3,32,1152]{2,1,0:T(8,128)(2,1)}, bf16[3,32,1152]{2,1,0:T(8,128)(2,1)S(1)}, u32[]{:S(2)}, u32[]{:S(2)}) collective-permute-start(bf16[3,32,1152]{2,1,0:T(8,128)(2,1)} %shard_map.272), channel_id=1, source_target_pairs={{0,3},{1,0},{2,1},{3,2},{4,7},{5,4},{6,5},{7,6},{8,11},{9,8},{10,9... | collective-permute-start | bytes 663560 | tf_op jit(solution)/shard_map/ppermute | solution.py:70
  15.7 19.0 %collective-permute-start.5 = (bf16[3,32,1152]{2,1,0:T(8,128)(2,1)}, bf16[3,32,1152]{2,1,0:T(8,128)(2,1)S(1)}, u32[]{:S(2)}, u32[]{:S(2)}) collective-permute-start(bf16[3,32,1152]{2,1,0:T(8,128)(2,1)} %shard_map.272), channel_id=1, source_target_pairs={{0,2},{1,3},{2,0},{3,1},{4,6},{5,7},{6,4},{7,5},{8,10},{9,11},{10,... | collective-permute-start | bytes 663560 | tf_op jit(solution)/shard_map/ppermute | solution.py:70
  15.7 19.0 %collective-permute-start = (bf16[3,32,1152]{2,1,0:T(8,128)(2,1)}, bf16[3,32,1152]{2,1,0:T(8,128)(2,1)S(1)}, u32[]{:S(2)}, u32[]{:S(2)}) collective-permute-start(bf16[3,32,1152]{2,1,0:T(8,128)(2,1)} %shard_map.272), channel_id=1, source_target_pairs={{0,1},{1,2},{2,3},{3,0},{4,5},{5,6},{6,7},{7,4},{8,9},{9,10},{10,1... | collective-permute-start | bytes 663560 | tf_op jit(solution)/shard_map/ppermute | solution.py:70
  17.7 1.4 collective-permute-start.14
  34.8 192.2 %all-gather.4.cloned.1.call-start = ((), (), s32[]{:S(2)}) async-start(), calls=%async_computation.2 | async-start | bytes 4456448 | tf_op jit(solution)/shard_map/all_gather | solution.py:974
  35.5 245.9 %reduce-scatter.3.cloned.1.call-start = ((), (), s32[]{:S(2)}) async-start(), calls=%async_computation.3 | async-start | bytes 5242880 | tf_op jit(solution)/shard_map/reduce_scatter | solution.py:1020
  36.4 13.4 %collective-permute-start.7 = (bf16[2,3,32,1152]{3,2,1,0:T(8,128)(2,1)S(1)}, bf16[2,3,32,1152]{3,2,1,0:T(8,128)(2,1)S(1)}, u32[]{:S(2)}, u32[]{:S(2)}) collective-permute-start(bf16[2,3,32,1152]{3,2,1,0:T(8,128)(2,1)S(1)} %get-tuple-element.175), channel_id=1, source_target_pairs={{0,16},{1,17},{2,18},{3,19},{4,20},{5,21},{6,22},{7,23},{8,24},{9,... | collective-permute-start | bytes 1327112 | tf_op jit(solution)/shard_map/ppermute | solution.py:70
  38.0 16.8 %collective-permute-start.1 = (bf16[2,3,32,1152]{3,2,1,0:T(8,128)(2,1)S(1)}, bf16[2,3,32,1152]{3,2,1,0:T(8,128)(2,1)S(1)}, u32[]{:S(2)}, u32[]{:S(2)}) collective-permute-start(bf16[2,3,32,1152]{3,2,1,0:T(8,128)(2,1)S(1)} %get-tuple-element.177), channel_id=1, source_target_pairs={{0,8},{1,9},{2,10},{3,11},{4,12},{5,13},{6,14},{7,15},{8,0},{9,1},... | collective-permute-start | bytes 1327112 | tf_op jit(solution)/shard_map/ppermute | solution.py:70
  40.7 38.8 %collective-permute-start.13 = (bf16[512,1024]{1,0:T(8,128)(2,1)}, bf16[512,1024]{1,0:T(8,128)(2,1)}, u32[]{:S(2)}, u32[]{:S(2)}) collective-permute-start(bf16[512,1024]{1,0:T(8,128)(2,1)} %broadcast_select_fusion.out_change), channel_id=1, source_target_pairs={{0,4},{1,5},{2,6},{3,7},{4,0},{5,1},{6,2},{7,3},{8,12},{9,13},{10,... | collective-permute-start | bytes 3145736 | tf_op jit(solution)/shard_map/ppermute | solution.py:70
  40.8 43.4 %copy-start.68 = (f32[8,8,128]{2,1,0:T(8,128)S(1)}, f32[8,8,128]{2,1,0:T(8,128)}, u32[]{:S(2)}) copy-start(f32[8,8,128]{2,1,0:T(8,128)} %constant.347.clone) | copy-start | bytes 98308
  40.8 32.9 %collective-permute-start.11 = (bf16[512,1024]{1,0:T(8,128)(2,1)S(1)}, bf16[512,1024]{1,0:T(8,128)(2,1)}, u32[]{:S(2)}, u32[]{:S(2)}) collective-permute-start(bf16[512,1024]{1,0:T(8,128)(2,1)S(1)} %shard_map.276), channel_id=1, source_target_pairs={{0,1},{1,2},{2,3},{3,4},{4,5},{5,6},{6,7},{7,8},{8,9},{9,10},{10,1... | collective-permute-start | bytes 3145736 | tf_op jit(solution)/shard_map/ppermute | solution.py:73
  50.8 32.3 %collective-permute-start.9 = (bf16[2,2,3,32,1152]{4,3,2,1,0:T(8,128)(2,1)}, bf16[2,2,3,32,1152]{4,3,2,1,0:T(8,128)(2,1)}, u32[]{:S(2)}, u32[]{:S(2)}) collective-permute-start(bf16[2,2,3,32,1152]{4,3,2,1,0:T(8,128)(2,1)} %pad_maximum_fusion.3.refs_4_), channel_id=1, source_target_pairs={{0,8},{1,9},{2,10},{3,11},{4,12},{5,13},{6,14},{7,15},{8,0},{9,1},... | collective-permute-start | bytes 2654216 | tf_op jit(solution)/shard_map/ppermute | solution.py:70
  54.9 28.1 %collective-permute-start.3 = (bf16[2,2,3,32,1152]{4,3,2,1,0:T(8,128)(2,1)S(1)}, bf16[2,2,3,32,1152]{4,3,2,1,0:T(8,128)(2,1)}, u32[]{:S(2)}, u32[]{:S(2)}) collective-permute-start(bf16[2,2,3,32,1152]{4,3,2,1,0:T(8,128)(2,1)S(1)} %pad_maximum_fusion.2.refs_0_), channel_id=1, source_target_pairs={{0,16},{1,17},{2,18},{3,19},{4,20},{5,21},{6,22},{7,23},{8,24},{9,... | collective-permute-start | bytes 2654216 | tf_op jit(solution)/shard_map/ppermute | solution.py:70
  73.8 43.5 %collective-permute-start.12 = (bf16[512,1024]{1,0:T(8,128)(2,1)}, bf16[512,1024]{1,0:T(8,128)(2,1)S(1)}, u32[]{:S(2)}, u32[]{:S(2)}) collective-permute-start(bf16[512,1024]{1,0:T(8,128)(2,1)} %collective-permute-done.11.tokens.refs_4_), channel_id=1, source_target_pairs={{0,1},{1,2},{2,3},{3,4},{4,5},{5,6},{6,7},{7,8},{8,9},{9,10},{10,1... | collective-permute-start | bytes 3145736 | tf_op jit(solution)/shard_map/ppermute | solution.py:73
  79.1 11.5 %collective-permute-start.8 = (bf16[2,2,3,32,1152]{4,3,2,1,0:T(8,128)(2,1)}, bf16[2,2,3,32,1152]{4,3,2,1,0:T(8,128)(2,1)}, u32[]{:S(2)}, u32[]{:S(2)}) collective-permute-start(bf16[2,2,3,32,1152]{4,3,2,1,0:T(8,128)(2,1)} %pad_maximum_fusion.3.refs_4_), channel_id=1, source_target_pairs={{0,4},{1,5},{2,6},{3,7},{4,0},{5,1},{6,2},{7,3},{8,12},{9,13},{10,... | collective-permute-start | bytes 2654216 | tf_op jit(solution)/shard_map/ppermute | solution.py:70
  79.5 11.0 %collective-permute-start.2 = (bf16[2,2,3,32,1152]{4,3,2,1,0:T(8,128)(2,1)S(1)}, bf16[2,2,3,32,1152]{4,3,2,1,0:T(8,128)(2,1)}, u32[]{:S(2)}, u32[]{:S(2)}) collective-permute-start(bf16[2,2,3,32,1152]{4,3,2,1,0:T(8,128)(2,1)S(1)} %pad_maximum_fusion.2.refs_0_), channel_id=1, source_target_pairs={{0,4},{1,5},{2,6},{3,7},{4,0},{5,1},{6,2},{7,3},{8,12},{9,13},{10,... | collective-permute-start | bytes 2654216 | tf_op jit(solution)/shard_map/ppermute | solution.py:70
  83.1 7.5 %collective-permute-start.10 = (bf16[2,2,3,32,1152]{4,3,2,1,0:T(8,128)(2,1)}, bf16[2,2,3,32,1152]{4,3,2,1,0:T(8,128)(2,1)}, u32[]{:S(2)}, u32[]{:S(2)}) collective-permute-start(bf16[2,2,3,32,1152]{4,3,2,1,0:T(8,128)(2,1)} %collective-permute-done.9.refs_6_), channel_id=1, source_target_pairs={{0,4},{1,5},{2,6},{3,7},{4,0},{5,1},{6,2},{7,3},{8,12},{9,13},{10,... | collective-permute-start | bytes 2654216 | tf_op jit(solution)/shard_map/ppermute | solution.py:70
  83.1 7.5 %collective-permute-start.4 = (bf16[2,2,3,32,1152]{4,3,2,1,0:T(8,128)(2,1)}, bf16[2,2,3,32,1152]{4,3,2,1,0:T(8,128)(2,1)}, u32[]{:S(2)}, u32[]{:S(2)}) collective-permute-start(bf16[2,2,3,32,1152]{4,3,2,1,0:T(8,128)(2,1)} %collective-permute-done.3.refs_2_), channel_id=1, source_target_pairs={{0,4},{1,5},{2,6},{3,7},{4,0},{5,1},{6,2},{7,3},{8,12},{9,13},{10,... | collective-permute-start | bytes 2654216 | tf_op jit(solution)/shard_map/ppermute | solution.py:70
  150.1 3.1 collective-permute-start.15
  158.3 2.7 collective-permute-start.16
  182.9 205.4 %reduce-scatter.5.cloned.1.call-start = ((), (), s32[]{:S(2)}) async-start(), calls=%async_computation.4 | async-start | bytes 5242880 | tf_op jit(solution)/shard_map/reduce_scatter | solution.py:1024
  248.8 2.7 collective-permute-start.17
  283.7 25.7 %collective-permute-start.20 = (bf16[128,1024]{1,0:T(8,128)(2,1)}, bf16[128,1024]{1,0:T(8,128)(2,1)}, u32[]{:S(2)}, u32[]{:S(2)}) collective-permute-start(bf16[128,1024]{1,0:T(8,128)(2,1)} %get-tuple-element.168), channel_id=1, source_target_pairs={{0,3},{1,0},{2,1},{3,2},{4,7},{5,4},{6,5},{7,6},{8,11},{9,8},{10,9... | collective-permute-start | bytes 786440 | tf_op jit(solution)/shard_map/ppermute | solution.py:70
  286.8 23.4 %collective-permute-start.19 = (bf16[128,1024]{1,0:T(8,128)(2,1)}, bf16[128,1024]{1,0:T(8,128)(2,1)}, u32[]{:S(2)}, u32[]{:S(2)}) collective-permute-start(bf16[128,1024]{1,0:T(8,128)(2,1)} %get-tuple-element.169), channel_id=1, source_target_pairs={{0,2},{1,3},{2,0},{3,1},{4,6},{5,7},{6,4},{7,5},{8,10},{9,11},{10,... | collective-permute-start | bytes 786440 | tf_op jit(solution)/shard_map/ppermute | solution.py:70
  286.8 23.4 %collective-permute-start.18 = (bf16[128,1024]{1,0:T(8,128)(2,1)}, bf16[128,1024]{1,0:T(8,128)(2,1)}, u32[]{:S(2)}, u32[]{:S(2)}) collective-permute-start(bf16[128,1024]{1,0:T(8,128)(2,1)} %get-tuple-element.170), channel_id=1, source_target_pairs={{0,1},{1,2},{2,3},{3,0},{4,5},{5,6},{6,7},{7,4},{8,9},{9,10},{10,1... | collective-permute-start | bytes 786440 | tf_op jit(solution)/shard_map/ppermute | solution.py:70
  328.1 9.5 %collective-permute-start.22 = (bf16[4,4,64,1024]{3,2,1,0:T(8,128)(2,1)}, bf16[4,4,64,1024]{3,2,1,0:T(8,128)(2,1)}, u32[]{:S(2)}, u32[]{:S(2)}) collective-permute-start(bf16[4,4,64,1024]{3,2,1,0:T(8,128)(2,1)} %get-tuple-element.122), channel_id=1, source_target_pairs={{0,4},{1,5},{2,6},{3,7},{4,0},{5,1},{6,2},{7,3},{8,12},{9,13},{10,... | collective-permute-start | bytes 6291464 | tf_op jit(solution)/shard_map/ppermute | solution.py:70
  328.1 9.5 %collective-permute-start.21 = (bf16[4,4,64,1024]{3,2,1,0:T(8,128)(2,1)}, bf16[4,4,64,1024]{3,2,1,0:T(8,128)(2,1)}, u32[]{:S(2)}, u32[]{:S(2)}) collective-permute-start(bf16[4,4,64,1024]{3,2,1,0:T(8,128)(2,1)} %get-tuple-element.120.refs_6_), channel_id=1, source_target_pairs={{0,4},{1,5},{2,6},{3,7},{4,0},{5,1},{6,2},{7,3},{8,12},{9,13},{10,... | collective-permute-start | bytes 6291464 | tf_op jit(solution)/shard_map/ppermute | solution.py:70
  335.1 27.2 %collective-permute-start.24 = (bf16[512,1024]{1,0:T(8,128)(2,1)}, bf16[512,1024]{1,0:T(8,128)(2,1)S(1)}, u32[]{:S(2)}, u32[]{:S(2)}) collective-permute-start(bf16[512,1024]{1,0:T(8,128)(2,1)} %get-tuple-element.124.refs_0_), channel_id=1, source_target_pairs={{1,0},{2,1},{3,2},{4,3},{5,4},{6,5},{7,6},{8,7},{9,8},{10,9},{11,1... | collective-permute-start | bytes 3145736 | tf_op jit(solution)/shard_map/ppermute | solution.py:76
  344.3 29.1 %collective-permute-start.23 = (bf16[2,4,64,1024]{3,2,1,0:T(8,128)(2,1)}, bf16[2,4,64,1024]{3,2,1,0:T(8,128)(2,1)}, u32[]{:S(2)}, u32[]{:S(2)}) collective-permute-start(bf16[2,4,64,1024]{3,2,1,0:T(8,128)(2,1)} %get-tuple-element.125.refs_8_), channel_id=1, source_target_pairs={{0,8},{1,9},{2,10},{3,11},{4,12},{5,13},{6,14},{7,15},{8,0},{9,1},... | collective-permute-start | bytes 3145736 | tf_op jit(solution)/shard_map/ppermute | solution.py:70
  348.2 36.3 %collective-permute-start.25 = (bf16[2,4,64,1024]{3,2,1,0:T(8,128)(2,1)}, bf16[2,4,64,1024]{3,2,1,0:T(8,128)(2,1)}, u32[]{:S(2)}, u32[]{:S(2)}) collective-permute-start(bf16[2,4,64,1024]{3,2,1,0:T(8,128)(2,1)} %get-tuple-element.129.refs_10_), channel_id=1, source_target_pairs={{0,16},{1,17},{2,18},{3,19},{4,20},{5,21},{6,22},{7,23},{8,24},{9,... | collective-permute-start | bytes 3145736 | tf_op jit(solution)/shard_map/ppermute | solution.py:70
  368.8 26.5 %collective-permute-start.27 = (bf16[512,1024]{1,0:T(8,128)(2,1)}, bf16[512,1024]{1,0:T(8,128)(2,1)S(1)}, u32[]{:S(2)}, u32[]{:S(2)}) collective-permute-start(bf16[512,1024]{1,0:T(8,128)(2,1)} %get-tuple-element.132.refs_0_), channel_id=1, source_target_pairs={{1,0},{2,1},{3,2},{4,3},{5,4},{6,5},{7,6},{8,7},{9,8},{10,9},{11,1... | collective-permute-start | bytes 3145736 | tf_op jit(solution)/shard_map/ppermute | solution.py:76
  376.8 39.4 %collective-permute-start.34 = (bf16[4,64,1024]{2,1,0:T(8,128)(2,1)}, bf16[4,64,1024]{2,1,0:T(8,128)(2,1)}, u32[]{:S(2)}, u32[]{:S(2)}) collective-permute-start(bf16[4,64,1024]{2,1,0:T(8,128)(2,1)} %get-tuple-element.133.refs_0_.refs_1_), channel_id=1, source_target_pairs={{0,16},{1,17},{2,18},{3,19},{4,20},{5,21},{6,22},{7,23},{8,24},{9,... | collective-permute-start | bytes 1572872 | tf_op jit(solution)/shard_map/ppermute | solution.py:70
  387.9 30.4 %collective-permute-start.35 = (bf16[4,64,1024]{2,1,0:T(8,128)(2,1)}, bf16[4,64,1024]{2,1,0:T(8,128)(2,1)}, u32[]{:S(2)}, u32[]{:S(2)}) collective-permute-start(bf16[4,64,1024]{2,1,0:T(8,128)(2,1)} %get-tuple-element.135.refs_2_.refs_3_), channel_id=1, source_target_pairs={{0,8},{1,9},{2,10},{3,11},{4,12},{5,13},{6,14},{7,15},{8,0},{9,1},... | collective-permute-start | bytes 1572872 | tf_op jit(solution)/shard_map/ppermute | solution.py:70
  388.2 8.0 %collective-permute-start.28 = (f32[2,2,4,384]{3,2,1,0:T(4,128)S(1)}, f32[2,2,4,384]{3,2,1,0:T(4,128)S(1)}, u32[]{:S(2)}, u32[]{:S(2)}) collective-permute-start(f32[2,2,4,384]{3,2,1,0:T(4,128)S(1)} %dynamic-slice_bitcast_fusion.9), channel_id=1, source_target_pairs={{0,4},{1,5},{2,6},{3,7},{4,0},{5,1},{6,2},{7,3},{8,12},{9,13},{10,... | collective-permute-start | bytes 73736 | tf_op jit(solution)/shard_map/ppermute | solution.py:70
  396.2 19.4 %collective-permute-start.29 = (f32[2,4,384]{2,1,0:T(4,128)S(1)}, f32[2,4,384]{2,1,0:T(4,128)S(1)}, u32[]{:S(2)}, u32[]{:S(2)}) collective-permute-start(f32[2,4,384]{2,1,0:T(4,128)S(1)} %dynamic-slice_bitcast_fusion.10), channel_id=1, source_target_pairs={{0,8},{1,9},{2,10},{3,11},{4,12},{5,13},{6,14},{7,15},{8,0},{9,1},... | collective-permute-start | bytes 36872 | tf_op jit(solution)/shard_map/ppermute | solution.py:70
  400.4 22.9 %collective-permute-start.41 = (bf16[2,32,2048]{2,1,0:T(8,128)(2,1)S(1)}, bf16[2,32,2048]{2,1,0:T(8,128)(2,1)S(1)}, u32[]{:S(2)}, u32[]{:S(2)}) collective-permute-start(bf16[2,32,2048]{2,1,0:T(8,128)(2,1)S(1)} %get-tuple-element.160), channel_id=1, source_target_pairs={{0,3},{1,0},{2,1},{3,2},{4,7},{5,4},{6,5},{7,6},{8,11},{9,8},{10,9... | collective-permute-start | bytes 786440 | tf_op jit(solution)/shard_map/ppermute | solution.py:70
  408.7 18.9 %collective-permute-start.40 = (bf16[2,32,2048]{2,1,0:T(8,128)(2,1)S(1)}, bf16[2,32,2048]{2,1,0:T(8,128)(2,1)S(1)}, u32[]{:S(2)}, u32[]{:S(2)}) collective-permute-start(bf16[2,32,2048]{2,1,0:T(8,128)(2,1)S(1)} %get-tuple-element.161), channel_id=1, source_target_pairs={{0,2},{1,3},{2,0},{3,1},{4,6},{5,7},{6,4},{7,5},{8,10},{9,11},{10,... | collective-permute-start | bytes 786440 | tf_op jit(solution)/shard_map/ppermute | solution.py:70
  415.6 12.1 %collective-permute-start.39 = (bf16[2,32,2048]{2,1,0:T(8,128)(2,1)S(1)}, bf16[2,32,2048]{2,1,0:T(8,128)(2,1)S(1)}, u32[]{:S(2)}, u32[]{:S(2)}) collective-permute-start(bf16[2,32,2048]{2,1,0:T(8,128)(2,1)S(1)} %get-tuple-element.162), channel_id=1, source_target_pairs={{0,1},{1,2},{2,3},{3,0},{4,5},{5,6},{6,7},{7,4},{8,9},{9,10},{10,1... | collective-permute-start | bytes 786440 | tf_op jit(solution)/shard_map/ppermute | solution.py:70
  416.1 7.1 %collective-permute-start.30 = (f32[4,384]{1,0:T(4,128)S(1)}, f32[4,384]{1,0:T(4,128)S(1)}, u32[]{:S(2)}, u32[]{:S(2)}) collective-permute-start(f32[4,384]{1,0:T(4,128)S(1)} %fusion.34), channel_id=1, source_target_pairs={{0,16},{1,17},{2,18},{3,19},{4,20},{5,21},{6,22},{7,23},{8,24},{9,... | collective-permute-start | bytes 18440 | tf_op jit(solution)/shard_map/ppermute | solution.py:70
  419.9 18.9 %collective-permute-start.38 = (bf16[4,32,1024]{2,1,0:T(8,128)(2,1)S(1)}, bf16[4,32,1024]{2,1,0:T(8,128)(2,1)S(1)}, u32[]{:S(2)}, u32[]{:S(2)}) collective-permute-start(bf16[4,32,1024]{2,1,0:T(8,128)(2,1)S(1)} %get-tuple-element.164), channel_id=1, source_target_pairs={{0,3},{1,0},{2,1},{3,2},{4,7},{5,4},{6,5},{7,6},{8,11},{9,8},{10,9... | collective-permute-start | bytes 786440 | tf_op jit(solution)/shard_map/ppermute | solution.py:70
  423.2 15.6 %collective-permute-start.36 = (bf16[4,32,1024]{2,1,0:T(8,128)(2,1)S(1)}, bf16[4,32,1024]{2,1,0:T(8,128)(2,1)S(1)}, u32[]{:S(2)}, u32[]{:S(2)}) collective-permute-start(bf16[4,32,1024]{2,1,0:T(8,128)(2,1)S(1)} %get-tuple-element.166), channel_id=1, source_target_pairs={{0,1},{1,2},{2,3},{3,0},{4,5},{5,6},{6,7},{7,4},{8,9},{9,10},{10,1... | collective-permute-start | bytes 786440 | tf_op jit(solution)/shard_map/ppermute | solution.py:70
  423.2 26.9 %collective-permute-start.37 = (bf16[4,32,1024]{2,1,0:T(8,128)(2,1)S(1)}, bf16[4,32,1024]{2,1,0:T(8,128)(2,1)S(1)}, u32[]{:S(2)}, u32[]{:S(2)}) collective-permute-start(bf16[4,32,1024]{2,1,0:T(8,128)(2,1)S(1)} %get-tuple-element.167), channel_id=1, source_target_pairs={{0,2},{1,3},{2,0},{3,1},{4,6},{5,7},{6,4},{7,5},{8,10},{9,11},{10,... | collective-permute-start | bytes 786440 | tf_op jit(solution)/shard_map/ppermute | solution.py:70
  427.6 25.7 %collective-permute-start.26 = (bf16[512,1024]{1,0:T(8,128)(2,1)S(1)}, bf16[512,1024]{1,0:T(8,128)(2,1)S(1)}, u32[]{:S(2)}, u32[]{:S(2)}) collective-permute-start(bf16[512,1024]{1,0:T(8,128)(2,1)S(1)} %shard_map.304.refs_0_), channel_id=1, source_target_pairs={{0,4},{1,5},{2,6},{3,7},{4,0},{5,1},{6,2},{7,3},{8,12},{9,13},{10,... | collective-permute-start | bytes 3145736 | tf_op jit(solution)/shard_map/ppermute | solution.py:70
  427.7 22.8 %collective-permute-start.31 = (f32[384]{0:T(512)S(1)}, f32[384]{0:T(512)S(1)}, u32[]{:S(2)}, u32[]{:S(2)}) collective-permute-start(f32[384]{0:T(512)S(1)} %get-tuple-element.154), channel_id=1, source_target_pairs={{0,1},{1,2},{2,3},{3,0},{4,5},{5,6},{6,7},{7,4},{8,9},{9,10},{10,1... | collective-permute-start | bytes 4616 | tf_op jit(solution)/shard_map/ppermute | solution.py:70
  438.8 11.7 %collective-permute-start.33 = (f32[384]{0:T(512)S(1)}, f32[384]{0:T(512)S(1)}, u32[]{:S(2)}, u32[]{:S(2)}) collective-permute-start(f32[384]{0:T(512)S(1)} %get-tuple-element.155), channel_id=1, source_target_pairs={{0,3},{1,0},{2,1},{3,2},{4,7},{5,4},{6,5},{7,6},{8,11},{9,8},{10,9... | collective-permute-start | bytes 4616 | tf_op jit(solution)/shard_map/ppermute | solution.py:70
  438.8 11.7 %collective-permute-start.32 = (f32[384]{0:T(512)S(1)}, f32[384]{0:T(512)S(1)}, u32[]{:S(2)}, u32[]{:S(2)}) collective-permute-start(f32[384]{0:T(512)S(1)} %get-tuple-element.156), channel_id=1, source_target_pairs={{0,2},{1,3},{2,0},{3,1},{4,6},{5,7},{6,4},{7,5},{8,10},{9,11},{10,... | collective-permute-start | bytes 4616 | tf_op jit(solution)/shard_map/ppermute | solution.py:70
  450.3 2.8 collective-permute-start.42
  (80 other events, 470.4 us)
Sparse Core Ops, SparseCore 0:
  34.9 113.8 all-gather.5
  152.1 74.7 all-gather.3
  229.9 51.2 reduce-scatter.2
  284.4 52.6 reduce-scatter.4

commit v4 on v3

--- a/solution.py
+++ b/solution.py
@@ -328,25 +328,29 @@
     )(left, right, *earlier)
 
 
-def product_nn_kernel(left, right, *refs):
-    refs[-1][...] = dot_nn(left[...], right[...]).astype(refs[-1].dtype)
-
-
-def product_nn(left, right, kind, row_block, rows, earlier=()):
-    depth, wide = right.shape
-    return pl.pallas_call(
-        product_nn_kernel,
-        grid=(wide // TILE,),
-        in_specs=[
-            pl.BlockSpec((rows, depth), lambda i: (row_block, 0)),
-            pl.BlockSpec((depth, TILE), lambda i: (0, i)),
-        ]
+def branch_kernel(hidden, down, *refs):
+    kept, given = refs[-2:]
+    product = dot_nn(hidden[...], down[...])
+    rows = kept.shape[0]
+    kept[...] = product[:rows]
+    given[...] = product[rows:].astype(bf16)
+
+
+def branch_terms(hidden, down, earlier=()):
+    tokens, units = hidden.shape
+    width = down.shape[1]
+    rows = tokens // 2
+    tile = pl.BlockSpec((rows, TILE), lambda i: (0, i))
+    return pl.pallas_call(
+        branch_kernel,
+        grid=(width // TILE,),
+        in_specs=[pl.BlockSpec((tokens, units), lambda i: (0, 0)), pl.BlockSpec((units, TILE), lambda i: (0, i))]
         + [pl.BlockSpec(memory_space=pl.ANY)] * len(earlier),
-        out_specs=pl.BlockSpec((rows, TILE), lambda i: (0, i)),
-        out_shape=jax.ShapeDtypeStruct((rows, wide), kind),
+        out_specs=[tile, tile],
+        out_shape=[jax.ShapeDtypeStruct((rows, width), f32), jax.ShapeDtypeStruct((rows, width), bf16)],
         compiler_params=pltpu.CompilerParams(vmem_limit_bytes=VMEM_LIMIT),
         cost_estimate=SHORT,
-    )(left, right, *earlier)
+    )(hidden, down, *earlier)
 
 
 def chunk_kernel(count, with_arrived, *refs):
@@ -365,13 +369,13 @@
 
 def chunk_back(pairs, chunk, kind, arrived=None, earlier=()):
     rows, width = chunk[0].shape
-    tile = pl.BlockSpec((rows, TILE), lambda i: (0, i))
-    sums = pl.BlockSpec((1, TILE), lambda i: (0, i))
+    tile = pl.BlockSpec((rows, WIDE), lambda i: (0, i))
+    sums = pl.BlockSpec((1, WIDE), lambda i: (0, i))
     return pl.pallas_call(
         functools.partial(chunk_kernel, len(pairs), arrived is not None),
-        grid=(width // TILE,),
+        grid=(width // WIDE,),
         in_specs=[pl.BlockSpec((rows, left.shape[1]), lambda i, at=at: (at, 0)) for left, at, _ in pairs]
-        + [pl.BlockSpec((TILE, right.shape[1]), lambda i: (i, 0)) for *_, right in pairs]
+        + [pl.BlockSpec((WIDE, right.shape[1]), lambda i: (i, 0)) for *_, right in pairs]
         + [tile, pl.BlockSpec((rows, LANES), lambda i: (0, 0))]
         + [tile] * (arrived is not None)
         + [pl.BlockSpec(memory_space=pl.ANY)] * len(earlier),
@@ -430,7 +434,13 @@
 
 
 def joined_kernel_terms(blocks, core, tokens_ext, context, query, key, value, branch, *refs):
-    given_ahead, given_behind, kept_ahead, kept_behind = refs[-4:]
+    given_ahead, given_behind, kept_ahead, kept_behind, query_sum, value_sum = refs[-6:]
+
+    @pl.when(pl.program_id(0) == 0)
+    def _():
+        query_sum[...] = jnp.sum(query[...].astype(f32), axis=0, keepdims=True)
+        value_sum[...] = jnp.sum(value[...].astype(f32), axis=0, keepdims=True)
+
     left = tokens_ext[...]
     own = left[left.shape[0] - query.shape[0] :]
     rows = kept_ahead.shape[2]
@@ -450,6 +460,7 @@
     rows = width // count
     half = (1, 4, rows // 4, width)
     stacked = pl.BlockSpec(half, lambda i, at, core: (i, 0, 0, 0))
+    sums = pl.BlockSpec((1, width), lambda i, at, core: (0, 0))
 
     def whole(array):
         return pl.BlockSpec(array.shape, lambda i, at, core: (0, 0))
@@ -465,9 +476,9 @@
                 *(whole(right) for right in rights),
                 *[pl.BlockSpec(memory_space=pl.ANY)] * len(earlier),
             ],
-            out_specs=[stacked] * 4,
+            out_specs=[stacked] * 4 + [sums] * 2,
         ),
-        out_shape=[jax.ShapeDtypeStruct((count, *half[1:]), bf16)] * 4,
+        out_shape=[jax.ShapeDtypeStruct((count, *half[1:]), bf16)] * 4 + [jax.ShapeDtypeStruct((1, width), f32)] * 2,
         compiler_params=pltpu.CompilerParams(vmem_limit_bytes=VMEM_LIMIT),
         cost_estimate=SHORT,
     )(
@@ -1069,8 +1080,7 @@
     nears = [*joined_near[0], *joined_near[1]]
     up_rows_both = after(up_plane, *nears).reshape(2, nz, up_rows, ff_core).swapaxes(0, 1)
     returned = grid.to_earlier(returned)
-    branch_given = product_nn(hidden, down_mat, bf16, 1, tok_rows, nears)
-    branch_kept = product_nn(hidden, down_mat, f32, 0, tok_rows, (branch_given,))
+    branch_kept, branch_given = branch_terms(hidden, down_mat, nears)
     joined_far = [far_sums(part, joined_near[part], returned, branch_kept) for part in range(2)]
     both = [half.reshape(4, nz // 2, -1, width) for half in joined_far]
     both = jnp.concatenate(both, axis=1)
@@ -1097,8 +1107,8 @@
     gain_one_grad, shift_one_grad = (sum(total).reshape(-1) for total in zip(*chunk_sums))
     joined_vec_grad = jnp.stack(
         [
-            jnp.sum(query_change.astype(f32), axis=0).reshape(HEADS, HEAD_DIM),
-            jnp.sum(value_change.astype(f32), axis=0).reshape(HEADS, HEAD_DIM),
+            joined_given[4].reshape(HEADS, HEAD_DIM),
+            joined_given[5].reshape(HEADS, HEAD_DIM),
         ],
         axis=1,
     ).reshape(-1)

time: 466 us -> 464 us (level)
    pallas_call x2 -> x1, Pallas kernels: 11 us -> 8.34 us  [branch_terms(): pl.pallas_call(branch_kernel, grid=(width // TILE,), in_specs=[pl.BlockSp...]
    unnamed x175 -> x197, local copies, waits for them, and re-layouts: 31.8 us -> 32.4 us
where the time goes in v4:
time: 464 us; the launch traced here: 459 us
  Pallas kernels  202 us (44%)
  waiting for transfers between devices  106 us (23%)
  starting transfers between devices  71.6 us (15%)
  local copies, waits for them, and re-layouts  41 us (9%)
  other arithmetic  22.1 us (5%)
  between operations  16 us (3%)
    ppermute x39, starting transfers between devices, shift(): lax.ppermute(block, ALL, list(zip(places.ravel().tolist(), ahead.ravel()....  60.1 us
    ppermute x39, waiting for transfers between devices, shift(): lax.ppermute(block, ALL, list(zip(places.ravel().tolist(), ahead.ravel()....  42.3 us
    all_gather x1, waiting for transfers between devices, on_device(): lax.all_gather(after(down_weight, *joined_line[1:]), lines, axis=0, tiled...  36.1 us
    pallas_call x2, Pallas kernels, attend_back(): pl.pallas_call(functools.partial(attend_back_kernel, first_pair=first_pai...  34 us
    unnamed x197, local copies, waits for them, and re-layouts  32.4 us
    pallas_call x1, Pallas kernels, attend(): pl.pallas_call(attend_kernel, grid=(steps,), in_specs=[pl.BlockSpec((tok_...  21.3 us
    pallas_call x3, Pallas kernels, project(): pl.pallas_call(functools.partial(projection_kernel, kinds, len(others)),...  19.3 us
    pallas_call x3, Pallas kernels, chunk_back(): pl.pallas_call(functools.partial(chunk_kernel, len(pairs), arrived is not...  18.8 us
  transfers between devices with their start and end apart: 47, of which 18 were waited for; matrix products, arithmetic and copies ran while one was open for 7% of the time, Pallas kernels for 44%

profile of v4, /device:TPU:0, one launch (start us, length us, event | category | flops | bytes accessed | tf_op | source)
XLA Modules:
  0.0 459.3 jit_solution(9757992337259983556)
XLA Ops:
  10.7 5.0 %collective-permute-start.6 = (bf16[3,32,1152]{2,1,0:T(8,128)(2,1)}, bf16[3,32,1152]{2,1,0:T(8,128)(2,1)S(1)}, u32[]{:S(2)}, u32[]{:S(2)}) collective-permute-start(bf16[3,32,1152]{2,1,0:T(8,128)(2,1)} %shard_map.272), channel_id=1, source_target_pairs={{0,3},{1,0},{2,1},{3,2},{4,7},{5,4},{6,5},{7,6},{8,11},{9,8},{10,9... | collective-permute-start | bytes 663560 | tf_op jit(solution)/shard_map/ppermute | solution.py:70
  21.9 12.8 %collective-permute-done.5.refs_2_ = bf16[3,32,1152]{2,1,0:T(8,128)(2,1)S(1)} collective-permute-done((bf16[3,32,1152]{2,1,0:T(8,128)(2,1)}, bf16[3,32,1152]{2,1,0:T(8,128)(2,1)S(1)}, u32[]{:S(2)}, u32[]{:S(2)}) %collective-permute-start.5) | collective-permute-done | bytes 221216 | tf_op jit(solution)/shard_map/ppermute | solution.py:70
  40.8 3.9 collective-permute-start.11
  44.7 5.1 %collective-permute-done.7 = bf16[2,3,32,1152]{3,2,1,0:T(8,128)(2,1)S(1)} collective-permute-done((bf16[2,3,32,1152]{3,2,1,0:T(8,128)(2,1)S(1)}, bf16[2,3,32,1152]{3,2,1,0:T(8,128)(2,1)S(1)}, u32[]{:S(2)}, u32[]{:S(2)}) %collective-permute-start.7) | collective-permute-done | bytes 442400 | tf_op jit(solution)/shard_map/ppermute | solution.py:70
  51.6 3.3 collective-permute-done.1
  56.0 17.7 %collective-permute-done.11.tokens.refs_4_ = bf16[512,1024]{1,0:T(8,128)(2,1)} collective-permute-done((bf16[512,1024]{1,0:T(8,128)(2,1)S(1)}, bf16[512,1024]{1,0:T(8,128)(2,1)}, u32[]{:S(2)}, u32[]{:S(2)}) %collective-permute-start.11) | collective-permute-done | bytes 1048608 | tf_op jit(solution)/shard_map/ppermute | solution.py:73
  73.8 4.8 %collective-permute-start.12 = (bf16[512,1024]{1,0:T(8,128)(2,1)}, bf16[512,1024]{1,0:T(8,128)(2,1)S(1)}, u32[]{:S(2)}, u32[]{:S(2)}) collective-permute-start(bf16[512,1024]{1,0:T(8,128)(2,1)} %collective-permute-done.11.tokens.refs_4_), channel_id=1, source_target_pairs={{0,1},{1,2},{2,3},{3,4},{4,5},{5,6},{6,7},{7,8},{8,9},{9,10},{10,1... | collective-permute-start | bytes 3145736 | tf_op jit(solution)/shard_map/ppermute | solution.py:73
  79.7 3.4 collective-permute-done.9.refs_6_
  85.1 2.4 select_convert_fusion.1.key_side
  90.5 7.4 %shard_map.273 = (bf16[32,32,1024]{2,1,0:T(8,128)(2,1)}, bf16[32,32,1024]{2,1,0:T(8,128)(2,1)}, bf16[32,32,1024]{2,1,0:T(8,128)(2,1)}, bf16[32,32,128]{2,1,0:T(8,128)(2,1)S(1)}) custom-call(s32[32]{0:T(128)S(1)} %stack.305.places, bf16[2,2,3,32,1152]{4,3,2,1,0:T(8,128)(2,1)S(1)} %pad_maximum_fusion.2.refs_0_, ...), custom_call_target="tpu_custom_call" | custom-call | flops 1 | bytes 1 | tf_op jit(solution)/shard_map/pallas_call | solution.py:138
  103.2 7.1 %shard_map.275 = (bf16[1536,1024]{1,0:T(8,128)(2,1)}, f32[512,128]{1,0:T(8,128)S(1)}, bf16[1536,1024]{1,0:T(8,128)(2,1)}, bf16[1536,1024]{1,0:T(8,128)(2,1)}, bf16[512,1024]{1,0:T(8,128)(2,1)S(1)}) custom-call(bf16[512,1024]{1,0:T(8,128)(2,1)S(1)} %copy-done.1, f32[1,1024]{1,0:T(1,128)S(1)} %copy-done.43, f32[1,1024]{1,0:T(1,128)S(1)} %copy-done.45, ...), custom_call_target="tpu_custom_call" | custom-call | flops 1 | bytes 1 | tf_op jit(solution)/shard_map/pallas_call | solution.py:847
  111.0 6.3 %shard_map.277 = (bf16[1536,1024]{1,0:T(8,128)(2,1)}, f32[512,128]{1,0:T(8,128)S(1)}, bf16[1536,1024]{1,0:T(8,128)(2,1)}, bf16[1536,1024]{1,0:T(8,128)(2,1)}) custom-call(bf16[512,1024]{1,0:T(8,128)(2,1)} %collective-permute-done.11.tokens.refs_4_, f32[1,1024]{1,0:T(1,128)S(1)} %copy-done.44, ...), custom_call_target="tpu_custom_call", output_to_operand_aliasing={{0}: (7, {}), {2}: (8, {}), {3}: (9, {})} | custom-call | flops 1 | bytes 1 | tf_op jit(solution)/shard_map/pallas_call | solution.py:847
  117.3 6.0 %shard_map.278 = (bf16[1536,1024]{1,0:T(8,128)(2,1)}, f32[512,128]{1,0:T(8,128)S(1)}, bf16[1536,1024]{1,0:T(8,128)(2,1)}, bf16[1536,1024]{1,0:T(8,128)(2,1)}) custom-call(bf16[512,1024]{1,0:T(8,128)(2,1)S(1)} %collective-permute-done.12.tokens.refs_4_, f32[1,1024]{1,0:T(1,128)S(1)} %copy-done.44, ...), custom_call_target="tpu_custom_call", output_to_operand_aliasing={{0}: (7, {}), {2}: (8, {}), {3}: (9, {})} | custom-call | flops 1 | bytes 1 | tf_op jit(solution)/shard_map/pallas_call | solution.py:847
  124.0 21.3 %shard_map.280 = (bf16[512,1024]{1,0:T(8,128)(2,1)S(1)}, f32[512,128]{1,0:T(8,128)S(1)}) custom-call(bf16[512,1024]{1,0:T(8,128)(2,1)} %copy-done.7, bf16[1536,1024]{1,0:T(8,128)(2,1)} %get-tuple-element.102.key, bf16[1536,1024]{1,0:T(8,128)(2,1)} %get-tuple-element.103.value, bf16[512,128]{1,0:T(8,128)(2,1)S(1)} %select_convert_fusion.2.query_side, ...), custom_call_target="tpu_custom_call" | custom-call | flops 1 | bytes 1 | tf_op jit(solution)/shard_map/pallas_call | solution.py:604
  146.0 2.7 all-gather.6.cloned.1.call-done
  151.0 2.4 collective-permute-done.15
  159.0 2.3 collective-permute-done.16.other
  161.3 11.6 %shard_map.283 = (bf16[1024,2048]{1,0:T(8,128)(2,1)}, bf16[1024,2048]{1,0:T(8,128)(2,1)}) custom-call(s32[1]{0:T(128)} %bitcast.66.core, bf16[512,1024]{1,0:T(8,128)(2,1)S(1)} %add_convert_fusion.own, bf16[512,1024]{1,0:T(8,128)(2,1)S(1)} %collective-permute-done.16.other, bf16[16,5,32,1024]{3,2,1,0:T(8,128)(2,1)} %bitcast.226, ...), custom_call_target="tpu_custom_call" | custom-call | flops 1 | bytes 1 | tf_op jit(solution)/shard_map/pallas_call | solution.py:771
  172.9 9.6 %shard_map.285 = (bf16[2048,1024]{1,0:T(8,128)(2,1)}, f32[1,1024]{1,0:T(1,128)S(1)}) custom-call(bf16[1024,2048]{1,0:T(8,128)(2,1)} %get-tuple-element.109.left.refs_1_.hidden, bf16[1024,1024]{1,0:T(8,128)(2,1)S(1)} %copy-done.4), custom_call_target="tpu_custom_call" | custom-call | flops 1 | bytes 1 | tf_op jit(solution)/shard_map/pallas_call | solution.py:252
  183.3 2.2 copy-done.2
  185.5 5.4 %shard_map.288 = bf16[32,32,2048]{2,1,0:T(8,128)(2,1)} custom-call(s32[32]{0:T(128)S(1)} %shard_map.287.places, bf16[16,5,32,1024]{3,2,1,0:T(8,128)(2,1)} %bitcast.228), custom_call_target="tpu_custom_call" | custom-call | flops 1 | bytes 1 | tf_op jit(solution)/shard_map/pallas_call | solution.py:138
  190.9 36.1 %all-gather.4.cloned.1.call-done.down = bf16[2048,1024]{1,0:T(8,128)(2,1)} async-done(((bf16[128,1024]{1,0:T(8,128)(2,1)}), bf16[2048,1024]{1,0:T(8,128)(2,1)}) %all-gather.4.cloned.1.call-update) | async-done | bytes 4194320 | tf_op jit(solution)/shard_map/all_gather | solution.py:985
  227.0 8.7 %shard_map.286 = (bf16[1024,2048]{1,0:T(8,128)(2,1)}, f32[1,2048]{1,0:T(1,128)S(1)}) custom-call(bf16[1024,1024]{1,0:T(8,128)(2,1)S(1)} %copy-done.4, bf16[2048,1024]{1,0:T(8,128)(2,1)} %all-gather.4.cloned.1.call-done.down, bf16[1024,2048]{1,0:T(8,128)(2,1)} %get-tuple-element.111.slope, bf16[2048,1024]{1,0:T(8,128)(2,1)} %get-tuple-element.112.refs_0_), custom_call_target="tpu_custom_call" | custom-call | flops 1 | bytes 1 | tf_op jit(solution)/shard_map/pallas_call | solution.py:797
  235.8 5.0 %shard_map.289.refs_0_ = bf16[512,1024]{1,0:T(8,128)(2,1)S(1)} custom-call(bf16[1024,2048]{1,0:T(8,128)(2,1)} %get-tuple-element.113.left.right.pre_change, bf16[1024,2048]{1,0:T(8,128)(2,1)} %bitcast.229), custom_call_target="tpu_custom_call" | custom-call | flops 1 | bytes 1 | tf_op jit(solution)/shard_map/pallas_call | solution.py:316
  240.8 8.0 %shard_map.290.refs_0_ = bf16[1024,2048]{1,0:T(8,128)(2,1)} custom-call(bf16[512,1024]{1,0:T(8,128)(2,1)S(1)} %copy-done.10, bf16[512,1024]{1,0:T(8,128)(2,1)S(1)} %copy-done.20, bf16[1024,2048]{1,0:T(8,128)(2,1)} %get-tuple-element.113.left.right.pre_change, bf16[512,1024]{1,0:T(8,128)(2,1)S(1)} %shard_map.289.refs_0_), custom_call_target="tpu_custom_call" | custom-call | flops 1 | bytes 1 | tf_op jit(solution)/shard_map/pallas_call | solution.py:275
  249.0 2.6 collective-permute-done.17.arrived
  251.6 9.4 %shard_map.291 = (f32[512,1024]{1,0:T(8,128)}, bf16[512,1024]{1,0:T(8,128)(2,1)S(1)}, bf16[512,1024]{1,0:T(8,128)(2,1)S(1)}, f32[1,1024]{1,0:T(1,128)S(1)}, f32[...) custom-call(bf16[1024,2048]{1,0:T(8,128)(2,1)} %get-tuple-element.113.left.right.pre_change, bf16[1024,2048]{1,0:T(8,128)(2,1)} %bitcast.230, ...), custom_call_target="tpu_custom_call" | custom-call | flops 1 | bytes 1 | tf_op jit(solution)/shard_map/pallas_call | solution.py:417
  264.7 16.9 %shard_map.292 = (bf16[512,1024]{1,0:T(8,128)(2,1)S(1)}, bf16[1536,1024]{1,0:T(8,128)(2,1)}, bf16[1536,1024]{1,0:T(8,128)(2,1)}) custom-call(bf16[512,1024]{1,0:T(8,128)(2,1)} %copy-done.7, bf16[1536,1024]{1,0:T(8,128)(2,1)} %get-tuple-element.102.key, bf16[1536,1024]{1,0:T(8,128)(2,1)} %get-tuple-element.103.value, bf16[512,1024]{1,0:T(8,128)(2,1)} %copy-done.14, ...), custom_call_target="tpu_custom_call" | custom-call | flops 1 | bytes 1 | tf_op jit(solution)/shard_map/pallas_call | solution.py:692
  283.8 3.1 collective-permute-start.20
  292.1 17.2 %shard_map.295 = (bf16[512,1024]{1,0:T(8,128)(2,1)S(1)}, bf16[1536,1024]{1,0:T(8,128)(2,1)}, bf16[1536,1024]{1,0:T(8,128)(2,1)}) custom-call(bf16[512,1024]{1,0:T(8,128)(2,1)} %copy-done.7, bf16[1536,1024]{1,0:T(8,128)(2,1)} %get-tuple-element.102.key, ...), custom_call_target="tpu_custom_call", output_to_operand_aliasing={{0}: (9, {}), {1}: (10, {}), {2}: (11, {})} | custom-call | flops 1 | bytes 1 | tf_op jit(solution)/shard_map/pallas_call | solution.py:692
  313.3 15.6 %shard_map.297 = (bf16[4,4,64,1024]{3,2,1,0:T(8,128)(2,1)}, bf16[4,4,64,1024]{3,2,1,0:T(8,128)(2,1)}, bf16[4,4,64,1024]{3,2,1,0:T(8,128)(2,1)}, bf16[4,4,64,1024...) custom-call(s32[4]{0:T(128)S(1)} %pad_add_fusion.blocks, s32[1]{0:T(128)} %bitcast.66.core, ...), custom_call_target="tpu_custom_call" | custom-call | flops 1 | bytes 1 | tf_op jit(solution)/shard_map/pallas_call | solution.py:468
  329.5 5.6 %shard_map.298 = (bf16[512,1024]{1,0:T(8,128)(2,1)}, f32[1,1024]{1,0:T(1,128)S(1)}, f32[1,1024]{1,0:T(1,128)S(1)}) custom-call(bf16[1536,1024]{1,0:T(8,128)(2,1)} %get-tuple-element.120.key.refs_0_, bf16[1536,1024]{1,0:T(8,128)(2,1)} %get-tuple-element.121.value.refs_1_, bf16[1024,1024]{1,0:T(8,128)(2,1)} %bitcast.202, bf16[1024,1024]{1,0:T(8,128)(2,1)} %bitcast.222, ...), custom_call_target="tpu_custom_call" | custom-call | flops 1 | bytes 1 | tf_op jit(solution)/shard_map/pallas_call | solution.py:374
  337.9 5.7 %shard_map.299 = (bf16[2,4,64,1024]{3,2,1,0:T(8,128)(2,1)}, bf16[2,4,64,1024]{3,2,1,0:T(8,128)(2,1)S(1)}, bf16[2,4,64,1024]{3,2,1,0:T(8,128)(2,1)}, bf16[2,4,64,1024]{3,2,1,0:T(8,128)(2,1)}) custom-call(bf16[2,2,4,64,1024]{4,3,2,1,0:T(8,128)(2,1)} %bitcast.237, bf16[2,2,4,64,1024]{4,3,2,1,0:T(8,128)(2,1)} %bitcast.112.arrived_ahead, ...), custom_call_target="tpu_custom_call" | custom-call | flops 1 | bytes 1 | tf_op jit(solution)/shard_map/pallas_call | solution.py:505
  344.6 3.8 collective-permute-start.23
  350.4 7.3 %shard_map.300 = (f32[512,1024]{1,0:T(8,128)}, f32[1,1024]{1,0:T(1,128)S(1)}, f32[1,1024]{1,0:T(1,128)S(1)}) custom-call(bf16[1536,1024]{1,0:T(8,128)(2,1)} %get-tuple-element.120.key.refs_0_, bf16[1536,1024]{1,0:T(8,128)(2,1)} %get-tuple-element.121.value.refs_1_, bf16[512,1024]{1,0:T(8,128)(2,1)S(1)} %get-tuple-element.119.query.refs_2_, ...), custom_call_target="tpu_custom_call" | custom-call | flops 1 | bytes 1 | tf_op jit(solution)/shard_map/pallas_call | solution.py:374
  358.8 4.3 collective-permute-done.24.refs_6_
  363.2 5.9 %shard_map.301 = (bf16[512,1024]{1,0:T(8,128)(2,1)}, f32[1,1024]{1,0:T(1,128)S(1)}, f32[1,1024]{1,0:T(1,128)S(1)}) custom-call(bf16[1536,1024]{1,0:T(8,128)(2,1)} %get-tuple-element.120.key.refs_0_, bf16[1536,1024]{1,0:T(8,128)(2,1)} %get-tuple-element.121.value.refs_1_, bf16[1024,1024]{1,0:T(8,128)(2,1)} %bitcast.204, bf16[1024,1024]{1,0:T(8,128)(2,1)} %bitcast.224, ...), custom_call_target="tpu_custom_call" | custom-call | flops 1 | bytes 1 | tf_op jit(solution)/shard_map/pallas_call | solution.py:374
  377.2 2.1 shard_map.302
  379.4 7.5 %collective-permute-start.34 = (bf16[4,64,1024]{2,1,0:T(8,128)(2,1)}, bf16[4,64,1024]{2,1,0:T(8,128)(2,1)}, u32[]{:S(2)}, u32[]{:S(2)}) collective-permute-start(bf16[4,64,1024]{2,1,0:T(8,128)(2,1)} %get-tuple-element.137.refs_0_.refs_1_), channel_id=1, source_target_pairs={{0,16},{1,17},{2,18},{3,19},{4,20},{5,21},{6,22},{7,23},{8,24},{9,... | collective-permute-start | bytes 1572872 | tf_op jit(solution)/shard_map/ppermute | solution.py:70
  388.1 2.1 shard_map.303
  396.7 3.8 collective-permute-start.29
  400.6 2.8 collective-permute-start.41
  403.4 8.3 %shard_map.304 = (f32[512,1024]{1,0:T(8,128)}, bf16[512,1024]{1,0:T(8,128)(2,1)S(1)}) custom-call(bf16[1024,2048]{1,0:T(8,128)(2,1)} %get-tuple-element.109.left.refs_1_.hidden, bf16[2048,1024]{1,0:T(8,128)(2,1)} %all-gather.4.cloned.1.call-done.down, bf16[4,64,1024]{2,1,0:T(8,128)(2,1)} %get-tuple-element.137.refs_0_.refs_1_, ...), custom_call_target="tpu_custom_call" | custom-call | flops 1 | bytes 1 | tf_op jit(solution)/shard_map/pallas_call | solution.py:344
  416.1 3.3 collective-permute-start.38
  422.5 3.2 collective-permute-done.40.refs_2_
  425.7 7.3 %collective-permute-start.31 = (f32[384]{0:T(512)S(1)}, f32[384]{0:T(512)S(1)}, u32[]{:S(2)}, u32[]{:S(2)}) collective-permute-start(f32[384]{0:T(512)S(1)} %get-tuple-element.162), channel_id=1, source_target_pairs={{0,1},{1,2},{2,3},{3,0},{4,5},{5,6},{6,7},{7,4},{8,9},{9,10},{10,1... | collective-permute-start | bytes 4616 | tf_op jit(solution)/shard_map/ppermute | solution.py:70
  433.0 3.6 collective-permute-done.38.refs_3_.refs_6_
  436.6 9.6 %collective-permute-start.32 = (f32[384]{0:T(512)S(1)}, f32[384]{0:T(512)S(1)}, u32[]{:S(2)}, u32[]{:S(2)}) collective-permute-start(f32[384]{0:T(512)S(1)} %get-tuple-element.164), channel_id=1, source_target_pairs={{0,2},{1,3},{2,0},{3,1},{4,6},{5,7},{6,4},{7,5},{8,10},{9,11},{10,... | collective-permute-start | bytes 4616 | tf_op jit(solution)/shard_map/ppermute | solution.py:70
  (373 shorter events, 91.7 us)
Async XLA Ops:
  7.2 141.6 %all-gather.6.cloned.1.call-start = ((), (), s32[]{:S(2)}) async-start(), calls=%async_computation.5 | async-start | bytes 5570560 | tf_op jit(solution)/shard_map/all_gather | solution.py:984
  10.7 11.2 %collective-permute-start.6 = (bf16[3,32,1152]{2,1,0:T(8,128)(2,1)}, bf16[3,32,1152]{2,1,0:T(8,128)(2,1)S(1)}, u32[]{:S(2)}, u32[]{:S(2)}) collective-permute-start(bf16[3,32,1152]{2,1,0:T(8,128)(2,1)} %shard_map.272), channel_id=1, source_target_pairs={{0,3},{1,0},{2,1},{3,2},{4,7},{5,4},{6,5},{7,6},{8,11},{9,8},{10,9... | collective-permute-start | bytes 663560 | tf_op jit(solution)/shard_map/ppermute | solution.py:70
  15.7 19.0 %collective-permute-start.5 = (bf16[3,32,1152]{2,1,0:T(8,128)(2,1)}, bf16[3,32,1152]{2,1,0:T(8,128)(2,1)S(1)}, u32[]{:S(2)}, u32[]{:S(2)}) collective-permute-start(bf16[3,32,1152]{2,1,0:T(8,128)(2,1)} %shard_map.272), channel_id=1, source_target_pairs={{0,2},{1,3},{2,0},{3,1},{4,6},{5,7},{6,4},{7,5},{8,10},{9,11},{10,... | collective-permute-start | bytes 663560 | tf_op jit(solution)/shard_map/ppermute | solution.py:70
  15.7 19.0 %collective-permute-start = (bf16[3,32,1152]{2,1,0:T(8,128)(2,1)}, bf16[3,32,1152]{2,1,0:T(8,128)(2,1)S(1)}, u32[]{:S(2)}, u32[]{:S(2)}) collective-permute-start(bf16[3,32,1152]{2,1,0:T(8,128)(2,1)} %shard_map.272), channel_id=1, source_target_pairs={{0,1},{1,2},{2,3},{3,0},{4,5},{5,6},{6,7},{7,4},{8,9},{9,10},{10,1... | collective-permute-start | bytes 663560 | tf_op jit(solution)/shard_map/ppermute | solution.py:70
  17.7 1.4 collective-permute-start.14
  34.8 192.2 %all-gather.4.cloned.1.call-start = ((), (), s32[]{:S(2)}) async-start(), calls=%async_computation.2 | async-start | bytes 4456448 | tf_op jit(solution)/shard_map/all_gather | solution.py:985
  35.5 246.0 %reduce-scatter.3.cloned.1.call-start = ((), (), s32[]{:S(2)}) async-start(), calls=%async_computation.3 | async-start | bytes 5242880 | tf_op jit(solution)/shard_map/reduce_scatter | solution.py:1031
  36.4 13.4 %collective-permute-start.7 = (bf16[2,3,32,1152]{3,2,1,0:T(8,128)(2,1)S(1)}, bf16[2,3,32,1152]{3,2,1,0:T(8,128)(2,1)S(1)}, u32[]{:S(2)}, u32[]{:S(2)}) collective-permute-start(bf16[2,3,32,1152]{3,2,1,0:T(8,128)(2,1)S(1)} %get-tuple-element.183), channel_id=1, source_target_pairs={{0,16},{1,17},{2,18},{3,19},{4,20},{5,21},{6,22},{7,23},{8,24},{9,... | collective-permute-start | bytes 1327112 | tf_op jit(solution)/shard_map/ppermute | solution.py:70
  38.0 16.8 %collective-permute-start.1 = (bf16[2,3,32,1152]{3,2,1,0:T(8,128)(2,1)S(1)}, bf16[2,3,32,1152]{3,2,1,0:T(8,128)(2,1)S(1)}, u32[]{:S(2)}, u32[]{:S(2)}) collective-permute-start(bf16[2,3,32,1152]{3,2,1,0:T(8,128)(2,1)S(1)} %get-tuple-element.185), channel_id=1, source_target_pairs={{0,8},{1,9},{2,10},{3,11},{4,12},{5,13},{6,14},{7,15},{8,0},{9,1},... | collective-permute-start | bytes 1327112 | tf_op jit(solution)/shard_map/ppermute | solution.py:70
  40.7 38.9 %collective-permute-start.13 = (bf16[512,1024]{1,0:T(8,128)(2,1)}, bf16[512,1024]{1,0:T(8,128)(2,1)}, u32[]{:S(2)}, u32[]{:S(2)}) collective-permute-start(bf16[512,1024]{1,0:T(8,128)(2,1)} %broadcast_select_fusion.out_change), channel_id=1, source_target_pairs={{0,4},{1,5},{2,6},{3,7},{4,0},{5,1},{6,2},{7,3},{8,12},{9,13},{10,... | collective-permute-start | bytes 3145736 | tf_op jit(solution)/shard_map/ppermute | solution.py:70
  40.8 43.3 %copy-start.79 = (f32[8,8,128]{2,1,0:T(8,128)S(1)}, f32[8,8,128]{2,1,0:T(8,128)}, u32[]{:S(2)}) copy-start(f32[8,8,128]{2,1,0:T(8,128)} %constant.347.clone) | copy-start | bytes 98308
  40.8 32.9 %collective-permute-start.11 = (bf16[512,1024]{1,0:T(8,128)(2,1)S(1)}, bf16[512,1024]{1,0:T(8,128)(2,1)}, u32[]{:S(2)}, u32[]{:S(2)}) collective-permute-start(bf16[512,1024]{1,0:T(8,128)(2,1)S(1)} %shard_map.276), channel_id=1, source_target_pairs={{0,1},{1,2},{2,3},{3,4},{4,5},{5,6},{6,7},{7,8},{8,9},{9,10},{10,1... | collective-permute-start | bytes 3145736 | tf_op jit(solution)/shard_map/ppermute | solution.py:73
  50.8 32.3 %collective-permute-start.9 = (bf16[2,2,3,32,1152]{4,3,2,1,0:T(8,128)(2,1)}, bf16[2,2,3,32,1152]{4,3,2,1,0:T(8,128)(2,1)}, u32[]{:S(2)}, u32[]{:S(2)}) collective-permute-start(bf16[2,2,3,32,1152]{4,3,2,1,0:T(8,128)(2,1)} %pad_maximum_fusion.3.refs_4_), channel_id=1, source_target_pairs={{0,8},{1,9},{2,10},{3,11},{4,12},{5,13},{6,14},{7,15},{8,0},{9,1},... | collective-permute-start | bytes 2654216 | tf_op jit(solution)/shard_map/ppermute | solution.py:70
  54.9 28.1 %collective-permute-start.3 = (bf16[2,2,3,32,1152]{4,3,2,1,0:T(8,128)(2,1)S(1)}, bf16[2,2,3,32,1152]{4,3,2,1,0:T(8,128)(2,1)}, u32[]{:S(2)}, u32[]{:S(2)}) collective-permute-start(bf16[2,2,3,32,1152]{4,3,2,1,0:T(8,128)(2,1)S(1)} %pad_maximum_fusion.2.refs_0_), channel_id=1, source_target_pairs={{0,16},{1,17},{2,18},{3,19},{4,20},{5,21},{6,22},{7,23},{8,24},{9,... | collective-permute-start | bytes 2654216 | tf_op jit(solution)/shard_map/ppermute | solution.py:70
  73.8 43.5 %collective-permute-start.12 = (bf16[512,1024]{1,0:T(8,128)(2,1)}, bf16[512,1024]{1,0:T(8,128)(2,1)S(1)}, u32[]{:S(2)}, u32[]{:S(2)}) collective-permute-start(bf16[512,1024]{1,0:T(8,128)(2,1)} %collective-permute-done.11.tokens.refs_4_), channel_id=1, source_target_pairs={{0,1},{1,2},{2,3},{3,4},{4,5},{5,6},{6,7},{7,8},{8,9},{9,10},{10,1... | collective-permute-start | bytes 3145736 | tf_op jit(solution)/shard_map/ppermute | solution.py:73
  79.1 11.4 %collective-permute-start.8 = (bf16[2,2,3,32,1152]{4,3,2,1,0:T(8,128)(2,1)}, bf16[2,2,3,32,1152]{4,3,2,1,0:T(8,128)(2,1)}, u32[]{:S(2)}, u32[]{:S(2)}) collective-permute-start(bf16[2,2,3,32,1152]{4,3,2,1,0:T(8,128)(2,1)} %pad_maximum_fusion.3.refs_4_), channel_id=1, source_target_pairs={{0,4},{1,5},{2,6},{3,7},{4,0},{5,1},{6,2},{7,3},{8,12},{9,13},{10,... | collective-permute-start | bytes 2654216 | tf_op jit(solution)/shard_map/ppermute | solution.py:70
  79.6 10.9 %collective-permute-start.2 = (bf16[2,2,3,32,1152]{4,3,2,1,0:T(8,128)(2,1)S(1)}, bf16[2,2,3,32,1152]{4,3,2,1,0:T(8,128)(2,1)}, u32[]{:S(2)}, u32[]{:S(2)}) collective-permute-start(bf16[2,2,3,32,1152]{4,3,2,1,0:T(8,128)(2,1)S(1)} %pad_maximum_fusion.2.refs_0_), channel_id=1, source_target_pairs={{0,4},{1,5},{2,6},{3,7},{4,0},{5,1},{6,2},{7,3},{8,12},{9,13},{10,... | collective-permute-start | bytes 2654216 | tf_op jit(solution)/shard_map/ppermute | solution.py:70
  83.1 7.5 %collective-permute-start.10 = (bf16[2,2,3,32,1152]{4,3,2,1,0:T(8,128)(2,1)}, bf16[2,2,3,32,1152]{4,3,2,1,0:T(8,128)(2,1)}, u32[]{:S(2)}, u32[]{:S(2)}) collective-permute-start(bf16[2,2,3,32,1152]{4,3,2,1,0:T(8,128)(2,1)} %collective-permute-done.9.refs_6_), channel_id=1, source_target_pairs={{0,4},{1,5},{2,6},{3,7},{4,0},{5,1},{6,2},{7,3},{8,12},{9,13},{10,... | collective-permute-start | bytes 2654216 | tf_op jit(solution)/shard_map/ppermute | solution.py:70
  83.1 7.5 %collective-permute-start.4 = (bf16[2,2,3,32,1152]{4,3,2,1,0:T(8,128)(2,1)}, bf16[2,2,3,32,1152]{4,3,2,1,0:T(8,128)(2,1)}, u32[]{:S(2)}, u32[]{:S(2)}) collective-permute-start(bf16[2,2,3,32,1152]{4,3,2,1,0:T(8,128)(2,1)} %collective-permute-done.3.refs_2_), channel_id=1, source_target_pairs={{0,4},{1,5},{2,6},{3,7},{4,0},{5,1},{6,2},{7,3},{8,12},{9,13},{10,... | collective-permute-start | bytes 2654216 | tf_op jit(solution)/shard_map/ppermute | solution.py:70
  150.1 3.3 collective-permute-start.15
  158.6 2.7 collective-permute-start.16
  183.1 207.5 %reduce-scatter.5.cloned.1.call-start = ((), (), s32[]{:S(2)}) async-start(), calls=%async_computation.4 | async-start | bytes 5242880 | tf_op jit(solution)/shard_map/reduce_scatter | solution.py:1035
  248.8 2.7 collective-permute-start.17
  283.8 25.5 %collective-permute-start.20 = (bf16[128,1024]{1,0:T(8,128)(2,1)}, bf16[128,1024]{1,0:T(8,128)(2,1)}, u32[]{:S(2)}, u32[]{:S(2)}) collective-permute-start(bf16[128,1024]{1,0:T(8,128)(2,1)} %get-tuple-element.176), channel_id=1, source_target_pairs={{0,3},{1,0},{2,1},{3,2},{4,7},{5,4},{6,5},{7,6},{8,11},{9,8},{10,9... | collective-permute-start | bytes 786440 | tf_op jit(solution)/shard_map/ppermute | solution.py:70
  286.9 23.4 %collective-permute-start.19 = (bf16[128,1024]{1,0:T(8,128)(2,1)}, bf16[128,1024]{1,0:T(8,128)(2,1)}, u32[]{:S(2)}, u32[]{:S(2)}) collective-permute-start(bf16[128,1024]{1,0:T(8,128)(2,1)} %get-tuple-element.177), channel_id=1, source_target_pairs={{0,2},{1,3},{2,0},{3,1},{4,6},{5,7},{6,4},{7,5},{8,10},{9,11},{10,... | collective-permute-start | bytes 786440 | tf_op jit(solution)/shard_map/ppermute | solution.py:70
  286.9 23.4 %collective-permute-start.18 = (bf16[128,1024]{1,0:T(8,128)(2,1)}, bf16[128,1024]{1,0:T(8,128)(2,1)}, u32[]{:S(2)}, u32[]{:S(2)}) collective-permute-start(bf16[128,1024]{1,0:T(8,128)(2,1)} %get-tuple-element.178), channel_id=1, source_target_pairs={{0,1},{1,2},{2,3},{3,0},{4,5},{5,6},{6,7},{7,4},{8,9},{9,10},{10,1... | collective-permute-start | bytes 786440 | tf_op jit(solution)/shard_map/ppermute | solution.py:70
  329.0 8.8 %collective-permute-start.22 = (bf16[4,4,64,1024]{3,2,1,0:T(8,128)(2,1)}, bf16[4,4,64,1024]{3,2,1,0:T(8,128)(2,1)}, u32[]{:S(2)}, u32[]{:S(2)}) collective-permute-start(bf16[4,4,64,1024]{3,2,1,0:T(8,128)(2,1)} %get-tuple-element.126), channel_id=1, source_target_pairs={{0,4},{1,5},{2,6},{3,7},{4,0},{5,1},{6,2},{7,3},{8,12},{9,13},{10,... | collective-permute-start | bytes 6291464 | tf_op jit(solution)/shard_map/ppermute | solution.py:70
  329.0 8.8 %collective-permute-start.21 = (bf16[4,4,64,1024]{3,2,1,0:T(8,128)(2,1)}, bf16[4,4,64,1024]{3,2,1,0:T(8,128)(2,1)}, u32[]{:S(2)}, u32[]{:S(2)}) collective-permute-start(bf16[4,4,64,1024]{3,2,1,0:T(8,128)(2,1)} %get-tuple-element.124.refs_6_), channel_id=1, source_target_pairs={{0,4},{1,5},{2,6},{3,7},{4,0},{5,1},{6,2},{7,3},{8,12},{9,13},{10,... | collective-permute-start | bytes 6291464 | tf_op jit(solution)/shard_map/ppermute | solution.py:70
  335.8 27.3 %collective-permute-start.24 = (bf16[512,1024]{1,0:T(8,128)(2,1)}, bf16[512,1024]{1,0:T(8,128)(2,1)S(1)}, u32[]{:S(2)}, u32[]{:S(2)}) collective-permute-start(bf16[512,1024]{1,0:T(8,128)(2,1)} %get-tuple-element.128.refs_0_), channel_id=1, source_target_pairs={{1,0},{2,1},{3,2},{4,3},{5,4},{6,5},{7,6},{8,7},{9,8},{10,9},{11,1... | collective-permute-start | bytes 3145736 | tf_op jit(solution)/shard_map/ppermute | solution.py:76
  344.6 31.4 %collective-permute-start.23 = (bf16[2,4,64,1024]{3,2,1,0:T(8,128)(2,1)}, bf16[2,4,64,1024]{3,2,1,0:T(8,128)(2,1)}, u32[]{:S(2)}, u32[]{:S(2)}) collective-permute-start(bf16[2,4,64,1024]{3,2,1,0:T(8,128)(2,1)} %get-tuple-element.129.refs_8_), channel_id=1, source_target_pairs={{0,8},{1,9},{2,10},{3,11},{4,12},{5,13},{6,14},{7,15},{8,0},{9,1},... | collective-permute-start | bytes 3145736 | tf_op jit(solution)/shard_map/ppermute | solution.py:70
  348.4 38.4 %collective-permute-start.25 = (bf16[2,4,64,1024]{3,2,1,0:T(8,128)(2,1)}, bf16[2,4,64,1024]{3,2,1,0:T(8,128)(2,1)}, u32[]{:S(2)}, u32[]{:S(2)}) collective-permute-start(bf16[2,4,64,1024]{3,2,1,0:T(8,128)(2,1)} %get-tuple-element.133.refs_10_), channel_id=1, source_target_pairs={{0,16},{1,17},{2,18},{3,19},{4,20},{5,21},{6,22},{7,23},{8,24},{9,... | collective-permute-start | bytes 3145736 | tf_op jit(solution)/shard_map/ppermute | solution.py:70
  369.1 26.8 %collective-permute-start.27 = (bf16[512,1024]{1,0:T(8,128)(2,1)}, bf16[512,1024]{1,0:T(8,128)(2,1)S(1)}, u32[]{:S(2)}, u32[]{:S(2)}) collective-permute-start(bf16[512,1024]{1,0:T(8,128)(2,1)} %get-tuple-element.136.refs_0_), channel_id=1, source_target_pairs={{1,0},{2,1},{3,2},{4,3},{5,4},{6,5},{7,6},{8,7},{9,8},{10,9},{11,1... | collective-permute-start | bytes 3145736 | tf_op jit(solution)/shard_map/ppermute | solution.py:76
  379.4 32.9 %collective-permute-start.34 = (bf16[4,64,1024]{2,1,0:T(8,128)(2,1)}, bf16[4,64,1024]{2,1,0:T(8,128)(2,1)}, u32[]{:S(2)}, u32[]{:S(2)}) collective-permute-start(bf16[4,64,1024]{2,1,0:T(8,128)(2,1)} %get-tuple-element.137.refs_0_.refs_1_), channel_id=1, source_target_pairs={{0,16},{1,17},{2,18},{3,19},{4,20},{5,21},{6,22},{7,23},{8,24},{9,... | collective-permute-start | bytes 1572872 | tf_op jit(solution)/shard_map/ppermute | solution.py:70
  390.2 24.3 %collective-permute-start.35 = (bf16[4,64,1024]{2,1,0:T(8,128)(2,1)}, bf16[4,64,1024]{2,1,0:T(8,128)(2,1)}, u32[]{:S(2)}, u32[]{:S(2)}) collective-permute-start(bf16[4,64,1024]{2,1,0:T(8,128)(2,1)} %get-tuple-element.139.refs_2_.refs_3_), channel_id=1, source_target_pairs={{0,8},{1,9},{2,10},{3,11},{4,12},{5,13},{6,14},{7,15},{8,0},{9,1},... | collective-permute-start | bytes 1572872 | tf_op jit(solution)/shard_map/ppermute | solution.py:70
  390.5 6.2 %collective-permute-start.28 = (f32[2,2,4,384]{3,2,1,0:T(4,128)S(1)}, f32[2,2,4,384]{3,2,1,0:T(4,128)S(1)}, u32[]{:S(2)}, u32[]{:S(2)}) collective-permute-start(f32[2,2,4,384]{3,2,1,0:T(4,128)S(1)} %dynamic-slice_bitcast_fusion.9), channel_id=1, source_target_pairs={{0,4},{1,5},{2,6},{3,7},{4,0},{5,1},{6,2},{7,3},{8,12},{9,13},{10,... | collective-permute-start | bytes 73736 | tf_op jit(solution)/shard_map/ppermute | solution.py:70
  396.7 15.0 %collective-permute-start.29 = (f32[2,4,384]{2,1,0:T(4,128)S(1)}, f32[2,4,384]{2,1,0:T(4,128)S(1)}, u32[]{:S(2)}, u32[]{:S(2)}) collective-permute-start(f32[2,4,384]{2,1,0:T(4,128)S(1)} %dynamic-slice_bitcast_fusion.10), channel_id=1, source_target_pairs={{0,8},{1,9},{2,10},{3,11},{4,12},{5,13},{6,14},{7,15},{8,0},{9,1},... | collective-permute-start | bytes 36872 | tf_op jit(solution)/shard_map/ppermute | solution.py:70
  400.6 18.9 %collective-permute-start.41 = (bf16[2,32,2048]{2,1,0:T(8,128)(2,1)S(1)}, bf16[2,32,2048]{2,1,0:T(8,128)(2,1)S(1)}, u32[]{:S(2)}, u32[]{:S(2)}) collective-permute-start(bf16[2,32,2048]{2,1,0:T(8,128)(2,1)S(1)} %get-tuple-element.168), channel_id=1, source_target_pairs={{0,3},{1,0},{2,1},{3,2},{4,7},{5,4},{6,5},{7,6},{8,11},{9,8},{10,9... | collective-permute-start | bytes 786440 | tf_op jit(solution)/shard_map/ppermute | solution.py:70
  403.4 22.3 %collective-permute-start.40 = (bf16[2,32,2048]{2,1,0:T(8,128)(2,1)S(1)}, bf16[2,32,2048]{2,1,0:T(8,128)(2,1)S(1)}, u32[]{:S(2)}, u32[]{:S(2)}) collective-permute-start(bf16[2,32,2048]{2,1,0:T(8,128)(2,1)S(1)} %get-tuple-element.169), channel_id=1, source_target_pairs={{0,2},{1,3},{2,0},{3,1},{4,6},{5,7},{6,4},{7,5},{8,10},{9,11},{10,... | collective-permute-start | bytes 786440 | tf_op jit(solution)/shard_map/ppermute | solution.py:70
  411.7 14.0 %collective-permute-start.39 = (bf16[2,32,2048]{2,1,0:T(8,128)(2,1)S(1)}, bf16[2,32,2048]{2,1,0:T(8,128)(2,1)S(1)}, u32[]{:S(2)}, u32[]{:S(2)}) collective-permute-start(bf16[2,32,2048]{2,1,0:T(8,128)(2,1)S(1)} %get-tuple-element.170), channel_id=1, source_target_pairs={{0,1},{1,2},{2,3},{3,0},{4,5},{5,6},{6,7},{7,4},{8,9},{9,10},{10,1... | collective-permute-start | bytes 786440 | tf_op jit(solution)/shard_map/ppermute | solution.py:70
  412.3 7.2 %collective-permute-start.30 = (f32[4,384]{1,0:T(4,128)S(1)}, f32[4,384]{1,0:T(4,128)S(1)}, u32[]{:S(2)}, u32[]{:S(2)}) collective-permute-start(f32[4,384]{1,0:T(4,128)S(1)} %fusion.34), channel_id=1, source_target_pairs={{0,16},{1,17},{2,18},{3,19},{4,20},{5,21},{6,22},{7,23},{8,24},{9,... | collective-permute-start | bytes 18440 | tf_op jit(solution)/shard_map/ppermute | solution.py:70
  416.1 20.4 %collective-permute-start.38 = (bf16[4,32,1024]{2,1,0:T(8,128)(2,1)S(1)}, bf16[4,32,1024]{2,1,0:T(8,128)(2,1)S(1)}, u32[]{:S(2)}, u32[]{:S(2)}) collective-permute-start(bf16[4,32,1024]{2,1,0:T(8,128)(2,1)S(1)} %get-tuple-element.172), channel_id=1, source_target_pairs={{0,3},{1,0},{2,1},{3,2},{4,7},{5,4},{6,5},{7,6},{8,11},{9,8},{10,9... | collective-permute-start | bytes 786440 | tf_op jit(solution)/shard_map/ppermute | solution.py:70
  419.5 17.1 %collective-permute-start.36 = (bf16[4,32,1024]{2,1,0:T(8,128)(2,1)S(1)}, bf16[4,32,1024]{2,1,0:T(8,128)(2,1)S(1)}, u32[]{:S(2)}, u32[]{:S(2)}) collective-permute-start(bf16[4,32,1024]{2,1,0:T(8,128)(2,1)S(1)} %get-tuple-element.174), channel_id=1, source_target_pairs={{0,1},{1,2},{2,3},{3,0},{4,5},{5,6},{6,7},{7,4},{8,9},{9,10},{10,1... | collective-permute-start | bytes 786440 | tf_op jit(solution)/shard_map/ppermute | solution.py:70
  419.5 28.5 %collective-permute-start.37 = (bf16[4,32,1024]{2,1,0:T(8,128)(2,1)S(1)}, bf16[4,32,1024]{2,1,0:T(8,128)(2,1)S(1)}, u32[]{:S(2)}, u32[]{:S(2)}) collective-permute-start(bf16[4,32,1024]{2,1,0:T(8,128)(2,1)S(1)} %get-tuple-element.175), channel_id=1, source_target_pairs={{0,2},{1,3},{2,0},{3,1},{4,6},{5,7},{6,4},{7,5},{8,10},{9,11},{10,... | collective-permute-start | bytes 786440 | tf_op jit(solution)/shard_map/ppermute | solution.py:70
  425.7 25.4 %collective-permute-start.26 = (bf16[512,1024]{1,0:T(8,128)(2,1)S(1)}, bf16[512,1024]{1,0:T(8,128)(2,1)S(1)}, u32[]{:S(2)}, u32[]{:S(2)}) collective-permute-start(bf16[512,1024]{1,0:T(8,128)(2,1)S(1)} %get-tuple-element.142), channel_id=1, source_target_pairs={{0,4},{1,5},{2,6},{3,7},{4,0},{5,1},{6,2},{7,3},{8,12},{9,13},{10,... | collective-permute-start | bytes 3145736 | tf_op jit(solution)/shard_map/ppermute | solution.py:70
  425.7 22.5 %collective-permute-start.31 = (f32[384]{0:T(512)S(1)}, f32[384]{0:T(512)S(1)}, u32[]{:S(2)}, u32[]{:S(2)}) collective-permute-start(f32[384]{0:T(512)S(1)} %get-tuple-element.162), channel_id=1, source_target_pairs={{0,1},{1,2},{2,3},{3,0},{4,5},{5,6},{6,7},{7,4},{8,9},{9,10},{10,1... | collective-permute-start | bytes 4616 | tf_op jit(solution)/shard_map/ppermute | solution.py:70
  436.6 11.7 %collective-permute-start.33 = (f32[384]{0:T(512)S(1)}, f32[384]{0:T(512)S(1)}, u32[]{:S(2)}, u32[]{:S(2)}) collective-permute-start(f32[384]{0:T(512)S(1)} %get-tuple-element.163), channel_id=1, source_target_pairs={{0,3},{1,0},{2,1},{3,2},{4,7},{5,4},{6,5},{7,6},{8,11},{9,8},{10,9... | collective-permute-start | bytes 4616 | tf_op jit(solution)/shard_map/ppermute | solution.py:70
  436.6 11.7 %collective-permute-start.32 = (f32[384]{0:T(512)S(1)}, f32[384]{0:T(512)S(1)}, u32[]{:S(2)}, u32[]{:S(2)}) collective-permute-start(f32[384]{0:T(512)S(1)} %get-tuple-element.164), channel_id=1, source_target_pairs={{0,2},{1,3},{2,0},{3,1},{4,6},{5,7},{6,4},{7,5},{8,10},{9,11},{10,... | collective-permute-start | bytes 4616 | tf_op jit(solution)/shard_map/ppermute | solution.py:70
  448.1 2.8 collective-permute-start.42
  (91 other events, 542.0 us)
Sparse Core Ops, SparseCore 0:
  34.9 113.8 all-gather.5
  152.1 74.8 all-gather.3
  230.0 51.2 reduce-scatter.2
  284.4 52.6 reduce-scatter.4

commit v5 on v4

--- a/solution.py
+++ b/solution.py
@@ -1081,7 +1081,7 @@
     up_rows_both = after(up_plane, *nears).reshape(2, nz, up_rows, ff_core).swapaxes(0, 1)
     returned = grid.to_earlier(returned)
     branch_kept, branch_given = branch_terms(hidden, down_mat, nears)
-    joined_far = [far_sums(part, joined_near[part], returned, branch_kept) for part in range(2)]
+    joined_far = [far_sums(part, joined_near[part], returned) for part in range(2)]
     both = [half.reshape(4, nz // 2, -1, width) for half in joined_far]
     both = jnp.concatenate(both, axis=1)
 

time: 464 us -> 464 us (level)
  waiting for transfers between devices: 106 us -> 98.8 us
  starting transfers between devices: 71.6 us -> 78.2 us
    ppermute x39, waiting for transfers between devices: 42.3 us -> 35.5 us  [shift(): lax.ppermute(block, ALL, list(zip(places.ravel().tolist(), ahead.ravel()....]
    ppermute x39, starting transfers between devices: 60.1 us -> 66.7 us  [shift(): lax.ppermute(block, ALL, list(zip(places.ravel().tolist(), ahead.ravel()....]
  transfers between devices with their start and end apart: 47 -> 47, of which waited for: 18 -> 16; matrix products, arithmetic and copies ran while one was open for 7% -> 7% of each run, Pallas kernels for 44% -> 44%
where the time goes in v5:
time: 464 us; the launch traced here: 459 us
  Pallas kernels  202 us (44%)
  waiting for transfers between devices  98.8 us (21%)
  starting transfers between devices  78.2 us (17%)
  local copies, waits for them, and re-layouts  41 us (9%)
  other arithmetic  22.1 us (5%)
  between operations  16 us (3%)
    ppermute x39, starting transfers between devices, shift(): lax.ppermute(block, ALL, list(zip(places.ravel().tolist(), ahead.ravel()....  66.7 us
    all_gather x1, waiting for transfers between devices, on_device(): lax.all_gather(after(down_weight, *joined_line[1:]), lines, axis=0, tiled...  36.1 us
    ppermute x39, waiting for transfers between devices, shift(): lax.ppermute(block, ALL, list(zip(places.ravel().tolist(), ahead.ravel()....  35.5 us
    pallas_call x2, Pallas kernels, attend_back(): pl.pallas_call(functools.partial(attend_back_kernel, first_pair=first_pai...  34 us
    unnamed x197, local copies, waits for them, and re-layouts  32.4 us
    pallas_call x1, Pallas kernels, attend(): pl.pallas_call(attend_kernel, grid=(steps,), in_specs=[pl.BlockSpec((tok_...  21.3 us
    pallas_call x3, Pallas kernels, project(): pl.pallas_call(functools.partial(projection_kernel, kinds, len(others)),...  19.3 us
    pallas_call x3, Pallas kernels, chunk_back(): pl.pallas_call(functools.partial(chunk_kernel, len(pairs), arrived is not...  18.8 us
  transfers between devices with their start and end apart: 47, of which 16 were waited for; matrix products, arithmetic and copies ran while one was open for 7% of the time, Pallas kernels for 44%

profile of v5, /device:TPU:0, one launch (start us, length us, event | category | flops | bytes accessed | tf_op | source)
XLA Modules:
  0.0 459.3 jit_solution(2316624363806216091)
XLA Ops:
  10.7 5.0 %collective-permute-start.6 = (bf16[3,32,1152]{2,1,0:T(8,128)(2,1)}, bf16[3,32,1152]{2,1,0:T(8,128)(2,1)S(1)}, u32[]{:S(2)}, u32[]{:S(2)}) collective-permute-start(bf16[3,32,1152]{2,1,0:T(8,128)(2,1)} %shard_map.272), channel_id=1, source_target_pairs={{0,3},{1,0},{2,1},{3,2},{4,7},{5,4},{6,5},{7,6},{8,11},{9,8},{10,9... | collective-permute-start | bytes 663560 | tf_op jit(solution)/shard_map/ppermute | solution.py:70
  21.9 12.8 %collective-permute-done.5.refs_2_ = bf16[3,32,1152]{2,1,0:T(8,128)(2,1)S(1)} collective-permute-done((bf16[3,32,1152]{2,1,0:T(8,128)(2,1)}, bf16[3,32,1152]{2,1,0:T(8,128)(2,1)S(1)}, u32[]{:S(2)}, u32[]{:S(2)}) %collective-permute-start.5) | collective-permute-done | bytes 221216 | tf_op jit(solution)/shard_map/ppermute | solution.py:70
  40.8 3.9 collective-permute-start.11
  44.7 5.1 %collective-permute-done.7 = bf16[2,3,32,1152]{3,2,1,0:T(8,128)(2,1)S(1)} collective-permute-done((bf16[2,3,32,1152]{3,2,1,0:T(8,128)(2,1)S(1)}, bf16[2,3,32,1152]{3,2,1,0:T(8,128)(2,1)S(1)}, u32[]{:S(2)}, u32[]{:S(2)}) %collective-permute-start.7) | collective-permute-done | bytes 442400 | tf_op jit(solution)/shard_map/ppermute | solution.py:70
  51.6 3.3 collective-permute-done.1
  56.0 17.7 %collective-permute-done.11.tokens.refs_4_ = bf16[512,1024]{1,0:T(8,128)(2,1)} collective-permute-done((bf16[512,1024]{1,0:T(8,128)(2,1)S(1)}, bf16[512,1024]{1,0:T(8,128)(2,1)}, u32[]{:S(2)}, u32[]{:S(2)}) %collective-permute-start.11) | collective-permute-done | bytes 1048608 | tf_op jit(solution)/shard_map/ppermute | solution.py:73
  73.8 4.8 %collective-permute-start.12 = (bf16[512,1024]{1,0:T(8,128)(2,1)}, bf16[512,1024]{1,0:T(8,128)(2,1)S(1)}, u32[]{:S(2)}, u32[]{:S(2)}) collective-permute-start(bf16[512,1024]{1,0:T(8,128)(2,1)} %collective-permute-done.11.tokens.refs_4_), channel_id=1, source_target_pairs={{0,1},{1,2},{2,3},{3,4},{4,5},{5,6},{6,7},{7,8},{8,9},{9,10},{10,1... | collective-permute-start | bytes 3145736 | tf_op jit(solution)/shard_map/ppermute | solution.py:73
  79.7 3.4 collective-permute-done.9.refs_6_
  85.1 2.4 select_convert_fusion.1.key_side
  90.5 7.4 %shard_map.273 = (bf16[32,32,1024]{2,1,0:T(8,128)(2,1)}, bf16[32,32,1024]{2,1,0:T(8,128)(2,1)}, bf16[32,32,1024]{2,1,0:T(8,128)(2,1)}, bf16[32,32,128]{2,1,0:T(8,128)(2,1)S(1)}) custom-call(s32[32]{0:T(128)S(1)} %stack.305.places, bf16[2,2,3,32,1152]{4,3,2,1,0:T(8,128)(2,1)S(1)} %pad_maximum_fusion.2.refs_0_, ...), custom_call_target="tpu_custom_call" | custom-call | flops 1 | bytes 1 | tf_op jit(solution)/shard_map/pallas_call | solution.py:138
  103.2 7.1 %shard_map.275 = (bf16[1536,1024]{1,0:T(8,128)(2,1)}, f32[512,128]{1,0:T(8,128)S(1)}, bf16[1536,1024]{1,0:T(8,128)(2,1)}, bf16[1536,1024]{1,0:T(8,128)(2,1)}, bf16[512,1024]{1,0:T(8,128)(2,1)S(1)}) custom-call(bf16[512,1024]{1,0:T(8,128)(2,1)S(1)} %copy-done.1, f32[1,1024]{1,0:T(1,128)S(1)} %copy-done.43, f32[1,1024]{1,0:T(1,128)S(1)} %copy-done.45, ...), custom_call_target="tpu_custom_call" | custom-call | flops 1 | bytes 1 | tf_op jit(solution)/shard_map/pallas_call | solution.py:847
  111.0 6.3 %shard_map.277 = (bf16[1536,1024]{1,0:T(8,128)(2,1)}, f32[512,128]{1,0:T(8,128)S(1)}, bf16[1536,1024]{1,0:T(8,128)(2,1)}, bf16[1536,1024]{1,0:T(8,128)(2,1)}) custom-call(bf16[512,1024]{1,0:T(8,128)(2,1)} %collective-permute-done.11.tokens.refs_4_, f32[1,1024]{1,0:T(1,128)S(1)} %copy-done.44, ...), custom_call_target="tpu_custom_call", output_to_operand_aliasing={{0}: (7, {}), {2}: (8, {}), {3}: (9, {})} | custom-call | flops 1 | bytes 1 | tf_op jit(solution)/shard_map/pallas_call | solution.py:847
  117.3 6.0 %shard_map.278 = (bf16[1536,1024]{1,0:T(8,128)(2,1)}, f32[512,128]{1,0:T(8,128)S(1)}, bf16[1536,1024]{1,0:T(8,128)(2,1)}, bf16[1536,1024]{1,0:T(8,128)(2,1)}) custom-call(bf16[512,1024]{1,0:T(8,128)(2,1)S(1)} %collective-permute-done.12.tokens.refs_4_, f32[1,1024]{1,0:T(1,128)S(1)} %copy-done.44, ...), custom_call_target="tpu_custom_call", output_to_operand_aliasing={{0}: (7, {}), {2}: (8, {}), {3}: (9, {})} | custom-call | flops 1 | bytes 1 | tf_op jit(solution)/shard_map/pallas_call | solution.py:847
  124.0 21.3 %shard_map.280 = (bf16[512,1024]{1,0:T(8,128)(2,1)S(1)}, f32[512,128]{1,0:T(8,128)S(1)}) custom-call(bf16[512,1024]{1,0:T(8,128)(2,1)} %copy-done.7, bf16[1536,1024]{1,0:T(8,128)(2,1)} %get-tuple-element.102.key, bf16[1536,1024]{1,0:T(8,128)(2,1)} %get-tuple-element.103.value, bf16[512,128]{1,0:T(8,128)(2,1)S(1)} %select_convert_fusion.2.query_side, ...), custom_call_target="tpu_custom_call" | custom-call | flops 1 | bytes 1 | tf_op jit(solution)/shard_map/pallas_call | solution.py:604
  146.0 2.7 all-gather.6.cloned.1.call-done
  151.0 2.4 collective-permute-done.15
  159.0 2.3 collective-permute-done.16.other
  161.3 11.6 %shard_map.283 = (bf16[1024,2048]{1,0:T(8,128)(2,1)}, bf16[1024,2048]{1,0:T(8,128)(2,1)}) custom-call(s32[1]{0:T(128)} %bitcast.66.core, bf16[512,1024]{1,0:T(8,128)(2,1)S(1)} %add_convert_fusion.own, bf16[512,1024]{1,0:T(8,128)(2,1)S(1)} %collective-permute-done.16.other, bf16[16,5,32,1024]{3,2,1,0:T(8,128)(2,1)} %bitcast.226, ...), custom_call_target="tpu_custom_call" | custom-call | flops 1 | bytes 1 | tf_op jit(solution)/shard_map/pallas_call | solution.py:771
  172.9 9.6 %shard_map.285 = (bf16[2048,1024]{1,0:T(8,128)(2,1)}, f32[1,1024]{1,0:T(1,128)S(1)}) custom-call(bf16[1024,2048]{1,0:T(8,128)(2,1)} %get-tuple-element.109.left.refs_1_.hidden, bf16[1024,1024]{1,0:T(8,128)(2,1)S(1)} %copy-done.4), custom_call_target="tpu_custom_call" | custom-call | flops 1 | bytes 1 | tf_op jit(solution)/shard_map/pallas_call | solution.py:252
  183.3 2.2 copy-done.2
  185.5 5.4 %shard_map.288 = bf16[32,32,2048]{2,1,0:T(8,128)(2,1)} custom-call(s32[32]{0:T(128)S(1)} %shard_map.287.places, bf16[16,5,32,1024]{3,2,1,0:T(8,128)(2,1)} %bitcast.228), custom_call_target="tpu_custom_call" | custom-call | flops 1 | bytes 1 | tf_op jit(solution)/shard_map/pallas_call | solution.py:138
  190.9 36.1 %all-gather.4.cloned.1.call-done.down = bf16[2048,1024]{1,0:T(8,128)(2,1)} async-done(((bf16[128,1024]{1,0:T(8,128)(2,1)}), bf16[2048,1024]{1,0:T(8,128)(2,1)}) %all-gather.4.cloned.1.call-update) | async-done | bytes 4194320 | tf_op jit(solution)/shard_map/all_gather | solution.py:985
  227.0 8.7 %shard_map.286 = (bf16[1024,2048]{1,0:T(8,128)(2,1)}, f32[1,2048]{1,0:T(1,128)S(1)}) custom-call(bf16[1024,1024]{1,0:T(8,128)(2,1)S(1)} %copy-done.4, bf16[2048,1024]{1,0:T(8,128)(2,1)} %all-gather.4.cloned.1.call-done.down, bf16[1024,2048]{1,0:T(8,128)(2,1)} %get-tuple-element.111.slope, bf16[2048,1024]{1,0:T(8,128)(2,1)} %get-tuple-element.112.refs_0_), custom_call_target="tpu_custom_call" | custom-call | flops 1 | bytes 1 | tf_op jit(solution)/shard_map/pallas_call | solution.py:797
  235.8 5.0 %shard_map.289.refs_0_ = bf16[512,1024]{1,0:T(8,128)(2,1)S(1)} custom-call(bf16[1024,2048]{1,0:T(8,128)(2,1)} %get-tuple-element.113.left.right.pre_change, bf16[1024,2048]{1,0:T(8,128)(2,1)} %bitcast.229), custom_call_target="tpu_custom_call" | custom-call | flops 1 | bytes 1 | tf_op jit(solution)/shard_map/pallas_call | solution.py:316
  240.8 8.0 %shard_map.290.refs_0_ = bf16[1024,2048]{1,0:T(8,128)(2,1)} custom-call(bf16[512,1024]{1,0:T(8,128)(2,1)S(1)} %copy-done.10, bf16[512,1024]{1,0:T(8,128)(2,1)S(1)} %copy-done.20, bf16[1024,2048]{1,0:T(8,128)(2,1)} %get-tuple-element.113.left.right.pre_change, bf16[512,1024]{1,0:T(8,128)(2,1)S(1)} %shard_map.289.refs_0_), custom_call_target="tpu_custom_call" | custom-call | flops 1 | bytes 1 | tf_op jit(solution)/shard_map/pallas_call | solution.py:275
  249.0 2.6 collective-permute-done.17.arrived
  251.6 9.4 %shard_map.291 = (f32[512,1024]{1,0:T(8,128)}, bf16[512,1024]{1,0:T(8,128)(2,1)S(1)}, bf16[512,1024]{1,0:T(8,128)(2,1)S(1)}, f32[1,1024]{1,0:T(1,128)S(1)}, f32[...) custom-call(bf16[1024,2048]{1,0:T(8,128)(2,1)} %get-tuple-element.113.left.right.pre_change, bf16[1024,2048]{1,0:T(8,128)(2,1)} %bitcast.230, ...), custom_call_target="tpu_custom_call" | custom-call | flops 1 | bytes 1 | tf_op jit(solution)/shard_map/pallas_call | solution.py:417
  264.7 16.9 %shard_map.292 = (bf16[512,1024]{1,0:T(8,128)(2,1)S(1)}, bf16[1536,1024]{1,0:T(8,128)(2,1)}, bf16[1536,1024]{1,0:T(8,128)(2,1)}) custom-call(bf16[512,1024]{1,0:T(8,128)(2,1)} %copy-done.7, bf16[1536,1024]{1,0:T(8,128)(2,1)} %get-tuple-element.102.key, bf16[1536,1024]{1,0:T(8,128)(2,1)} %get-tuple-element.103.value, bf16[512,1024]{1,0:T(8,128)(2,1)} %copy-done.14, ...), custom_call_target="tpu_custom_call" | custom-call | flops 1 | bytes 1 | tf_op jit(solution)/shard_map/pallas_call | solution.py:692
  283.8 3.1 collective-permute-start.20
  292.1 17.2 %shard_map.295 = (bf16[512,1024]{1,0:T(8,128)(2,1)S(1)}, bf16[1536,1024]{1,0:T(8,128)(2,1)}, bf16[1536,1024]{1,0:T(8,128)(2,1)}) custom-call(bf16[512,1024]{1,0:T(8,128)(2,1)} %copy-done.7, bf16[1536,1024]{1,0:T(8,128)(2,1)} %get-tuple-element.102.key, ...), custom_call_target="tpu_custom_call", output_to_operand_aliasing={{0}: (9, {}), {1}: (10, {}), {2}: (11, {})} | custom-call | flops 1 | bytes 1 | tf_op jit(solution)/shard_map/pallas_call | solution.py:692
  310.2 2.0 shard_map.296.refs_0_
  313.3 15.6 %shard_map.297 = (bf16[4,4,64,1024]{3,2,1,0:T(8,128)(2,1)}, bf16[4,4,64,1024]{3,2,1,0:T(8,128)(2,1)}, bf16[4,4,64,1024]{3,2,1,0:T(8,128)(2,1)}, bf16[4,4,64,1024...) custom-call(s32[4]{0:T(128)S(1)} %pad_add_fusion.blocks, s32[1]{0:T(128)} %bitcast.66.core, ...), custom_call_target="tpu_custom_call" | custom-call | flops 1 | bytes 1 | tf_op jit(solution)/shard_map/pallas_call | solution.py:468
  329.5 5.6 %shard_map.298 = (bf16[512,1024]{1,0:T(8,128)(2,1)}, f32[1,1024]{1,0:T(1,128)S(1)}, f32[1,1024]{1,0:T(1,128)S(1)}) custom-call(bf16[1536,1024]{1,0:T(8,128)(2,1)} %get-tuple-element.120.key.refs_0_, bf16[1536,1024]{1,0:T(8,128)(2,1)} %get-tuple-element.121.value.refs_1_, bf16[1024,1024]{1,0:T(8,128)(2,1)} %bitcast.202, bf16[1024,1024]{1,0:T(8,128)(2,1)} %bitcast.222, ...), custom_call_target="tpu_custom_call" | custom-call | flops 1 | bytes 1 | tf_op jit(solution)/shard_map/pallas_call | solution.py:374
  337.9 5.7 %shard_map.299 = (bf16[2,4,64,1024]{3,2,1,0:T(8,128)(2,1)}, bf16[2,4,64,1024]{3,2,1,0:T(8,128)(2,1)S(1)}, bf16[2,4,64,1024]{3,2,1,0:T(8,128)(2,1)}, bf16[2,4,64,1024]{3,2,1,0:T(8,128)(2,1)}) custom-call(bf16[2,2,4,64,1024]{4,3,2,1,0:T(8,128)(2,1)} %bitcast.237, bf16[2,2,4,64,1024]{4,3,2,1,0:T(8,128)(2,1)} %bitcast.112.arrived_ahead, ...), custom_call_target="tpu_custom_call" | custom-call | flops 1 | bytes 1 | tf_op jit(solution)/shard_map/pallas_call | solution.py:505
  344.6 3.8 collective-permute-start.23
  350.4 7.3 %shard_map.300 = (f32[512,1024]{1,0:T(8,128)}, f32[1,1024]{1,0:T(1,128)S(1)}, f32[1,1024]{1,0:T(1,128)S(1)}) custom-call(bf16[1536,1024]{1,0:T(8,128)(2,1)} %get-tuple-element.120.key.refs_0_, bf16[1536,1024]{1,0:T(8,128)(2,1)} %get-tuple-element.121.value.refs_1_, bf16[512,1024]{1,0:T(8,128)(2,1)S(1)} %get-tuple-element.119.query.refs_2_, ...), custom_call_target="tpu_custom_call" | custom-call | flops 1 | bytes 1 | tf_op jit(solution)/shard_map/pallas_call | solution.py:374
  358.8 4.3 collective-permute-done.24.refs_6_
  363.2 5.9 %shard_map.301 = (bf16[512,1024]{1,0:T(8,128)(2,1)}, f32[1,1024]{1,0:T(1,128)S(1)}, f32[1,1024]{1,0:T(1,128)S(1)}) custom-call(bf16[1536,1024]{1,0:T(8,128)(2,1)} %get-tuple-element.120.key.refs_0_, bf16[1536,1024]{1,0:T(8,128)(2,1)} %get-tuple-element.121.value.refs_1_, bf16[1024,1024]{1,0:T(8,128)(2,1)} %bitcast.204, bf16[1024,1024]{1,0:T(8,128)(2,1)} %bitcast.224, ...), custom_call_target="tpu_custom_call" | custom-call | flops 1 | bytes 1 | tf_op jit(solution)/shard_map/pallas_call | solution.py:374
  377.2 2.1 shard_map.302
  379.4 7.5 %collective-permute-start.34 = (bf16[4,64,1024]{2,1,0:T(8,128)(2,1)}, bf16[4,64,1024]{2,1,0:T(8,128)(2,1)}, u32[]{:S(2)}, u32[]{:S(2)}) collective-permute-start(bf16[4,64,1024]{2,1,0:T(8,128)(2,1)} %get-tuple-element.137.refs_0_.refs_1_), channel_id=1, source_target_pairs={{0,16},{1,17},{2,18},{3,19},{4,20},{5,21},{6,22},{7,23},{8,24},{9,... | collective-permute-start | bytes 1572872 | tf_op jit(solution)/shard_map/ppermute | solution.py:70
  388.1 2.2 shard_map.303
  396.7 3.8 collective-permute-start.29
  400.6 2.8 collective-permute-start.41
  408.0 6.2 %collective-permute-start.38 = (bf16[4,32,1024]{2,1,0:T(8,128)(2,1)S(1)}, bf16[4,32,1024]{2,1,0:T(8,128)(2,1)S(1)}, u32[]{:S(2)}, u32[]{:S(2)}) collective-permute-start(bf16[4,32,1024]{2,1,0:T(8,128)(2,1)S(1)} %get-tuple-element.172), channel_id=1, source_target_pairs={{0,3},{1,0},{2,1},{3,2},{4,7},{5,4},{6,5},{7,6},{8,11},{9,8},{10,9... | collective-permute-start | bytes 786440 | tf_op jit(solution)/shard_map/ppermute | solution.py:70
  414.2 2.6 collective-permute-start.37
  418.5 8.3 %shard_map.304 = (f32[512,1024]{1,0:T(8,128)}, bf16[512,1024]{1,0:T(8,128)(2,1)S(1)}) custom-call(bf16[1024,2048]{1,0:T(8,128)(2,1)} %get-tuple-element.109.left.refs_1_.hidden, bf16[2048,1024]{1,0:T(8,128)(2,1)} %all-gather.4.cloned.1.call-done.down, bf16[4,64,1024]{2,1,0:T(8,128)(2,1)} %get-tuple-element.137.refs_0_.refs_1_, ...), custom_call_target="tpu_custom_call" | custom-call | flops 1 | bytes 1 | tf_op jit(solution)/shard_map/pallas_call | solution.py:344
  427.0 6.0 %collective-permute-start.31 = (f32[384]{0:T(512)S(1)}, f32[384]{0:T(512)S(1)}, u32[]{:S(2)}, u32[]{:S(2)}) collective-permute-start(f32[384]{0:T(512)S(1)} %get-tuple-element.162), channel_id=1, source_target_pairs={{0,1},{1,2},{2,3},{3,0},{4,5},{5,6},{6,7},{7,4},{8,9},{9,10},{10,1... | collective-permute-start | bytes 4616 | tf_op jit(solution)/shard_map/ppermute | solution.py:70
  433.0 13.2 %collective-permute-start.32 = (f32[384]{0:T(512)S(1)}, f32[384]{0:T(512)S(1)}, u32[]{:S(2)}, u32[]{:S(2)}) collective-permute-start(f32[384]{0:T(512)S(1)} %get-tuple-element.164), channel_id=1, source_target_pairs={{0,2},{1,3},{2,0},{3,1},{4,6},{5,7},{6,4},{7,5},{8,10},{9,11},{10,... | collective-permute-start | bytes 4616 | tf_op jit(solution)/shard_map/ppermute | solution.py:70
  (373 shorter events, 88.7 us)
Async XLA Ops:
  7.2 141.6 %all-gather.6.cloned.1.call-start = ((), (), s32[]{:S(2)}) async-start(), calls=%async_computation.5 | async-start | bytes 5570560 | tf_op jit(solution)/shard_map/all_gather | solution.py:984
  10.7 11.2 %collective-permute-start.6 = (bf16[3,32,1152]{2,1,0:T(8,128)(2,1)}, bf16[3,32,1152]{2,1,0:T(8,128)(2,1)S(1)}, u32[]{:S(2)}, u32[]{:S(2)}) collective-permute-start(bf16[3,32,1152]{2,1,0:T(8,128)(2,1)} %shard_map.272), channel_id=1, source_target_pairs={{0,3},{1,0},{2,1},{3,2},{4,7},{5,4},{6,5},{7,6},{8,11},{9,8},{10,9... | collective-permute-start | bytes 663560 | tf_op jit(solution)/shard_map/ppermute | solution.py:70
  15.7 19.0 %collective-permute-start.5 = (bf16[3,32,1152]{2,1,0:T(8,128)(2,1)}, bf16[3,32,1152]{2,1,0:T(8,128)(2,1)S(1)}, u32[]{:S(2)}, u32[]{:S(2)}) collective-permute-start(bf16[3,32,1152]{2,1,0:T(8,128)(2,1)} %shard_map.272), channel_id=1, source_target_pairs={{0,2},{1,3},{2,0},{3,1},{4,6},{5,7},{6,4},{7,5},{8,10},{9,11},{10,... | collective-permute-start | bytes 663560 | tf_op jit(solution)/shard_map/ppermute | solution.py:70
  15.7 19.0 %collective-permute-start = (bf16[3,32,1152]{2,1,0:T(8,128)(2,1)}, bf16[3,32,1152]{2,1,0:T(8,128)(2,1)S(1)}, u32[]{:S(2)}, u32[]{:S(2)}) collective-permute-start(bf16[3,32,1152]{2,1,0:T(8,128)(2,1)} %shard_map.272), channel_id=1, source_target_pairs={{0,1},{1,2},{2,3},{3,0},{4,5},{5,6},{6,7},{7,4},{8,9},{9,10},{10,1... | collective-permute-start | bytes 663560 | tf_op jit(solution)/shard_map/ppermute | solution.py:70
  17.7 1.4 collective-permute-start.14
  34.8 192.2 %all-gather.4.cloned.1.call-start = ((), (), s32[]{:S(2)}) async-start(), calls=%async_computation.2 | async-start | bytes 4456448 | tf_op jit(solution)/shard_map/all_gather | solution.py:985
  35.5 246.0 %reduce-scatter.3.cloned.1.call-start = ((), (), s32[]{:S(2)}) async-start(), calls=%async_computation.3 | async-start | bytes 5242880 | tf_op jit(solution)/shard_map/reduce_scatter | solution.py:1031
  36.4 13.4 %collective-permute-start.7 = (bf16[2,3,32,1152]{3,2,1,0:T(8,128)(2,1)S(1)}, bf16[2,3,32,1152]{3,2,1,0:T(8,128)(2,1)S(1)}, u32[]{:S(2)}, u32[]{:S(2)}) collective-permute-start(bf16[2,3,32,1152]{3,2,1,0:T(8,128)(2,1)S(1)} %get-tuple-element.183), channel_id=1, source_target_pairs={{0,16},{1,17},{2,18},{3,19},{4,20},{5,21},{6,22},{7,23},{8,24},{9,... | collective-permute-start | bytes 1327112 | tf_op jit(solution)/shard_map/ppermute | solution.py:70
  38.0 16.8 %collective-permute-start.1 = (bf16[2,3,32,1152]{3,2,1,0:T(8,128)(2,1)S(1)}, bf16[2,3,32,1152]{3,2,1,0:T(8,128)(2,1)S(1)}, u32[]{:S(2)}, u32[]{:S(2)}) collective-permute-start(bf16[2,3,32,1152]{3,2,1,0:T(8,128)(2,1)S(1)} %get-tuple-element.185), channel_id=1, source_target_pairs={{0,8},{1,9},{2,10},{3,11},{4,12},{5,13},{6,14},{7,15},{8,0},{9,1},... | collective-permute-start | bytes 1327112 | tf_op jit(solution)/shard_map/ppermute | solution.py:70
  40.7 38.9 %collective-permute-start.13 = (bf16[512,1024]{1,0:T(8,128)(2,1)}, bf16[512,1024]{1,0:T(8,128)(2,1)}, u32[]{:S(2)}, u32[]{:S(2)}) collective-permute-start(bf16[512,1024]{1,0:T(8,128)(2,1)} %broadcast_select_fusion.out_change), channel_id=1, source_target_pairs={{0,4},{1,5},{2,6},{3,7},{4,0},{5,1},{6,2},{7,3},{8,12},{9,13},{10,... | collective-permute-start | bytes 3145736 | tf_op jit(solution)/shard_map/ppermute | solution.py:70
  40.8 43.3 %copy-start.79 = (f32[8,8,128]{2,1,0:T(8,128)S(1)}, f32[8,8,128]{2,1,0:T(8,128)}, u32[]{:S(2)}) copy-start(f32[8,8,128]{2,1,0:T(8,128)} %constant.347.clone) | copy-start | bytes 98308
  40.8 32.9 %collective-permute-start.11 = (bf16[512,1024]{1,0:T(8,128)(2,1)S(1)}, bf16[512,1024]{1,0:T(8,128)(2,1)}, u32[]{:S(2)}, u32[]{:S(2)}) collective-permute-start(bf16[512,1024]{1,0:T(8,128)(2,1)S(1)} %shard_map.276), channel_id=1, source_target_pairs={{0,1},{1,2},{2,3},{3,4},{4,5},{5,6},{6,7},{7,8},{8,9},{9,10},{10,1... | collective-permute-start | bytes 3145736 | tf_op jit(solution)/shard_map/ppermute | solution.py:73
  50.8 32.3 %collective-permute-start.9 = (bf16[2,2,3,32,1152]{4,3,2,1,0:T(8,128)(2,1)}, bf16[2,2,3,32,1152]{4,3,2,1,0:T(8,128)(2,1)}, u32[]{:S(2)}, u32[]{:S(2)}) collective-permute-start(bf16[2,2,3,32,1152]{4,3,2,1,0:T(8,128)(2,1)} %pad_maximum_fusion.3.refs_4_), channel_id=1, source_target_pairs={{0,8},{1,9},{2,10},{3,11},{4,12},{5,13},{6,14},{7,15},{8,0},{9,1},... | collective-permute-start | bytes 2654216 | tf_op jit(solution)/shard_map/ppermute | solution.py:70
  54.9 28.1 %collective-permute-start.3 = (bf16[2,2,3,32,1152]{4,3,2,1,0:T(8,128)(2,1)S(1)}, bf16[2,2,3,32,1152]{4,3,2,1,0:T(8,128)(2,1)}, u32[]{:S(2)}, u32[]{:S(2)}) collective-permute-start(bf16[2,2,3,32,1152]{4,3,2,1,0:T(8,128)(2,1)S(1)} %pad_maximum_fusion.2.refs_0_), channel_id=1, source_target_pairs={{0,16},{1,17},{2,18},{3,19},{4,20},{5,21},{6,22},{7,23},{8,24},{9,... | collective-permute-start | bytes 2654216 | tf_op jit(solution)/shard_map/ppermute | solution.py:70
  73.8 43.5 %collective-permute-start.12 = (bf16[512,1024]{1,0:T(8,128)(2,1)}, bf16[512,1024]{1,0:T(8,128)(2,1)S(1)}, u32[]{:S(2)}, u32[]{:S(2)}) collective-permute-start(bf16[512,1024]{1,0:T(8,128)(2,1)} %collective-permute-done.11.tokens.refs_4_), channel_id=1, source_target_pairs={{0,1},{1,2},{2,3},{3,4},{4,5},{5,6},{6,7},{7,8},{8,9},{9,10},{10,1... | collective-permute-start | bytes 3145736 | tf_op jit(solution)/shard_map/ppermute | solution.py:73
  79.1 11.4 %collective-permute-start.8 = (bf16[2,2,3,32,1152]{4,3,2,1,0:T(8,128)(2,1)}, bf16[2,2,3,32,1152]{4,3,2,1,0:T(8,128)(2,1)}, u32[]{:S(2)}, u32[]{:S(2)}) collective-permute-start(bf16[2,2,3,32,1152]{4,3,2,1,0:T(8,128)(2,1)} %pad_maximum_fusion.3.refs_4_), channel_id=1, source_target_pairs={{0,4},{1,5},{2,6},{3,7},{4,0},{5,1},{6,2},{7,3},{8,12},{9,13},{10,... | collective-permute-start | bytes 2654216 | tf_op jit(solution)/shard_map/ppermute | solution.py:70
  79.6 10.9 %collective-permute-start.2 = (bf16[2,2,3,32,1152]{4,3,2,1,0:T(8,128)(2,1)S(1)}, bf16[2,2,3,32,1152]{4,3,2,1,0:T(8,128)(2,1)}, u32[]{:S(2)}, u32[]{:S(2)}) collective-permute-start(bf16[2,2,3,32,1152]{4,3,2,1,0:T(8,128)(2,1)S(1)} %pad_maximum_fusion.2.refs_0_), channel_id=1, source_target_pairs={{0,4},{1,5},{2,6},{3,7},{4,0},{5,1},{6,2},{7,3},{8,12},{9,13},{10,... | collective-permute-start | bytes 2654216 | tf_op jit(solution)/shard_map/ppermute | solution.py:70
  83.1 7.5 %collective-permute-start.10 = (bf16[2,2,3,32,1152]{4,3,2,1,0:T(8,128)(2,1)}, bf16[2,2,3,32,1152]{4,3,2,1,0:T(8,128)(2,1)}, u32[]{:S(2)}, u32[]{:S(2)}) collective-permute-start(bf16[2,2,3,32,1152]{4,3,2,1,0:T(8,128)(2,1)} %collective-permute-done.9.refs_6_), channel_id=1, source_target_pairs={{0,4},{1,5},{2,6},{3,7},{4,0},{5,1},{6,2},{7,3},{8,12},{9,13},{10,... | collective-permute-start | bytes 2654216 | tf_op jit(solution)/shard_map/ppermute | solution.py:70
  83.1 7.5 %collective-permute-start.4 = (bf16[2,2,3,32,1152]{4,3,2,1,0:T(8,128)(2,1)}, bf16[2,2,3,32,1152]{4,3,2,1,0:T(8,128)(2,1)}, u32[]{:S(2)}, u32[]{:S(2)}) collective-permute-start(bf16[2,2,3,32,1152]{4,3,2,1,0:T(8,128)(2,1)} %collective-permute-done.3.refs_2_), channel_id=1, source_target_pairs={{0,4},{1,5},{2,6},{3,7},{4,0},{5,1},{6,2},{7,3},{8,12},{9,13},{10,... | collective-permute-start | bytes 2654216 | tf_op jit(solution)/shard_map/ppermute | solution.py:70
  150.1 3.3 collective-permute-start.15
  158.6 2.7 collective-permute-start.16
  183.1 207.5 %reduce-scatter.5.cloned.1.call-start = ((), (), s32[]{:S(2)}) async-start(), calls=%async_computation.4 | async-start | bytes 5242880 | tf_op jit(solution)/shard_map/reduce_scatter | solution.py:1035
  248.8 2.7 collective-permute-start.17
  283.8 25.5 %collective-permute-start.20 = (bf16[128,1024]{1,0:T(8,128)(2,1)}, bf16[128,1024]{1,0:T(8,128)(2,1)}, u32[]{:S(2)}, u32[]{:S(2)}) collective-permute-start(bf16[128,1024]{1,0:T(8,128)(2,1)} %get-tuple-element.176), channel_id=1, source_target_pairs={{0,3},{1,0},{2,1},{3,2},{4,7},{5,4},{6,5},{7,6},{8,11},{9,8},{10,9... | collective-permute-start | bytes 786440 | tf_op jit(solution)/shard_map/ppermute | solution.py:70
  286.9 23.4 %collective-permute-start.19 = (bf16[128,1024]{1,0:T(8,128)(2,1)}, bf16[128,1024]{1,0:T(8,128)(2,1)}, u32[]{:S(2)}, u32[]{:S(2)}) collective-permute-start(bf16[128,1024]{1,0:T(8,128)(2,1)} %get-tuple-element.177), channel_id=1, source_target_pairs={{0,2},{1,3},{2,0},{3,1},{4,6},{5,7},{6,4},{7,5},{8,10},{9,11},{10,... | collective-permute-start | bytes 786440 | tf_op jit(solution)/shard_map/ppermute | solution.py:70
  286.9 23.4 %collective-permute-start.18 = (bf16[128,1024]{1,0:T(8,128)(2,1)}, bf16[128,1024]{1,0:T(8,128)(2,1)}, u32[]{:S(2)}, u32[]{:S(2)}) collective-permute-start(bf16[128,1024]{1,0:T(8,128)(2,1)} %get-tuple-element.178), channel_id=1, source_target_pairs={{0,1},{1,2},{2,3},{3,0},{4,5},{5,6},{6,7},{7,4},{8,9},{9,10},{10,1... | collective-permute-start | bytes 786440 | tf_op jit(solution)/shard_map/ppermute | solution.py:70
  329.0 8.8 %collective-permute-start.22 = (bf16[4,4,64,1024]{3,2,1,0:T(8,128)(2,1)}, bf16[4,4,64,1024]{3,2,1,0:T(8,128)(2,1)}, u32[]{:S(2)}, u32[]{:S(2)}) collective-permute-start(bf16[4,4,64,1024]{3,2,1,0:T(8,128)(2,1)} %get-tuple-element.126), channel_id=1, source_target_pairs={{0,4},{1,5},{2,6},{3,7},{4,0},{5,1},{6,2},{7,3},{8,12},{9,13},{10,... | collective-permute-start | bytes 6291464 | tf_op jit(solution)/shard_map/ppermute | solution.py:70
  329.0 8.8 %collective-permute-start.21 = (bf16[4,4,64,1024]{3,2,1,0:T(8,128)(2,1)}, bf16[4,4,64,1024]{3,2,1,0:T(8,128)(2,1)}, u32[]{:S(2)}, u32[]{:S(2)}) collective-permute-start(bf16[4,4,64,1024]{3,2,1,0:T(8,128)(2,1)} %get-tuple-element.124.refs_6_), channel_id=1, source_target_pairs={{0,4},{1,5},{2,6},{3,7},{4,0},{5,1},{6,2},{7,3},{8,12},{9,13},{10,... | collective-permute-start | bytes 6291464 | tf_op jit(solution)/shard_map/ppermute | solution.py:70
  335.8 27.3 %collective-permute-start.24 = (bf16[512,1024]{1,0:T(8,128)(2,1)}, bf16[512,1024]{1,0:T(8,128)(2,1)S(1)}, u32[]{:S(2)}, u32[]{:S(2)}) collective-permute-start(bf16[512,1024]{1,0:T(8,128)(2,1)} %get-tuple-element.128.refs_0_), channel_id=1, source_target_pairs={{1,0},{2,1},{3,2},{4,3},{5,4},{6,5},{7,6},{8,7},{9,8},{10,9},{11,1... | collective-permute-start | bytes 3145736 | tf_op jit(solution)/shard_map/ppermute | solution.py:76
  344.6 31.4 %collective-permute-start.23 = (bf16[2,4,64,1024]{3,2,1,0:T(8,128)(2,1)}, bf16[2,4,64,1024]{3,2,1,0:T(8,128)(2,1)}, u32[]{:S(2)}, u32[]{:S(2)}) collective-permute-start(bf16[2,4,64,1024]{3,2,1,0:T(8,128)(2,1)} %get-tuple-element.129.refs_8_), channel_id=1, source_target_pairs={{0,8},{1,9},{2,10},{3,11},{4,12},{5,13},{6,14},{7,15},{8,0},{9,1},... | collective-permute-start | bytes 3145736 | tf_op jit(solution)/shard_map/ppermute | solution.py:70
  348.4 38.4 %collective-permute-start.25 = (bf16[2,4,64,1024]{3,2,1,0:T(8,128)(2,1)}, bf16[2,4,64,1024]{3,2,1,0:T(8,128)(2,1)}, u32[]{:S(2)}, u32[]{:S(2)}) collective-permute-start(bf16[2,4,64,1024]{3,2,1,0:T(8,128)(2,1)} %get-tuple-element.133.refs_10_), channel_id=1, source_target_pairs={{0,16},{1,17},{2,18},{3,19},{4,20},{5,21},{6,22},{7,23},{8,24},{9,... | collective-permute-start | bytes 3145736 | tf_op jit(solution)/shard_map/ppermute | solution.py:70
  369.1 26.8 %collective-permute-start.27 = (bf16[512,1024]{1,0:T(8,128)(2,1)}, bf16[512,1024]{1,0:T(8,128)(2,1)S(1)}, u32[]{:S(2)}, u32[]{:S(2)}) collective-permute-start(bf16[512,1024]{1,0:T(8,128)(2,1)} %get-tuple-element.136.refs_0_), channel_id=1, source_target_pairs={{1,0},{2,1},{3,2},{4,3},{5,4},{6,5},{7,6},{8,7},{9,8},{10,9},{11,1... | collective-permute-start | bytes 3145736 | tf_op jit(solution)/shard_map/ppermute | solution.py:76
  379.4 24.6 %collective-permute-start.34 = (bf16[4,64,1024]{2,1,0:T(8,128)(2,1)}, bf16[4,64,1024]{2,1,0:T(8,128)(2,1)}, u32[]{:S(2)}, u32[]{:S(2)}) collective-permute-start(bf16[4,64,1024]{2,1,0:T(8,128)(2,1)} %get-tuple-element.137.refs_0_.refs_1_), channel_id=1, source_target_pairs={{0,16},{1,17},{2,18},{3,19},{4,20},{5,21},{6,22},{7,23},{8,24},{9,... | collective-permute-start | bytes 1572872 | tf_op jit(solution)/shard_map/ppermute | solution.py:70
  390.2 16.0 %collective-permute-start.35 = (bf16[4,64,1024]{2,1,0:T(8,128)(2,1)}, bf16[4,64,1024]{2,1,0:T(8,128)(2,1)}, u32[]{:S(2)}, u32[]{:S(2)}) collective-permute-start(bf16[4,64,1024]{2,1,0:T(8,128)(2,1)} %get-tuple-element.139.refs_2_.refs_3_), channel_id=1, source_target_pairs={{0,8},{1,9},{2,10},{3,11},{4,12},{5,13},{6,14},{7,15},{8,0},{9,1},... | collective-permute-start | bytes 1572872 | tf_op jit(solution)/shard_map/ppermute | solution.py:70
  390.5 6.2 %collective-permute-start.28 = (f32[2,2,4,384]{3,2,1,0:T(4,128)S(1)}, f32[2,2,4,384]{3,2,1,0:T(4,128)S(1)}, u32[]{:S(2)}, u32[]{:S(2)}) collective-permute-start(f32[2,2,4,384]{3,2,1,0:T(4,128)S(1)} %dynamic-slice_bitcast_fusion.9), channel_id=1, source_target_pairs={{0,4},{1,5},{2,6},{3,7},{4,0},{5,1},{6,2},{7,3},{8,12},{9,13},{10,... | collective-permute-start | bytes 73736 | tf_op jit(solution)/shard_map/ppermute | solution.py:70
  396.7 6.6 %collective-permute-start.29 = (f32[2,4,384]{2,1,0:T(4,128)S(1)}, f32[2,4,384]{2,1,0:T(4,128)S(1)}, u32[]{:S(2)}, u32[]{:S(2)}) collective-permute-start(f32[2,4,384]{2,1,0:T(4,128)S(1)} %dynamic-slice_bitcast_fusion.10), channel_id=1, source_target_pairs={{0,8},{1,9},{2,10},{3,11},{4,12},{5,13},{6,14},{7,15},{8,0},{9,1},... | collective-permute-start | bytes 36872 | tf_op jit(solution)/shard_map/ppermute | solution.py:70
  400.6 13.6 %collective-permute-start.41 = (bf16[2,32,2048]{2,1,0:T(8,128)(2,1)S(1)}, bf16[2,32,2048]{2,1,0:T(8,128)(2,1)S(1)}, u32[]{:S(2)}, u32[]{:S(2)}) collective-permute-start(bf16[2,32,2048]{2,1,0:T(8,128)(2,1)S(1)} %get-tuple-element.168), channel_id=1, source_target_pairs={{0,3},{1,0},{2,1},{3,2},{4,7},{5,4},{6,5},{7,6},{8,11},{9,8},{10,9... | collective-permute-start | bytes 786440 | tf_op jit(solution)/shard_map/ppermute | solution.py:70
  403.4 23.5 %collective-permute-start.40 = (bf16[2,32,2048]{2,1,0:T(8,128)(2,1)S(1)}, bf16[2,32,2048]{2,1,0:T(8,128)(2,1)S(1)}, u32[]{:S(2)}, u32[]{:S(2)}) collective-permute-start(bf16[2,32,2048]{2,1,0:T(8,128)(2,1)S(1)} %get-tuple-element.169), channel_id=1, source_target_pairs={{0,2},{1,3},{2,0},{3,1},{4,6},{5,7},{6,4},{7,5},{8,10},{9,11},{10,... | collective-permute-start | bytes 786440 | tf_op jit(solution)/shard_map/ppermute | solution.py:70
  403.4 23.6 %collective-permute-start.39 = (bf16[2,32,2048]{2,1,0:T(8,128)(2,1)S(1)}, bf16[2,32,2048]{2,1,0:T(8,128)(2,1)S(1)}, u32[]{:S(2)}, u32[]{:S(2)}) collective-permute-start(bf16[2,32,2048]{2,1,0:T(8,128)(2,1)S(1)} %get-tuple-element.170), channel_id=1, source_target_pairs={{0,1},{1,2},{2,3},{3,0},{4,5},{5,6},{6,7},{7,4},{8,9},{9,10},{10,1... | collective-permute-start | bytes 786440 | tf_op jit(solution)/shard_map/ppermute | solution.py:70
  404.0 10.2 %collective-permute-start.30 = (f32[4,384]{1,0:T(4,128)S(1)}, f32[4,384]{1,0:T(4,128)S(1)}, u32[]{:S(2)}, u32[]{:S(2)}) collective-permute-start(f32[4,384]{1,0:T(4,128)S(1)} %fusion.34), channel_id=1, source_target_pairs={{0,16},{1,17},{2,18},{3,19},{4,20},{5,21},{6,22},{7,23},{8,24},{9,... | collective-permute-start | bytes 18440 | tf_op jit(solution)/shard_map/ppermute | solution.py:70
  408.0 25.1 %collective-permute-start.38 = (bf16[4,32,1024]{2,1,0:T(8,128)(2,1)S(1)}, bf16[4,32,1024]{2,1,0:T(8,128)(2,1)S(1)}, u32[]{:S(2)}, u32[]{:S(2)}) collective-permute-start(bf16[4,32,1024]{2,1,0:T(8,128)(2,1)S(1)} %get-tuple-element.172), channel_id=1, source_target_pairs={{0,3},{1,0},{2,1},{3,2},{4,7},{5,4},{6,5},{7,6},{8,11},{9,8},{10,9... | collective-permute-start | bytes 786440 | tf_op jit(solution)/shard_map/ppermute | solution.py:70
  414.1 18.9 %collective-permute-start.36 = (bf16[4,32,1024]{2,1,0:T(8,128)(2,1)S(1)}, bf16[4,32,1024]{2,1,0:T(8,128)(2,1)S(1)}, u32[]{:S(2)}, u32[]{:S(2)}) collective-permute-start(bf16[4,32,1024]{2,1,0:T(8,128)(2,1)S(1)} %get-tuple-element.174), channel_id=1, source_target_pairs={{0,1},{1,2},{2,3},{3,0},{4,5},{5,6},{6,7},{7,4},{8,9},{9,10},{10,1... | collective-permute-start | bytes 786440 | tf_op jit(solution)/shard_map/ppermute | solution.py:70
  414.2 33.8 %collective-permute-start.37 = (bf16[4,32,1024]{2,1,0:T(8,128)(2,1)S(1)}, bf16[4,32,1024]{2,1,0:T(8,128)(2,1)S(1)}, u32[]{:S(2)}, u32[]{:S(2)}) collective-permute-start(bf16[4,32,1024]{2,1,0:T(8,128)(2,1)S(1)} %get-tuple-element.175), channel_id=1, source_target_pairs={{0,2},{1,3},{2,0},{3,1},{4,6},{5,7},{6,4},{7,5},{8,10},{9,11},{10,... | collective-permute-start | bytes 786440 | tf_op jit(solution)/shard_map/ppermute | solution.py:70
  426.9 24.2 %collective-permute-start.26 = (bf16[512,1024]{1,0:T(8,128)(2,1)S(1)}, bf16[512,1024]{1,0:T(8,128)(2,1)S(1)}, u32[]{:S(2)}, u32[]{:S(2)}) collective-permute-start(bf16[512,1024]{1,0:T(8,128)(2,1)S(1)} %get-tuple-element.142), channel_id=1, source_target_pairs={{0,4},{1,5},{2,6},{3,7},{4,0},{5,1},{6,2},{7,3},{8,12},{9,13},{10,... | collective-permute-start | bytes 3145736 | tf_op jit(solution)/shard_map/ppermute | solution.py:70
  427.0 21.2 %collective-permute-start.31 = (f32[384]{0:T(512)S(1)}, f32[384]{0:T(512)S(1)}, u32[]{:S(2)}, u32[]{:S(2)}) collective-permute-start(f32[384]{0:T(512)S(1)} %get-tuple-element.162), channel_id=1, source_target_pairs={{0,1},{1,2},{2,3},{3,0},{4,5},{5,6},{6,7},{7,4},{8,9},{9,10},{10,1... | collective-permute-start | bytes 4616 | tf_op jit(solution)/shard_map/ppermute | solution.py:70
  433.0 15.2 %collective-permute-start.33 = (f32[384]{0:T(512)S(1)}, f32[384]{0:T(512)S(1)}, u32[]{:S(2)}, u32[]{:S(2)}) collective-permute-start(f32[384]{0:T(512)S(1)} %get-tuple-element.163), channel_id=1, source_target_pairs={{0,3},{1,0},{2,1},{3,2},{4,7},{5,4},{6,5},{7,6},{8,11},{9,8},{10,9... | collective-permute-start | bytes 4616 | tf_op jit(solution)/shard_map/ppermute | solution.py:70
  433.0 15.2 %collective-permute-start.32 = (f32[384]{0:T(512)S(1)}, f32[384]{0:T(512)S(1)}, u32[]{:S(2)}, u32[]{:S(2)}) collective-permute-start(f32[384]{0:T(512)S(1)} %get-tuple-element.164), channel_id=1, source_target_pairs={{0,2},{1,3},{2,0},{3,1},{4,6},{5,7},{6,4},{7,5},{8,10},{9,11},{10,... | collective-permute-start | bytes 4616 | tf_op jit(solution)/shard_map/ppermute | solution.py:70
  448.1 2.8 collective-permute-start.42
  (91 other events, 547.5 us)
Sparse Core Ops, SparseCore 0:
  34.9 113.8 all-gather.5
  152.1 74.8 all-gather.3
  230.0 51.2 reduce-scatter.2
  284.4 52.6 reduce-scatter.4
